TPU v7x, 128 devices: a whole 4x4x4 slice. The times are simulated.
128 devices in a mesh: dp: 16 (over x_lo, y, core), ctx: 8 (over z, x_hi).
Axes of the slice: x: 4 (x_hi: 2, x_lo: 2; x = x_hi * 2 + x_lo), y: 4, z: 4, core: 2. Of those that a mesh axis runs over, the one named last changes fastest.
Arguments:
- hidden_in: bfloat16 [16384, 2048], P(('dp', 'ctx')), may hold values from -4 to 4
- queries: bfloat16 [16384, 4096], P(('dp', 'ctx')), may hold values from -30 to 30
- keys: bfloat16 [16384, 512], P(('dp', 'ctx')), may hold values from -5 to 5
- values: bfloat16 [16384, 512], P(('dp', 'ctx')), may hold values from -8 to 8
- out_weight: bfloat16 [4096, 2048], P('ctx'), may hold values from -0.09375 to 0.09375
- norm_gain: float32 [2048], replicated, may hold values from 0.5 to 1.5
- routes: int32 [16384, 8], P(('dp', 'ctx')), may hold values from 0 to 127, all different within a row; in each aligned block of 128 rows (0 to 127, 128 to 255, ...) at most 12 rows name the same one
- gates: float32 [16384, 8], P(('dp', 'ctx')), may hold values from 0.05 to 0.75
- w_gate: bfloat16 [128, 2048, 768], P(('dp', 'ctx')), may hold values from -0.125 to 0.125
- w_up: bfloat16 [128, 2048, 768], P(('dp', 'ctx')), may hold values from -0.125 to 0.125
- w_down: bfloat16 [128, 768, 2048], P(('dp', 'ctx')), may hold values from -0.21875 to 0.21875
Outputs:
- attended: bfloat16 [16384, 2048], P(('dp', 'ctx'))
- expert_mix: bfloat16 [16384, 2048], P(('dp', 'ctx'))
- balance_loss: float32 [], replicated
- expert_load: float32 [128], replicated
Inputs may be any that keep to these rules, and one draw needn't show every extreme that they name: `routes`: in the rows of one device no expert is named more than 12 times; some expert is named exactly 12 times.
All inputs are finite; a program needn't handle non-finite values.
Results may differ from a plain program's by a relative error of at most 0.01.
Values may be sent and summed in bfloat16 or wider, within the bound.
No kernel may reach another device: no remote copies, remote signals or barrier semaphores. Data moves between devices by JAX's collectives and lax.ppermute only.
A program may use at most 128 MiB of HBM per device.

v0:
```python
import math

import jax
import jax.numpy as jnp
from jax import lax
from jax.sharding import PartitionSpec as P

H = 32
KV = 4
DH = 128
TOP = 8


def attention_rows(block, key_seq, value_seq):
    seq_rows = block.shape[0]
    head_count = block.shape[2]
    query_all = block.reshape(seq_rows, head_count, DH)
    block_rows = min(512, seq_rows)
    block_count = seq_rows // block_rows
    query_blocks = query_all.reshape(block_count, block_rows, head_count, DH)
    starts = jnp.arange(block_count, dtype=jnp.int32) * block_rows

    def attend_block(inputs):
        query_block, first = inputs
        scores = jnp.einsum(
            "qhd,kd->hqk", query_block, key_seq, preferred_element_type=jnp.float32
        ) / math.sqrt(DH)
        rows = first + jnp.arange(block_rows, dtype=jnp.int32)[:, None]
        cols = jnp.arange(seq_rows, dtype=jnp.int32)[None, :]
        scores = jnp.where(cols <= rows, scores, -jnp.inf)
        top_score = jnp.max(scores, axis=-1, keepdims=True)
        expo = jnp.exp(scores - top_score)
        weights = (expo / jnp.sum(expo, axis=-1, keepdims=True)).astype(jnp.bfloat16)
        result = jnp.einsum("hqk,kd->qhd", weights, value_seq, preferred_element_type=jnp.float32)
        return result.astype(jnp.bfloat16)

    outputs = lax.map(attend_block, (query_blocks, starts))
    return outputs.reshape(seq_rows, head_count, DH)


def expert_apply(rows_in, w_gate, w_up, w_down):
    gate_act = jnp.dot(rows_in, w_gate[0], preferred_element_type=jnp.float32)
    up_act = jnp.dot(rows_in, w_up[0], preferred_element_type=jnp.float32)
    expert_hidden = (jax.nn.silu(gate_act) * up_act).astype(jnp.bfloat16)
    return jnp.dot(expert_hidden, w_down[0], preferred_element_type=jnp.float32).astype(
        jnp.bfloat16
    )


def on_device(
    hidden_in, queries, keys, values, out_weight, norm_gain, routes, gates, w_gate, w_up, w_down
):
    ctx_count = lax.axis_size("ctx")
    dp_count = lax.axis_size("dp")
    exp_count = dp_count * ctx_count
    tok_rows = hidden_in.shape[0]
    seq_rows = tok_rows * ctx_count
    heads_here = out_weight.shape[0] // DH
    position = lax.axis_index("ctx")
    key_all, value_all = (
        lax.all_gather(keys, "ctx", axis=0, tiled=True),
        lax.all_gather(values, "ctx", axis=0, tiled=True),
    )
    head_pick = position * heads_here * KV // H
    key_seq = lax.dynamic_slice_in_dim(key_all, head_pick * DH, DH, 1)
    value_seq = lax.dynamic_slice_in_dim(value_all, head_pick * DH, DH, 1)
    query_local = queries.reshape(tok_rows, ctx_count, heads_here, DH)
    head_rows = attention_rows(
        lax.all_to_all(query_local, "ctx", split_axis=1, concat_axis=0, tiled=True),
        key_seq,
        value_seq,
    )
    head_flat = head_rows.reshape(seq_rows, heads_here * DH)
    projected = lax.psum_scatter(
        jnp.dot(head_flat, out_weight, preferred_element_type=jnp.float32),
        "ctx",
        scatter_dimension=0,
        tiled=True,
    )
    residual_sum = hidden_in.astype(jnp.float32) + projected
    attended = residual_sum.astype(jnp.bfloat16)
    mean_square = jnp.mean(residual_sum * residual_sum, axis=1, keepdims=True)
    normed = (residual_sum / jnp.sqrt(mean_square + 1e-06) * norm_gain).astype(jnp.bfloat16)
    capacity = 3 * tok_rows * TOP // (2 * exp_count)
    flat_ids = routes.reshape(-1)
    flat_gates = gates.reshape(-1)
    route_count = flat_ids.shape[0]
    onehot = (flat_ids[:, None] == jnp.arange(exp_count, dtype=jnp.int32)[None, :]).astype(
        jnp.int32
    )
    running = jnp.cumsum(onehot, axis=0)
    rank = jnp.sum((running - 1) * onehot, axis=1)
    slot = flat_ids * capacity + rank
    slot_source = (
        jnp.zeros((exp_count * capacity,), jnp.int32)
        .at[slot]
        .set(jnp.arange(route_count, dtype=jnp.int32) + 1)
    )
    live = slot_source > 0
    token_of = jnp.maximum(slot_source - 1, 0) // TOP
    outgoing = jnp.where(live[:, None], normed[token_of], jnp.zeros((), jnp.bfloat16))
    outgoing = outgoing.reshape(exp_count, capacity, normed.shape[1])
    block = lax.all_to_all(outgoing, ("dp", "ctx"), split_axis=0, concat_axis=0, tiled=True)
    result = expert_apply(block.reshape(-1, block.shape[2]), w_gate, w_up, w_down).reshape(
        block.shape
    )
    returned = lax.all_to_all(result, ("dp", "ctx"), split_axis=0, concat_axis=0, tiled=True)
    returned_flat = returned.reshape(exp_count * capacity, normed.shape[1])
    per_route = returned_flat[slot].astype(jnp.float32) * flat_gates[:, None]
    expert_mix = jnp.sum(per_route.reshape(tok_rows, TOP, normed.shape[1]), axis=1).astype(
        jnp.bfloat16
    )
    onehot_float = onehot.astype(jnp.float32)
    counts = jnp.sum(onehot_float, axis=0)
    gate_sums = jnp.dot(flat_gates, onehot_float, precision=lax.Precision.HIGHEST)
    total_counts, total_gates = lax.psum((counts, gate_sums), ("dp", "ctx"))
    token_total = tok_rows * exp_count
    balance_loss = exp_count * jnp.sum(
        total_counts / (token_total * TOP) * (total_gates / token_total)
    )
    expert_load = exp_count * total_counts / (token_total * TOP)
    return (attended, expert_mix, balance_loss, expert_load)


def solution(mesh):
    return jax.shard_map(
        on_device,
        mesh=mesh,
        in_specs=(
            P(("dp", "ctx"), None),
            P(("dp", "ctx"), None),
            P(("dp", "ctx"), None),
            P(("dp", "ctx"), None),
            P("ctx", None),
            P(),
            P(("dp", "ctx"), None),
            P(("dp", "ctx"), None),
            P(("dp", "ctx"), None, None),
            P(("dp", "ctx"), None, None),
            P(("dp", "ctx"), None, None),
        ),
        out_specs=(P(("dp", "ctx"), None), P(("dp", "ctx"), None), P(), P()),
        check_vma=False,
    )
```

profile of v0, /device:TPU:0, one launch (start us, length us, event | category | flops | bytes accessed | tf_op | source)
XLA Modules:
  0.0 653.5 jit_solution(7520992366644287067)
XLA Ops:
  8.7 2.3 copy.25
  10.9 7.9 %all-to-all-start = ((bf16[128,8,4,128]{0,3,2,1:T(8,128)(2,1)}), bf16[128,8,4,128]{0,3,2,1:T(8,128)(2,1)}, u32[]{:S(2)}, u32[]{:S(2)}) async-start(bf16[128,8,4,128]{0,3,2,1:T(8,128)(2,1)} %bitcast.96), calls=%async_computation | async-start | bytes 2097152 | tf_op jit(solution)/shard_map/all_to_all | solution.py:69
  18.9 18.7 %all-to-all-done = bf16[128,8,4,128]{0,3,2,1:T(8,128)(2,1)} async-done(((bf16[128,8,4,128]{0,3,2,1:T(8,128)(2,1)}), bf16[128,8,4,128]{0,3,2,1:T(8,128)(2,1)}, u32[]{:S(2)}, u32[]{:S(2)}) %all-to-all-start) | async-done | bytes 1048608 | tf_op jit(solution)/shard_map/all_to_all | solution.py:69
  37.6 2.3 copy.26
  39.9 23.2 %all-gather.3.cloned.1.call-done = bf16[1024,512]{1,0:T(8,128)(2,1)} async-done(((bf16[128,512]{1,0:T(8,128)(2,1)}), bf16[1024,512]{1,0:T(8,128)(2,1)}) %all-gather.3.cloned.1.call-update) | async-done | bytes 1048592 | tf_op jit(solution)/shard_map/all_gather | solution.py:61
  64.1 46.6 %all-gather.5.cloned.1.call-done = bf16[1024,512]{1,0:T(8,128)(2,1)} async-done(((bf16[128,512]{1,0:T(8,128)(2,1)}), bf16[1024,512]{1,0:T(8,128)(2,1)}) %all-gather.5.cloned.1.call-update) | async-done | bytes 1048592 | tf_op jit(solution)/shard_map/all_gather | solution.py:62
  110.7 1.7 constant_dynamic-slice_fusion
  112.4 32.0 %while.10 = (s32[]{:T(128)}, bf16[2,512,4,128]{3,2,1,0:T(4,128)(2,1)}, s32[2]{0:T(128)S(1)}, bf16[2,512,4,128]{3,1,0,2:T(8,128)(2,1)}, bf16[1024,128]{1,0:T(8,12...) while((s32[]{:T(128)}, bf16[2,512,4,128]{3,2,1,0:T(4,128)(2,1)}, s32[2]{0:T(128)S(1)}, ...), condition=%wide.region_3.4_spmd, body=%wide.region_0.3_spmd.sunk | while | flops 1087112704 | bytes 28856484 | solution.py:37
  114.8 7.4 %fusion.76 = (f32[4,512]{1,0:T(4,128)S(1)}, f32[4,512,1024]{2,1,0:T(8,128)}) fusion(pred[512,1024]{1,0:T(8,128)(4,1)} %iota_compare_fusion.6, bf16[2,512,4,128]{3,1,0,2:T(8,128)(2,1)} %get-tuple-element.127, s32[]{:T(128)S(6)} %copy.50, bf16[1024,128]{1,0:T(8,128)(2,1)S(1)} %get-tuple-element.128), kind=kOutput, calls=%fused_computation.82.clone.1 | convolution fusion | flops 545260544 | bytes 9707524 | tf_op jit(solution)/shard_map/while/body/eval_jaxpr/sub | solution.py:32
  122.2 4.8 fusion.77
  129.6 1.2 iota_compare_fusion.6
  130.8 7.4 %fusion.76 = (f32[4,512]{1,0:T(4,128)S(1)}, f32[4,512,1024]{2,1,0:T(8,128)}) fusion(pred[512,1024]{1,0:T(8,128)(4,1)} %iota_compare_fusion.6, bf16[2,512,4,128]{3,1,0,2:T(8,128)(2,1)} %get-tuple-element.127, s32[]{:T(128)S(6)} %copy.50, bf16[1024,128]{1,0:T(8,128)(2,1)S(1)} %get-tuple-element.128), kind=kOutput, calls=%fused_computation.82.clone.1 | convolution fusion | flops 545260544 | bytes 9707524 | tf_op jit(solution)/shard_map/while/body/eval_jaxpr/sub | solution.py:32
  138.2 4.8 fusion.77
  144.4 7.5 %fusion.40 = f32[1024,2048]{1,0:T(8,128)} fusion(bf16[512,2048]{1,0:T(8,128)(2,1)} %param.17, bf16[128,8,4,128]{3,2,1,0:T(4,128)(2,1)} %bitcast.101), kind=kOutput, calls=%fused_computation.42 | convolution fusion | flops 2147483648 | bytes 11534336 | tf_op jit(solution)/shard_map/dot_general | solution.py:75
  155.8 4.5 scatter_custom_fusion
  160.5 105.6 %reduce-scatter.2.cloned.1.call-done = f32[128,2048]{1,0:T(8,128)} async-done(((f32[1024,2048]{1,0:T(8,128)}), f32[128,2048]{1,0:T(8,128)}) %reduce-scatter.2.cloned.1.call-update) | async-done | bytes 1048592 | tf_op jit(solution)/shard_map/reduce_scatter | solution.py:74
  266.1 1.6 multiply_reduce_fusion
  267.7 2.6 multiply_convert_fusion.1
  270.2 13.8 %gather_fusion = bf16[1536,2048]{1,0:T(8,128)(2,1)} fusion(bf16[128,2048]{1,0:T(8,128)(2,1)} %get-tuple-element.65, s32[2048]{0:T(1024)S(1)} %pad_clamp_fusion), kind=kCustom, calls=%fused_computation | custom fusion | bytes 12589056 | tf_op jit(solution)/shard_map/gather | solution.py:101
  284.1 10.6 %gather.9 = bf16[128,12,2048]{2,1,0:T(8,128)(2,1)} reshape(bf16[1536,2048]{1,0:T(8,128)(2,1)} %gather_fusion) | data formatting | bytes 12582912 | tf_op jit(solution)/shard_map/gather | solution.py:101
  294.7 7.3 %broadcast_select_fusion = bf16[128,12,2048]{2,1,0:T(8,128)(2,1)} fusion(bf16[128,12,2048]{2,1,0:T(8,128)(2,1)} %gather.9, pred[128,12]{1,0:T(8,128)(4,1)S(1)} %broadcast_in_dim.43), kind=kLoop, calls=%fused_computation.34 | loop fusion | flops 3145728 | bytes 12584448 | tf_op jit(solution)/shard_map/jit(_where)/select_n | solution.py:101
  301.9 103.6 %all_to_all.25 = bf16[128,12,2048]{2,1,0:T(8,128)(2,1)} all-to-all(bf16[128,12,2048]{2,1,0:T(8,128)(2,1)} %broadcast_select_fusion), channel_id=1, replica_groups=mesh['dp'=16,'ctx'=8] {'dp','ctx'}, dimensions={0} | all-to-all | bytes 12582912 | tf_op jit(solution)/shard_map/all_to_all | solution.py:103
  405.5 10.7 %reshape.108 = bf16[1536,2048]{1,0:T(8,128)(2,1)} reshape(bf16[128,12,2048]{2,1,0:T(8,128)(2,1)} %all_to_all.25) | data formatting | bytes 12582912 | tf_op jit(solution)/shard_map/reshape | solution.py:104
  416.2 8.2 %fusion.38 = f32[1536,768]{1,0:T(8,128)S(1)} fusion(bf16[1536,2048]{1,0:T(8,128)(2,1)} %reshape.108, bf16[1,2048,768]{2,1,0:T(8,128)(2,1)} %param.21), kind=kOutput, calls=%fused_computation.39 | convolution fusion | flops 4831838208 | bytes 14155776 | tf_op jit(solution)/shard_map/dot_general | solution.py:42
  424.4 5.6 multiply_convert_fusion
  430.0 7.1 %convolution_convert_fusion = bf16[1536,2048]{1,0:T(8,128)(2,1)} fusion(bf16[1536,768]{1,0:T(8,128)(2,1)S(1)} %multiply_convert_fusion, bf16[1,768,2048]{2,1,0:T(8,128)(2,1)S(1)} %copy-done), kind=kOutput, calls=%fused_computation.35 | convolution fusion | flops 4834983936 | bytes 11796480 | tf_op jit(solution)/shard_map/dot_general | solution.py:45
  437.1 10.6 %reshape.109 = bf16[128,12,2048]{2,1,0:T(8,128)(2,1)} reshape(bf16[1536,2048]{1,0:T(8,128)(2,1)} %convolution_convert_fusion) | data formatting | bytes 12582912 | tf_op jit(solution)/shard_map/reshape | solution.py:104
  447.7 6.4 all-to-all-start.2
  455.1 158.5 %all-reduce = (f32[128]{0:T(128)S(1)}, f32[128]{0:T(128)S(1)}) all-reduce(f32[128]{0:T(128)S(1)} %convolution_bitcast_fusion, f32[128]{0:T(128)S(1)} %convert_reduce_fusion), channel_id=1, replica_groups=mesh['dp'=16,'ctx'=8] {'dp','ctx'}, use_global_device_ids=true, to_apply=%region_13.14 | all-reduce | flops 256 | bytes 2048 | tf_op jit(solution)/shard_map/psum | solution.py:116
  615.4 10.7 %reshape.110 = bf16[1536,2048]{1,0:T(8,128)(2,1)} reshape(bf16[128,12,2048]{2,1,0:T(8,128)(2,1)} %all-to-all-done.2) | data formatting | bytes 12582912 | tf_op jit(solution)/shard_map/reshape | solution.py:108
  626.1 12.4 %gather_fusion.1 = bf16[1024,2048]{1,0:T(8,128)(2,1)} fusion(bf16[1536,2048]{1,0:T(8,128)(2,1)} %reshape.110, s32[1024]{0:T(1024)S(1)} %broadcast_clamp_fusion), kind=kCustom, calls=%fused_computation.1 | custom fusion | bytes 8392704 | tf_op jit(solution)/shard_map/gather | solution.py:109
  638.5 7.3 %fusion.35 = bf16[128,2048]{1,0:T(8,128)(2,1)} fusion(bf16[1024,2048]{1,0:T(8,128)(2,1)} %gather_fusion.1, f32[128,8]{1,0:T(8,128)S(1)} %copy.34), kind=kLoop, calls=%fused_computation.33 | loop fusion | flops 6029312 | bytes 4722688 | tf_op jit(solution)/shard_map/reduce_sum | solution.py:110
  (66 shorter events, 15.0 us)
Async XLA Ops:
  7.2 422.9 %copy-start = (bf16[1,768,2048]{2,1,0:T(8,128)(2,1)S(1)}, bf16[1,768,2048]{2,1,0:T(8,128)(2,1)}, u32[]{:S(2)}) copy-start(bf16[1,768,2048]{2,1,0:T(8,128)(2,1)} %param.23) | copy-start | bytes 9437188
  7.2 56.0 %all-gather.3.cloned.1.call-start = ((), (), s32[]{:S(2)}) async-start(), calls=%async_computation.4 | async-start | bytes 1179648 | tf_op jit(solution)/shard_map/all_gather | solution.py:61
  7.9 102.8 %all-gather.5.cloned.1.call-start = ((), (), s32[]{:S(2)}) async-start(), calls=%async_computation.5 | async-start | bytes 1179648 | tf_op jit(solution)/shard_map/all_gather | solution.py:62
  10.9 26.6 %all-to-all-start = ((bf16[128,8,4,128]{0,3,2,1:T(8,128)(2,1)}), bf16[128,8,4,128]{0,3,2,1:T(8,128)(2,1)}, u32[]{:S(2)}, u32[]{:S(2)}) async-start(bf16[128,8,4,128]{0,3,2,1:T(8,128)(2,1)} %bitcast.96), calls=%async_computation | async-start | bytes 2097152 | tf_op jit(solution)/shard_map/all_to_all | solution.py:69
  18.8 247.3 %reduce-scatter.2.cloned.1.call-start = ((), (), s32[]{:S(2)}) async-start(), calls=%async_computation.6 | async-start | bytes 9437184 | tf_op jit(solution)/shard_map/reduce_scatter | solution.py:74
  122.2 4.8 copy-start.7
  127.4 1.0 copy-start.8
  138.2 4.8 copy-start.7
  143.4 1.0 copy-start.8
  151.9 0.7 copy-start.3
  151.9 115.8 %copy-start.4 = (f32[2048]{0:T(1024)S(1)}, f32[2048]{0:T(1024)}, u32[]{:S(2)}) copy-start(f32[2048]{0:T(1024)} %param.18) | copy-start | bytes 24580
  153.4 0.8 copy-start.2
  416.2 8.2 %copy-start.1 = (bf16[1536,2048]{1,0:T(8,128)(2,1)S(1)}, bf16[1536,2048]{1,0:T(8,128)(2,1)}, u32[]{:S(2)}) copy-start(bf16[1536,2048]{1,0:T(8,128)(2,1)} %reshape.108) | copy-start | bytes 18874372
  416.2 8.2 %copy-start.6 = (bf16[1,2048,768]{2,1,0:T(8,128)(2,1)S(1)}, bf16[1,2048,768]{2,1,0:T(8,128)(2,1)}, u32[]{:S(2)}) copy-start(bf16[1,2048,768]{2,1,0:T(8,128)(2,1)} %param.22) | copy-start | bytes 9437188
  447.7 6.4 copy-start.5
  447.7 167.7 %all-to-all-start.2 = ((bf16[128,12,2048]{2,1,0:T(8,128)(2,1)}), bf16[128,12,2048]{2,1,0:T(8,128)(2,1)}, u32[]{:S(2)}, u32[]{:S(2)}) async-start(bf16[128,12,2048]{2,1,0:T(8,128)(2,1)} %reshape.109), calls=%async_computation.3 | async-start | bytes 16777216 | tf_op jit(solution)/shard_map/all_to_all | solution.py:107
Sparse Core Ops, SparseCore 0:
  10.4 52.7 all-gather.2
  65.5 45.1 all-gather.4
  152.1 113.9 reduce-scatter.1
where the time goes:
time: 656 us; the launch traced here: 654 us
  blocking collectives  262 us (40%)
  waiting for transfers between devices  195 us (30%)
  local copies, waits for them, and re-layouts  87.1 us (13%)
  matrix products  53.2 us (8%)
  other arithmetic  25.4 us (4%)
  between operations  15.8 us (2%)
  starting transfers between devices  14.4 us (2%)
    psum x1, blocking collectives, on_device(): total_counts, total_gates = lax.psum((counts, gate_sums), ('dp', 'ctx'))  159 us
    reduce_scatter x1, waiting for transfers between devices, on_device(): lax.psum_scatter(jnp.dot(head_flat, out_weight, preferred_element_type=jn...  106 us
    all_to_all x1, blocking collectives, on_device(): lax.all_to_all(outgoing, ('dp', 'ctx'), split_axis=0, concat_axis=0, tile...  104 us
    all_gather x1, waiting for transfers between devices, on_device(): lax.all_gather(values, 'ctx', axis=0, tiled=True)  46.6 us
    gather x2, local copies, waits for them, and re-layouts, on_device(): normed[token_of]  24.4 us
    all_gather x1, waiting for transfers between devices, on_device(): lax.all_gather(keys, 'ctx', axis=0, tiled=True)  23.2 us
    all_to_all x1, waiting for transfers between devices, on_device(): lax.all_to_all(query_local, 'ctx', split_axis=1, concat_axis=0, tiled=True)  18.7 us
    sub x2, matrix products, attend_block(): expo = jnp.exp(scores - top_score)  14.8 us
  transfers between devices with their start and end apart: 5, of which 4 were waited for; matrix products, arithmetic and copies ran while one was open for 2% of the time, Pallas kernels for 0%

commit v1 on v0

v1 whole, which is shorter than its diff:
```python
import functools
import math

import jax
import jax.numpy as jnp
from jax import lax
from jax.experimental import pallas as pl
from jax.experimental.pallas import tpu as pltpu
from jax.sharding import PartitionSpec as P

H = 32
KV = 4
DH = 128
TOP = 8
D = 2048
FF = 768
TOK = 128
NE = 128
CTX = 8
GH = H // KV
HALF = 512
WHOLE = 8
CAP = 12
QUARTER = 256
WIDE = 3072
ALL = ("dp", "ctx")
Z_GROUPS = [[0, 2, 4, 6], [1, 3, 5, 7]]
BF = jnp.bfloat16
F32 = jnp.float32
VMEM_LIMIT = 56 * 1024 * 1024


def params(**more):
    return pltpu.CompilerParams(vmem_limit_bytes=VMEM_LIMIT, **more)


def dot(a, b):
    return jnp.dot(a, b, preferred_element_type=F32)


def route_kernel(routes_ref, gates_ref, pick1_ref, pick2_ref, mix1_ref, mix2_ref, stat_ref):
    experts = lax.broadcasted_iota(jnp.int32, (NE, TOK), 0)
    named = jnp.zeros((NE, TOK), F32)
    weight = jnp.zeros((NE, TOK), F32)
    for k in range(TOP):
        hit = routes_ref[k : k + 1, :] == experts
        named = jnp.where(hit, 1.0, named)
        weight = jnp.where(hit, gates_ref[k : k + 1, :], weight)
    earlier = lax.broadcasted_iota(jnp.int32, (TOK, TOK), 0) < lax.broadcasted_iota(
        jnp.int32, (TOK, TOK), 1
    )
    rank = dot(named.astype(BF), earlier.astype(F32).astype(BF))
    rank = jnp.where(named > 0, rank, -1.0)
    rank = jnp.broadcast_to(rank[:, None, :], (NE, 8, TOK)).reshape(NE * 8, TOK)
    weights = jnp.broadcast_to(weight[:, None, :], (NE, 8, TOK)).reshape(NE * 8, TOK)
    row = lax.broadcasted_iota(jnp.int32, (NE * 8, TOK), 0) & 7
    pick1 = rank == row.astype(F32)
    pick1_ref[...] = jnp.where(pick1, 1.0, 0.0).astype(BF)
    base = rank == (WHOLE + (row & 3)).astype(F32)
    left = base & (row < 4)
    right = base & (row >= 4)
    pick2_ref[:, :TOK] = jnp.where(left, 1.0, 0.0).astype(BF)
    pick2_ref[:, TOK:] = jnp.where(right, 1.0, 0.0).astype(BF)

    def put(ref, first, chosen):
        mix = jnp.transpose(jnp.where(chosen, weights, 0.0))
        high = mix.astype(BF)
        ref[first : first + TOK, :] = high
        ref[first + TOK : first + 2 * TOK, :] = (mix - high.astype(F32)).astype(BF)

    put(mix1_ref, 0, pick1)
    put(mix2_ref, 0, left)
    put(mix2_ref, 2 * TOK, right)
    stat_ref[...] = jnp.zeros((8, NE), F32)
    stat_ref[0:1, :] = jnp.sum(jnp.transpose(named), axis=0, keepdims=True)
    total = jnp.sum(jnp.transpose(weight), axis=0, keepdims=True)
    high = total.astype(BF).astype(F32)
    stat_ref[1:2, :] = high
    stat_ref[2:3, :] = total - high


def route_plan(routes, gates):
    return pl.pallas_call(
        route_kernel,
        out_shape=(
            jax.ShapeDtypeStruct((NE * 8, TOK), BF),
            jax.ShapeDtypeStruct((NE * 8, 2 * TOK), BF),
            jax.ShapeDtypeStruct((2 * TOK, NE * 8), BF),
            jax.ShapeDtypeStruct((4 * TOK, NE * 8), BF),
            jax.ShapeDtypeStruct((8, NE), F32),
        ),
        compiler_params=params(),
        name="route_plan",
    )(routes.T, gates.T)


def attend_kernel(half_ref, q_ref, kv_ref, out_ref):
    half = half_ref[0]
    keys = kv_ref[:, :DH]
    values = jnp.concatenate([kv_ref[:, DH:], jnp.ones((CTX * TOK, DH), BF)], axis=1)
    scale = math.log2(math.e) / math.sqrt(DH)
    rows = half * TOK + lax.broadcasted_iota(jnp.int32, (TOK, 2 * TOK), 0)
    seen = lax.broadcasted_iota(jnp.int32, (TOK, 2 * TOK), 1) <= rows
    for block in range(4):
        whole = block * 2 * TOK
        for head in range(GH):
            part, inner = divmod(head, GH // 2)
            first = (part ^ half) * HALF + inner * DH if part == 0 else (1 - half) * HALF + inner * DH
            q = q_ref[block, :, pl.ds(pl.multiple_of(first, DH), DH)]
            tail = lax.dot_general(
                q,
                keys[whole : whole + 2 * TOK],
                (((1,), (1,)), ((), ())),
                preferred_element_type=F32,
            )
            tail = jnp.where(seen, tail, -jnp.inf)
            top = jnp.max(tail, axis=1, keepdims=True)
            if block:
                body = lax.dot_general(
                    q, keys[:whole], (((1,), (1,)), ((), ())), preferred_element_type=F32
                )
                top = jnp.maximum(top, jnp.max(body, axis=1, keepdims=True))
            expo = jnp.exp2((tail - top) * scale).astype(BF)
            result = dot(expo, values[whole : whole + 2 * TOK])
            if block:
                expo = jnp.exp2((body - top) * scale).astype(BF)
                result = result + dot(expo, values[:whole])
            out_ref[block, :, head * DH : (head + 1) * DH] = (
                result[:, :DH] / result[:, DH:]
            ).astype(BF)


def attend(half, q, kv):
    return pl.pallas_call(
        attend_kernel,
        out_shape=jax.ShapeDtypeStruct(q.shape, BF),
        in_specs=[
            pl.BlockSpec(memory_space=pltpu.SMEM),
            pl.BlockSpec(memory_space=pltpu.VMEM),
            pl.BlockSpec(memory_space=pltpu.VMEM),
        ],
        out_specs=pl.BlockSpec(memory_space=pltpu.VMEM),
        compiler_params=params(),
        cost_estimate=pl.CostEstimate(
            flops=2 * 2 * 512 * 8 * 640 * 128, bytes_accessed=3 << 20, transcendentals=512 * 8 * 640
        ),
        name="attend",
    )(half, q, kv)


def project_kernel(core_ref, heads_ref, mine_ref, near_ref, far_ref, out_ref):
    core = core_ref[0]
    near = HALF + core * QUARTER
    far = HALF + (1 - core) * QUARTER
    total = dot(heads_ref[:, :HALF], mine_ref[...])
    total = total + dot(heads_ref[:, pl.ds(pl.multiple_of(near, QUARTER), QUARTER)], near_ref[...])
    total = total + dot(heads_ref[:, pl.ds(pl.multiple_of(far, QUARTER), QUARTER)], far_ref[...])
    out_ref[...] = total.astype(BF)


def project(core, heads, mine, near, far):
    rows, cols = heads.shape[0], 512
    return pl.pallas_call(
        project_kernel,
        grid=(D // cols,),
        out_shape=jax.ShapeDtypeStruct((rows, D), BF),
        in_specs=[
            pl.BlockSpec(memory_space=pltpu.SMEM),
            pl.BlockSpec((rows, 2 * HALF), lambda j: (0, 0)),
            pl.BlockSpec((HALF, cols), lambda j: (0, j)),
            pl.BlockSpec((QUARTER, cols), lambda j: (0, j)),
            pl.BlockSpec((QUARTER, cols), lambda j: (0, j)),
        ],
        out_specs=pl.BlockSpec((rows, cols), lambda j: (0, j)),
        compiler_params=params(),
        cost_estimate=pl.CostEstimate(
            flops=2 * rows * 2 * HALF * D, bytes_accessed=8 << 20, transcendentals=0
        ),
        name="project",
    )(core, heads, mine, near, far)


def residual_kernel(
    parts_ref, hidden_ref, gain_ref, pick1_ref, pick2_ref, att_ref, x_ref, norm_ref, stack_ref
):
    @pl.when(pl.program_id(0) == 0)
    def _():
        total = hidden_ref[...].astype(F32)
        for part in range(4):
            total = total + parts_ref[part].astype(F32)
        att_ref[...] = total.astype(BF)
        square = jnp.mean(total * total, axis=1, keepdims=True)
        normed = (total / jnp.sqrt(square + 1e-06) * gain_ref[...]).astype(BF)
        norm_ref[...] = normed
        stack_ref[:TOK, :] = normed[:, : D // 2]
        stack_ref[TOK:, :] = normed[:, D // 2 :]

    x_ref[:, :D] = dot(pick1_ref[...], norm_ref[...]).astype(BF)
    x_ref[:, D:] = dot(pick2_ref[...], stack_ref[...]).astype(BF)


def residual(parts, hidden, gain, pick1, pick2):
    steps = 4
    rows = NE * 8 // steps
    return pl.pallas_call(
        residual_kernel,
        grid=(steps,),
        out_shape=(
            jax.ShapeDtypeStruct((TOK, D), BF),
            jax.ShapeDtypeStruct((NE * 8, WIDE), BF),
        ),
        in_specs=[
            pl.BlockSpec((4, TOK, D), lambda i: (0, 0, 0)),
            pl.BlockSpec((TOK, D), lambda i: (0, 0)),
            pl.BlockSpec((1, D), lambda i: (0, 0)),
            pl.BlockSpec((rows, TOK), lambda i: (i, 0)),
            pl.BlockSpec((rows, 2 * TOK), lambda i: (i, 0)),
        ],
        out_specs=(
            pl.BlockSpec((TOK, D), lambda i: (0, 0)),
            pl.BlockSpec((rows, WIDE), lambda i: (i, 0)),
        ),
        scratch_shapes=[pltpu.VMEM((TOK, D), BF), pltpu.VMEM((2 * TOK, D // 2), BF)],
        compiler_params=params(),
        cost_estimate=pl.CostEstimate(flops=1 << 30, bytes_accessed=10 << 20, transcendentals=128),
        name="residual_norm_pick",
    )(parts, hidden, gain.reshape(1, D), pick1, pick2)


def expert_kernel(x_ref, gate_ref, up_ref, down_ref, stat_ref, y_ref):
    rows = x_ref.shape[0]
    count = rows // 2
    half = D // 2
    to = lax.broadcasted_iota(jnp.int32, (rows, rows), 0)
    at = lax.broadcasted_iota(jnp.int32, (rows, rows), 1)

    def source(i):
        side = (i >= count).astype(jnp.int32)
        own = i - side * count
        return (own >> 2) * 8 + side * 4 + (own & 3)

    sort = jnp.where(source(to) == at, 1.0, 0.0).astype(BF)
    back = jnp.where(source(at) == to, 1.0, 0.0).astype(BF)
    rest = dot(sort, x_ref[:, D:]).astype(BF)
    rest = jnp.concatenate([rest[:count], rest[count:]], axis=1)
    x = jnp.concatenate([x_ref[:, :D], rest], axis=0)
    gate = dot(x, gate_ref[0])
    hidden = (gate / (1.0 + jnp.exp(-gate)) * dot(x, up_ref[0])).astype(BF)
    y = dot(hidden, down_ref[0]).astype(BF)
    y_ref[:, :D] = y[:rows]
    rest = jnp.concatenate([y[rows:, :half], y[rows:, half:]], axis=0)
    y_ref[:, D:WIDE] = dot(back, rest).astype(BF)
    stat = jnp.broadcast_to(stat_ref[...][None], (rows // 8, 8, NE)).reshape(rows, NE)
    y_ref[:, WIDE:] = stat.astype(BF)


def expert_apply(x, w_gate, w_up, w_down, stat):
    rows = 256
    return pl.pallas_call(
        expert_kernel,
        grid=(NE * 8 // rows,),
        out_shape=jax.ShapeDtypeStruct((NE * 8, WIDE + NE), BF),
        in_specs=[
            pl.BlockSpec((rows, WIDE), lambda i: (i, 0)),
            pl.BlockSpec((1, D, FF), lambda i: (0, 0, 0)),
            pl.BlockSpec((1, D, FF), lambda i: (0, 0, 0)),
            pl.BlockSpec((1, FF, D), lambda i: (0, 0, 0)),
            pl.BlockSpec((8, NE), lambda i: (0, 0)),
        ],
        out_specs=pl.BlockSpec((rows, WIDE + NE), lambda i: (i, 0)),
        compiler_params=params(),
        cost_estimate=pl.CostEstimate(
            flops=6 * NE * CAP * D * FF, bytes_accessed=22 << 20, transcendentals=NE * CAP * FF
        ),
        name="experts",
    )(x, w_gate, w_up, w_down, stat)


def mix_kernel(mix1_ref, mix2_ref, y_ref, rest_ref, stat_ref, out_ref, load_ref, loss_ref):
    both = dot(mix1_ref[...], y_ref[...]) + dot(mix2_ref[...], rest_ref[...])
    out_ref[...] = (both[:TOK] + both[TOK:]).astype(BF)

    @pl.when(pl.program_id(0) == 0)
    def _():
        stat = jnp.sum(stat_ref[...].astype(F32).reshape(NE, 8, NE), axis=0)
        counts = stat[0:1]
        gates = stat[1:2] + stat[2:3]
        tokens = TOK * NE
        load = counts / (tokens * TOP)
        load_ref[...] = NE * load
        loss = NE * jnp.sum(load * (gates / tokens), axis=1, keepdims=True)
        loss_ref[...] = jnp.broadcast_to(loss, (1, NE))


def mix(mix1, mix2, y):
    cols = 512
    return pl.pallas_call(
        mix_kernel,
        grid=(D // cols,),
        out_shape=(
            jax.ShapeDtypeStruct((TOK, D), BF),
            jax.ShapeDtypeStruct((1, NE), F32),
            jax.ShapeDtypeStruct((1, NE), F32),
        ),
        in_specs=[
            pl.BlockSpec((2 * TOK, NE * 8), lambda j: (0, 0)),
            pl.BlockSpec((2 * TOK, NE * 8), lambda j: (j // 2, 0)),
            pl.BlockSpec((NE * 8, cols), lambda j: (0, j)),
            pl.BlockSpec((NE * 8, cols), lambda j: (0, D // cols + j % 2)),
            pl.BlockSpec((NE * 8, NE), lambda j: (0, WIDE // NE)),
        ],
        out_specs=(
            pl.BlockSpec((TOK, cols), lambda j: (0, j)),
            pl.BlockSpec((1, NE), lambda j: (0, 0)),
            pl.BlockSpec((1, NE), lambda j: (0, 0)),
        ),
        compiler_params=params(),
        cost_estimate=pl.CostEstimate(flops=2 << 30, bytes_accessed=8 << 20, transcendentals=0),
        name="mix",
    )(mix1, mix2, y, y, y)


def swap(x, axis, count, step):
    return lax.ppermute(x, axis, [(i, i ^ step) for i in range(count)])


def exchange(x, axes, groups=None):
    return lax.all_to_all(
        x, axes, split_axis=0, concat_axis=0, tiled=True, axis_index_groups=groups
    )


def on_device(
    hidden_in, queries, keys, values, out_weight, norm_gain, routes, gates, w_gate, w_up, w_down
):
    half = (lax.axis_index("ctx") % 2).astype(jnp.int32).reshape(1)
    kv = jnp.concatenate([keys.reshape(TOK, KV, DH), values.reshape(TOK, KV, DH)], axis=2)
    kv = jnp.transpose(kv, (1, 0, 2))
    kv = jnp.broadcast_to(kv[:, None], (KV, 2, TOK, 2 * DH)).reshape(CTX, TOK, 2 * DH)
    kv = exchange(kv, "ctx")
    q = jnp.transpose(queries.reshape(TOK, KV, GH * DH), (1, 0, 2))
    q = exchange(q, "ctx", Z_GROUPS)
    core = (lax.axis_index("dp") % 2).astype(jnp.int32).reshape(1)
    near = lax.dynamic_slice_in_dim(out_weight, core[0] * QUARTER, QUARTER, 0)
    near = swap(near, "ctx", CTX, 1)
    far = swap(near, "dp", 16, 1)
    pick1, pick2, mix1, mix2, stat = route_plan(routes, gates)
    heads = attend(half, q, kv.reshape(CTX * TOK, 2 * DH))
    partial = project(core, heads.reshape(4 * TOK, GH * DH), out_weight, near, far)
    parts = exchange(partial.reshape(4, TOK, D), "ctx", Z_GROUPS)
    attended, x = residual(parts, hidden_in, norm_gain, pick1, pick2)
    x = exchange(x.reshape(NE, 8, WIDE), ALL)
    y = expert_apply(x.reshape(NE * 8, WIDE), w_gate, w_up, w_down, stat)
    y = exchange(y.reshape(NE, 8, WIDE + NE), ALL)
    expert_mix, load, loss = mix(mix1, mix2, y.reshape(NE * 8, WIDE + NE))
    return attended, expert_mix, loss[0, 0], load[0]


def solution(mesh):
    rows = P(ALL, None)
    return jax.shard_map(
        on_device,
        mesh=mesh,
        in_specs=(
            rows,
            rows,
            rows,
            rows,
            P("ctx", None),
            P(),
            rows,
            rows,
            P(ALL, None, None),
            P(ALL, None, None),
            P(ALL, None, None),
        ),
        out_specs=(rows, rows, P(), P()),
        check_vma=False,
    )
```

time: 656 us -> 299 us (0.46)
  waiting for transfers between devices: 195 us -> 58.1 us
  blocking collectives: 262 us -> 164 us
  local copies, waits for them, and re-layouts: 87.1 us -> 8.42 us
  matrix products: 53.2 us -> 0 us
  Pallas kernels: 0 us -> 51.3 us
  other arithmetic: 25.4 us -> 0.13 us
  between operations: 15.8 us -> 0.73 us
    psum x1 -> x0, blocking collectives: 159 us -> none  [on_device(): total_counts, total_gates = lax.psum((counts, gate_sums), ('dp', 'ctx'))]
    reduce_scatter x1 -> x0, waiting for transfers between devices: 106 us -> none  [on_device(): lax.psum_scatter(jnp.dot(head_flat, out_weight, preferred_element_type=jn...]
    all_gather x2 -> x0, waiting for transfers between devices: 69.8 us -> none  [the longest x1 46.6 us: on_device(): lax.all_gather(values, 'ctx', axis=0, tiled=True)]
    all_to_all x1 -> x2, blocking collectives: 104 us -> 164 us  [exchange(): lax.all_to_all(x, axes, split_axis=0, concat_axis=0, tiled=True, axis_ind...]
    pallas_call x0 -> x6, Pallas kernels: none -> 51.3 us  [the longest x1 22.2 us: expert_apply(): pl.pallas_call(expert_kernel, grid=(NE * 8 // rows,), out_shape=jax.Shape...]
    dot_general x7 -> x0, matrix products: 38.4 us -> none  [the longest x2 9.58 us: attend_block(): jnp.einsum('hqk,kd->qhd', weights, value_seq, preferred_element_type=jnp....]
    gather x3 -> x0, local copies, waits for them, and re-layouts: 36.8 us -> none  [the longest x2 24.4 us: on_device(): normed[token_of]]
    reshape x4 -> x3, local copies, waits for them, and re-layouts: 32.1 us -> 3.2 us  [the longest x1 1.32 us: on_device(): q = jnp.transpose(queries.reshape(TOK, KV, GH * DH), (1, 0, 2))]
  transfers between devices with their start and end apart: 5 -> 5, of which waited for: 4 -> 4; matrix products, arithmetic and copies ran while one was open for 2% -> 2% of each run, Pallas kernels for 0% -> 3%
where the time goes in v1:
time: 299 us; the launch traced here: 298 us
  blocking collectives  164 us (55%)
  waiting for transfers between devices  58.1 us (19%)
  Pallas kernels  51.3 us (17%)
  starting transfers between devices  15.6 us (5%)
  local copies, waits for them, and re-layouts  8.42 us (3%)
    all_to_all x2, blocking collectives, exchange(): lax.all_to_all(x, axes, split_axis=0, concat_axis=0, tiled=True, axis_ind...  164 us
    all_to_all x3, waiting for transfers between devices, exchange(): lax.all_to_all(x, axes, split_axis=0, concat_axis=0, tiled=True, axis_ind...  41.8 us
    pallas_call x1, Pallas kernels, expert_apply(): pl.pallas_call(expert_kernel, grid=(NE * 8 // rows,), out_shape=jax.Shape...  22.2 us
    ppermute x2, waiting for transfers between devices, swap(): return lax.ppermute(x, axis, [(i, i ^ step) for i in range(count)])  16.4 us
    all_to_all x3, starting transfers between devices, exchange(): lax.all_to_all(x, axes, split_axis=0, concat_axis=0, tiled=True, axis_ind...  12.4 us
    pallas_call x1, Pallas kernels, residual(): pl.pallas_call(residual_kernel, grid=(steps,), out_shape=(jax.ShapeDtypeS...  6.91 us
    pallas_call x1, Pallas kernels, mix(): pl.pallas_call(mix_kernel, grid=(D // cols,), out_shape=(jax.ShapeDtypeSt...  6.8 us
    pallas_call x1, Pallas kernels, attend(): pl.pallas_call(attend_kernel, out_shape=jax.ShapeDtypeStruct(q.shape, BF)...  6.45 us
  transfers between devices with their start and end apart: 5, of which 4 were waited for; matrix products, arithmetic and copies ran while one was open for 2% of the time, Pallas kernels for 3%

profile of v1, /device:TPU:0, one launch (start us, length us, event | category | flops | bytes accessed | tf_op | source)
XLA Modules:
  0.0 298.4 jit_solution(9588122353172215037)
XLA Ops:
  0.6 0.0 copy-start.1
  0.7 1.4 constant_dynamic-slice_fusion
  2.0 3.2 %collective-permute-start = (bf16[256,2048]{1,0:T(8,128)(2,1)S(1)}, bf16[256,2048]{1,0:T(8,128)(2,1)}, u32[]{:S(2)}, u32[]{:S(2)}) collective-permute-start(bf16[256,2048]{1,0:T(8,128)(2,1)S(1)} %constant_dynamic-slice_fusion), channel_id=1, source_target_pairs={{0,1},{1,0},{2,3},{3,2},{4,5},{5,4},{6,7},{7,6},{8,9},{9,8},{10,11... | collective-permute-start | bytes 3145736 | tf_op jit(solution)/shard_map/ppermute | solution.py:324
  5.2 0.9 reshape.54
  6.2 0.9 reshape.55
  7.1 0.1 maximum_bitcast_fusion
  7.3 0.8 broadcast_in_dim.2
  8.1 5.3 %all-to-all-start.1 = ((bf16[8,128,256]{2,1,0:T(8,128)(2,1)}), bf16[8,128,256]{2,1,0:T(8,128)(2,1)S(1)}, u32[]{:S(2)}, u32[]{:S(2)}) async-start(bf16[8,128,256]{2,1,0:T(8,128)(2,1)} %bitcast.5), calls=%async_computation.1 | async-start | bytes 1048576 | tf_op jit(solution)/shard_map/all_to_all | solution.py:328
  13.4 16.4 %collective-permute-done.near_ref = bf16[256,2048]{1,0:T(8,128)(2,1)} collective-permute-done((bf16[256,2048]{1,0:T(8,128)(2,1)S(1)}, bf16[256,2048]{1,0:T(8,128)(2,1)}, u32[]{:S(2)}, u32[]{:S(2)}) %collective-permute-start) | collective-permute-done | bytes 1048608 | tf_op jit(solution)/shard_map/ppermute | solution.py:324
  29.8 0.0 collective-permute-start.1
  29.8 0.0 copy-done.1
  29.8 0.7 copy.16
  30.5 1.3 copy.17
  31.8 5.9 %all-to-all-done.1 = bf16[8,128,256]{2,1,0:T(8,128)(2,1)S(1)} async-done(((bf16[8,128,256]{2,1,0:T(8,128)(2,1)}), bf16[8,128,256]{2,1,0:T(8,128)(2,1)S(1)}, u32[]{:S(2)}, u32[]{:S(2)}) %all-to-all-start.1) | async-done | bytes 524320 | tf_op jit(solution)/shard_map/all_to_all | solution.py:328
  37.7 0.0 copy-start.3
  37.7 3.5 %all-to-all-start = ((bf16[4,128,1024]{2,1,0:T(8,128)(2,1)}), bf16[4,128,1024]{2,1,0:T(8,128)(2,1)S(1)}, u32[]{:S(2)}, u32[]{:S(2)}) async-start(bf16[4,128,1024]{2,1,0:T(8,128)(2,1)} %bitcast.3), calls=%async_computation | async-start | bytes 2097152 | tf_op jit(solution)/shard_map/all_to_all | solution.py:328
  41.2 14.2 %all-to-all-done.q_ref = bf16[4,128,1024]{2,1,0:T(8,128)(2,1)S(1)} async-done(((bf16[4,128,1024]{2,1,0:T(8,128)(2,1)}), bf16[4,128,1024]{2,1,0:T(8,128)(2,1)S(1)}, u32[]{:S(2)}, u32[]{:S(2)}) %all-to-all-start) | async-done | bytes 1048608 | tf_op jit(solution)/shard_map/all_to_all | solution.py:328
  55.4 0.0 copy-start.2
  55.4 0.0 copy-done.3
  55.4 1.0 copy-done.2
  56.4 6.5 %attend.1 = bf16[4,128,1024]{2,1,0:T(8,128)(2,1)} custom-call(s32[1]{0:T(128)} %bitcast.1.half_ref, bf16[4,128,1024]{2,1,0:T(8,128)(2,1)} %copy-done.2, bf16[1024,256]{1,0:T(8,128)(2,1)} %bitcast.28), custom_call_target="tpu_custom_call" | custom-call | flops 1342177280 | bytes 3145728 | tf_op jit(solution)/shard_map/attend/pallas_call | solution.py:134
  62.8 0.0 collective-permute-done.1.far_ref
  62.8 6.1 %project.1 = bf16[512,2048]{1,0:T(8,128)(2,1)} custom-call(s32[1]{0:T(128)} %bitcast.core_ref, bf16[512,1024]{1,0:T(8,128)(2,1)} %bitcast.34, bf16[512,2048]{1,0:T(8,128)(2,1)} %mine_ref.1, bf16[256,2048]{1,0:T(8,128)(2,1)} %collective-permute-done.near_ref, bf16[256,2048]{1,0:T(8,128)(2,1)} %collective-permute-done.1.far_ref), custom_call_target="tpu_custom_call" | custom-call | flops 2147483648 | bytes 8388608 | tf_op jit(solution)/shard_map/project/pallas_call | solution.py:163
  69.0 3.6 %all-to-all-start.2 = ((bf16[4,128,2048]{2,1,0:T(8,128)(2,1)}), bf16[4,128,2048]{2,1,0:T(8,128)(2,1)S(1)}, u32[]{:S(2)}, u32[]{:S(2)}) async-start(bf16[4,128,2048]{2,1,0:T(8,128)(2,1)} %bitcast.27), calls=%async_computation.2 | async-start | bytes 4194304 | tf_op jit(solution)/shard_map/all_to_all | solution.py:328
  72.6 2.8 route_plan.1
  75.4 21.7 %all-to-all-done.2.parts_ref = bf16[4,128,2048]{2,1,0:T(8,128)(2,1)S(1)} async-done(((bf16[4,128,2048]{2,1,0:T(8,128)(2,1)}), bf16[4,128,2048]{2,1,0:T(8,128)(2,1)S(1)}, u32[]{:S(2)}, u32[]{:S(2)}) %all-to-all-start.2) | async-done | bytes 2097184 | tf_op jit(solution)/shard_map/all_to_all | solution.py:328
  97.1 1.3 copy-done
  98.4 6.9 %residual_norm_pick.1 = (bf16[128,2048]{1,0:T(8,128)(2,1)}, bf16[1024,3072]{1,0:T(8,128)(2,1)}) custom-call(bf16[4,128,2048]{2,1,0:T(8,128)(2,1)} %copy-done, bf16[128,2048]{1,0:T(8,128)(2,1)} %hidden_ref.1, f32[1,2048]{1,0:T(1,128)} %bitcast.31, bf16[1024,128]{1,0:T(8,128)(2,1)} %get-tuple-element.14.pick1_ref, bf16[1024,256]{1,0:T(8,128)(2,1)} %get-tuple-element.15.pick2_ref), custom_call_target="tpu_custom_call" | custom-call | flops 1073741824 | bytes 10485760 | tf_op jit(solution)/shard_map/residual_norm_pick/pallas_call | solution.py:205
  105.3 81.1 %all_to_all.25 = bf16[128,8,3072]{2,1,0:T(8,128)(2,1)} all-to-all(bf16[128,8,3072]{2,1,0:T(8,128)(2,1)} %bitcast.24), channel_id=1, replica_groups=mesh['dp'=16,'ctx'=8] {'dp','ctx'}, dimensions={0} | all-to-all | bytes 12582912 | tf_op jit(solution)/shard_map/all_to_all | solution.py:328
  186.5 22.2 %experts.1 = bf16[1024,3200]{1,0:T(8,128)(2,1)} custom-call(bf16[1024,3072]{1,0:T(8,128)(2,1)} %bitcast.25, bf16[1,2048,768]{2,1,0:T(8,128)(2,1)} %gate_ref.1, bf16[1,2048,768]{2,1,0:T(8,128)(2,1)} %up_ref.1, bf16[1,768,2048]{2,1,0:T(8,128)(2,1)} %down_ref.1, f32[8,128]{1,0:T(8,128)} %get-tuple-element.20.stat_ref), custom_call_target="tpu_custom_call" | custom-call | flops 14495514624 | bytes 23068672 | tf_op jit(solution)/shard_map/experts/pallas_call | solution.py:259
  208.7 82.9 %all_to_all.26 = bf16[128,8,3200]{2,1,0:T(8,128)(2,1)} all-to-all(bf16[128,8,3200]{2,1,0:T(8,128)(2,1)} %bitcast.23), channel_id=1, replica_groups=mesh['dp'=16,'ctx'=8] {'dp','ctx'}, dimensions={0} | all-to-all | bytes 13107200 | tf_op jit(solution)/shard_map/all_to_all | solution.py:328
  291.6 6.8 %mix.1 = (bf16[128,2048]{1,0:T(8,128)(2,1)}, f32[1,128]{1,0:T(1,128)}, f32[1,128]{1,0:T(1,128)}) custom-call(bf16[256,1024]{1,0:T(8,128)(2,1)} %get-tuple-element.17.mix1_ref, bf16[512,1024]{1,0:T(8,128)(2,1)} %get-tuple-element.18.mix2_ref, bf16[1024,3200]{1,0:T(8,128)(2,1)} %bitcast.20, bf16[1024,3200]{1,0:T(8,128)(2,1)} %bitcast.21, ...), custom_call_target="tpu_custom_call" | custom-call | flops 2147483648 | bytes 8388608 | tf_op jit(solution)/shard_map/mix/pallas_call | solution.py:297
  (2 shorter events, 0.0 us)
Async XLA Ops:
  0.6 29.2 %copy-start.1 = (bf16[128,4096]{1,0:T(8,128)(2,1)S(1)}, bf16[128,4096]{1,0:T(8,128)(2,1)}, u32[]{:S(2)}) copy-start(bf16[128,4096]{1,0:T(8,128)(2,1)} %param.12) | copy-start | bytes 3145732
  2.0 27.8 %collective-permute-start = (bf16[256,2048]{1,0:T(8,128)(2,1)S(1)}, bf16[256,2048]{1,0:T(8,128)(2,1)}, u32[]{:S(2)}, u32[]{:S(2)}) collective-permute-start(bf16[256,2048]{1,0:T(8,128)(2,1)S(1)} %constant_dynamic-slice_fusion), channel_id=1, source_target_pairs={{0,1},{1,0},{2,3},{3,2},{4,5},{5,4},{6,7},{7,6},{8,9},{9,8},{10,11... | collective-permute-start | bytes 3145736 | tf_op jit(solution)/shard_map/ppermute | solution.py:324
  8.1 29.6 %all-to-all-start.1 = ((bf16[8,128,256]{2,1,0:T(8,128)(2,1)}), bf16[8,128,256]{2,1,0:T(8,128)(2,1)S(1)}, u32[]{:S(2)}, u32[]{:S(2)}) async-start(bf16[8,128,256]{2,1,0:T(8,128)(2,1)} %bitcast.5), calls=%async_computation.1 | async-start | bytes 1048576 | tf_op jit(solution)/shard_map/all_to_all | solution.py:328
  29.8 33.0 %collective-permute-start.1 = (bf16[256,2048]{1,0:T(8,128)(2,1)}, bf16[256,2048]{1,0:T(8,128)(2,1)}, u32[]{:S(2)}, u32[]{:S(2)}) collective-permute-start(bf16[256,2048]{1,0:T(8,128)(2,1)} %collective-permute-done.near_ref), channel_id=1, source_target_pairs={{0,8},{8,0},{16,24},{24,16},{32,40},{40,32},{48,56},{56,48},{64,72... | collective-permute-start | bytes 3145736 | tf_op jit(solution)/shard_map/ppermute | solution.py:324
  37.7 17.7 %copy-start.3 = (bf16[8,128,256]{2,1,0:T(8,128)(2,1)}, bf16[8,128,256]{2,1,0:T(8,128)(2,1)S(1)}, u32[]{:S(2)}) copy-start(bf16[8,128,256]{2,1,0:T(8,128)(2,1)S(1)} %all-to-all-done.1) | copy-start | bytes 1572868
  37.7 17.7 %all-to-all-start = ((bf16[4,128,1024]{2,1,0:T(8,128)(2,1)}), bf16[4,128,1024]{2,1,0:T(8,128)(2,1)S(1)}, u32[]{:S(2)}, u32[]{:S(2)}) async-start(bf16[4,128,1024]{2,1,0:T(8,128)(2,1)} %bitcast.3), calls=%async_computation | async-start | bytes 2097152 | tf_op jit(solution)/shard_map/all_to_all | solution.py:328
  55.4 1.0 copy-start.2
  69.0 28.1 %all-to-all-start.2 = ((bf16[4,128,2048]{2,1,0:T(8,128)(2,1)}), bf16[4,128,2048]{2,1,0:T(8,128)(2,1)S(1)}, u32[]{:S(2)}, u32[]{:S(2)}) async-start(bf16[4,128,2048]{2,1,0:T(8,128)(2,1)} %bitcast.27), calls=%async_computation.2 | async-start | bytes 4194304 | tf_op jit(solution)/shard_map/all_to_all | solution.py:328
  97.1 1.3 copy-start

commit v2 on v1

v2 whole, which is shorter than its diff:
```python
import functools
import math

import jax
import jax.numpy as jnp
from jax import lax
from jax.experimental import pallas as pl
from jax.experimental.pallas import tpu as pltpu
from jax.sharding import PartitionSpec as P

H = 32
KV = 4
DH = 128
TOP = 8
D = 2048
FF = 768
TOK = 128
NE = 128
CTX = 8
GH = H // KV
SENT = GH * DH + 4 * DH
HALF = 512
WHOLE = 8
CAP = 12
QUARTER = 256
WIDE = 3072
ALL = ("dp", "ctx")
Z_GROUPS = [[0, 2, 4, 6], [1, 3, 5, 7]]
BF = jnp.bfloat16
F32 = jnp.float32
def params(megabytes):
    return pltpu.CompilerParams(vmem_limit_bytes=megabytes << 20)


def near_core(x):
    return pltpu.with_memory_space_constraint(x, pltpu.VMEM)


def far_memory(x):
    return pltpu.with_memory_space_constraint(x, pltpu.HBM)


ANY = pl.BlockSpec(memory_space=pl.ANY)
VM = pl.BlockSpec(memory_space=pltpu.VMEM)
SM = pl.BlockSpec(memory_space=pltpu.SMEM)


def dot(a, b):
    return jnp.dot(a, b, preferred_element_type=F32)


def route_kernel(routes_ref, gates_ref, pick1_ref, pick2_ref, mix1_ref, mix2_ref, stat_ref):
    experts = lax.broadcasted_iota(jnp.int32, (NE, TOK), 0)
    named = jnp.zeros((NE, TOK), F32)
    weight = jnp.zeros((NE, TOK), F32)
    for k in range(TOP):
        hit = routes_ref[k : k + 1, :] == experts
        named = jnp.where(hit, 1.0, named)
        weight = jnp.where(hit, gates_ref[k : k + 1, :], weight)
    earlier = lax.broadcasted_iota(jnp.int32, (TOK, TOK), 0) < lax.broadcasted_iota(
        jnp.int32, (TOK, TOK), 1
    )
    rank = dot(named.astype(BF), earlier.astype(F32).astype(BF))
    rank = jnp.where(named > 0, rank, -1.0)
    rank = jnp.broadcast_to(rank[:, None, :], (NE, 8, TOK)).reshape(NE * 8, TOK)
    weights = jnp.broadcast_to(weight[:, None, :], (NE, 8, TOK)).reshape(NE * 8, TOK)
    row = lax.broadcasted_iota(jnp.int32, (NE * 8, TOK), 0) & 7
    pick1 = rank == row.astype(F32)
    pick1_ref[...] = jnp.where(pick1, 1.0, 0.0).astype(BF)
    base = rank == (WHOLE + (row & 3)).astype(F32)
    left = base & (row < 4)
    right = base & (row >= 4)
    pick2_ref[:, :TOK] = jnp.where(left, 1.0, 0.0).astype(BF)
    pick2_ref[:, TOK:] = jnp.where(right, 1.0, 0.0).astype(BF)

    def put(ref, first, chosen):
        mix = jnp.transpose(jnp.where(chosen, weights, 0.0))
        high = mix.astype(BF)
        ref[first : first + TOK, :] = high
        ref[first + TOK : first + 2 * TOK, :] = (mix - high.astype(F32)).astype(BF)

    put(mix1_ref, 0, pick1)
    put(mix2_ref, 0, left)
    put(mix2_ref, 2 * TOK, right)
    stat_ref[...] = jnp.zeros((8, NE), F32)
    stat_ref[0:1, :] = jnp.sum(jnp.transpose(named), axis=0, keepdims=True)
    total = jnp.sum(jnp.transpose(weight), axis=0, keepdims=True)
    high = total.astype(BF).astype(F32)
    stat_ref[1:2, :] = high
    stat_ref[2:3, :] = total - high


def route_plan(routes, gates):
    return pl.pallas_call(
        route_kernel,
        out_shape=(
            pltpu.HBM((NE * 8, TOK), BF),
            pltpu.HBM((NE * 8, 2 * TOK), BF),
            pltpu.HBM((2 * TOK, NE * 8), BF),
            pltpu.HBM((4 * TOK, NE * 8), BF),
            pltpu.HBM((8, NE), F32),
        ),
        in_specs=[VM] * 2,
        out_specs=(VM,) * 5,
        compiler_params=params(8),
        name="route_plan",
    )(routes.T, gates.T)


def send_kernel(q_ref, keys_ref, values_ref, partner_keys_ref, partner_values_ref, out_ref):
    parts = (keys_ref, values_ref, partner_keys_ref, partner_values_ref)
    wide = GH * DH
    for group in range(KV):
        out_ref[group, :, :wide] = q_ref[:, group * wide : (group + 1) * wide]
        for i, ref in enumerate(parts):
            first = wide + i * DH
            out_ref[group, :, first : first + DH] = ref[:, group * DH : (group + 1) * DH]


def send_rows(*arrays):
    return pl.pallas_call(
        send_kernel,
        out_shape=jax.ShapeDtypeStruct((KV, TOK, SENT), BF),
        in_specs=[VM] * 5,
        out_specs=VM,
        compiler_params=params(4),
        name="send_rows",
    )(*(near_core(x) for x in arrays))


def send_weight_kernel(core_ref, weight_ref, first_ref, second_ref, out_ref, sem):
    del first_ref, second_ref
    rows = pl.ds(pl.multiple_of(core_ref[0] * QUARTER, QUARTER), QUARTER)
    copy = pltpu.make_async_copy(weight_ref.at[rows], out_ref, sem)
    copy.start()
    copy.wait()


def send_weight(core, weight, first, second):
    return pl.pallas_call(
        send_weight_kernel,
        out_shape=jax.ShapeDtypeStruct((QUARTER, D), BF),
        in_specs=[SM, ANY, ANY, ANY],
        out_specs=ANY,
        scratch_shapes=[pltpu.SemaphoreType.DMA],
        compiler_params=params(4),
        name="send_weight",
    )(core, weight, first, second)


def attend_kernel(half_ref, sent_ref, out_ref):
    half = half_ref[0]
    one = jnp.ones((4 * TOK, DH), BF)

    def piece(i):
        first = GH * DH + i * DH
        return jnp.concatenate([sent_ref[z, :, first : first + DH] for z in range(4)], axis=0)

    keys = [piece(0), piece(2)]
    values = [jnp.concatenate([piece(i), one], axis=1) for i in (1, 3)]
    scale = math.log2(math.e) / math.sqrt(DH)
    below = lax.broadcasted_iota(jnp.int32, (TOK, TOK), 1) <= lax.broadcasted_iota(
        jnp.int32, (TOK, TOK), 0
    )
    for block in range(4):
        upto = (block + 1) * TOK
        for head in range(GH):
            part, inner = divmod(head, GH // 2)
            first = (half if part == 0 else 1 - half) * HALF + inner * DH
            q = sent_ref[block, :, pl.ds(pl.multiple_of(first, DH), DH)]
            scores = []
            for side in range(2):
                score = lax.dot_general(
                    q, keys[side][:upto], (((1,), (1,)), ((), ())), preferred_element_type=F32
                )
                seen = below if side == 0 else jnp.full((TOK, TOK), half, jnp.int32) == 1
                last = jnp.where(seen, score[:, upto - TOK :], -jnp.inf)
                if block:
                    last = jnp.concatenate([score[:, : upto - TOK], last], axis=1)
                scores.append(last)
            top = jnp.maximum(
                jnp.max(scores[0], axis=1, keepdims=True), jnp.max(scores[1], axis=1, keepdims=True)
            )
            result = 0.0
            for side in range(2):
                expo = jnp.exp2((scores[side] - top) * scale).astype(BF)
                result = result + dot(expo, values[side][:upto])
            out_ref[block, :, head * DH : (head + 1) * DH] = (
                result[:, :DH] / result[:, DH:]
            ).astype(BF)


def attend(half, sent):
    return pl.pallas_call(
        attend_kernel,
        out_shape=pltpu.VMEM((4, TOK, GH * DH), BF),
        in_specs=[SM, VM],
        out_specs=VM,
        compiler_params=params(16),
        cost_estimate=pl.CostEstimate(
            flops=2 * 2 * 512 * 8 * 640 * 128, bytes_accessed=3 << 20, transcendentals=512 * 8 * 640
        ),
        name="attend",
    )(half, near_core(sent))


def project_mine_kernel(heads_ref, mine_ref, out_ref):
    heads = heads_ref[:, :, :HALF].reshape(4 * TOK, HALF)
    cols = 512
    for j in range(0, D, cols):
        total = dot(heads, mine_ref[:, j : j + cols])
        out_ref[:, :, j : j + cols] = total.reshape(4, TOK, cols)


def project_mine(heads, mine):
    return pl.pallas_call(
        project_mine_kernel,
        out_shape=pltpu.VMEM((4, TOK, D), F32),
        in_specs=[VM] * 2,
        out_specs=VM,
        compiler_params=params(8),
        cost_estimate=pl.CostEstimate(
            flops=2 * 4 * TOK * HALF * D, bytes_accessed=8 << 20, transcendentals=0
        ),
        name="project_mine",
    )(near_core(heads), near_core(mine))


def project_kernel(steps, place_ref, heads_ref, mine_ref, near_ref, far_ref, *out_refs):
    core = place_ref[0]
    blocks = [(place_ref[1] + step) % 4 for step in steps]
    near = pl.multiple_of(HALF + core * QUARTER, QUARTER)
    far = pl.multiple_of(HALF + (1 - core) * QUARTER, QUARTER)

    def heads(first):
        rows = [heads_ref[block, :, pl.ds(first, QUARTER)] for block in blocks]
        return rows[0] if len(rows) == 1 else jnp.concatenate(rows, axis=0)

    second, third = heads(near), heads(far)
    cols = 512
    for j in range(0, D, cols):
        total = dot(second, near_ref[:, j : j + cols]) + dot(third, far_ref[:, j : j + cols])
        for i, block in enumerate(blocks):
            out = total[i * TOK : (i + 1) * TOK] + mine_ref[block, :, j : j + cols]
            out_refs[i][:, j : j + cols] = out.astype(out_refs[i].dtype)


def project(steps, kind, place, heads, mine, near, far):
    return pl.pallas_call(
        functools.partial(project_kernel, steps),
        out_shape=[pltpu.VMEM((TOK, D), kind)] * len(steps),
        in_specs=[SM] + [VM] * 4,
        out_specs=[VM] * len(steps),
        compiler_params=params(8),
        cost_estimate=pl.CostEstimate(
            flops=2 * len(steps) * TOK * HALF * D, bytes_accessed=8 << 20, transcendentals=0
        ),
        name="project",
    )(place, near_core(heads), near_core(mine), near_core(near), near_core(far))


def residual_kernel(
    own_ref, one_ref, two_ref, three_ref, hidden_any, gain_ref, pick1_any, pick2_any,
    att_ref, x_ref, hidden_ref, pick1_ref, pick2_ref, sems
):
    pairs = ((hidden_any, hidden_ref), (pick1_any, pick1_ref), (pick2_any, pick2_ref))
    copies = [pltpu.make_async_copy(a, b, sems.at[i]) for i, (a, b) in enumerate(pairs)]
    for copy in copies:
        copy.start()
    total = own_ref[...] + one_ref[...].astype(F32)
    total = total + (two_ref[...].astype(F32) + three_ref[...].astype(F32))
    copies[0].wait()
    total = total + hidden_ref[...].astype(F32)
    att_ref[...] = total.astype(BF)
    square = jnp.mean(total * total, axis=1, keepdims=True)
    normed = (total / jnp.sqrt(square + 1e-06) * gain_ref[...]).astype(BF)
    stack = jnp.concatenate([normed[:, : D // 2], normed[:, D // 2 :]], axis=0)
    copies[1].wait()
    copies[2].wait()
    rows = 256
    for first in range(0, NE * 8, rows):
        x_ref[first : first + rows, :D] = dot(pick1_ref[first : first + rows], normed).astype(BF)
        x_ref[first : first + rows, D:] = dot(pick2_ref[first : first + rows], stack).astype(BF)


def residual(sums, hidden, gain, pick1, pick2):
    return pl.pallas_call(
        residual_kernel,
        out_shape=(jax.ShapeDtypeStruct((TOK, D), BF), pltpu.VMEM((NE * 8, WIDE), BF)),
        in_specs=[VM] * 4 + [ANY, VM, ANY, ANY],
        out_specs=(VM, VM),
        scratch_shapes=[
            pltpu.VMEM(hidden.shape, BF),
            pltpu.VMEM(pick1.shape, BF),
            pltpu.VMEM(pick2.shape, BF),
            pltpu.SemaphoreType.DMA((3,)),
        ],
        compiler_params=params(12),
        cost_estimate=pl.CostEstimate(flops=1 << 30, bytes_accessed=10 << 20, transcendentals=128),
        name="residual_norm_pick",
    )(
        *(near_core(x) for x in sums),
        far_memory(hidden),
        gain.reshape(1, D),
        far_memory(pick1),
        far_memory(pick2),
    )


def expert_kernel(x_ref, gate_ref, up_ref, down_ref, stat_ref, y_ref):
    rows = 256
    count = rows // 2
    half = D // 2
    to = lax.broadcasted_iota(jnp.int32, (rows, rows), 0)
    at = lax.broadcasted_iota(jnp.int32, (rows, rows), 1)

    def source(i):
        side = (i >= count).astype(jnp.int32)
        own = i - side * count
        return (own >> 2) * 8 + side * 4 + (own & 3)

    sort = jnp.where(source(to) == at, 1.0, 0.0).astype(BF)
    back = jnp.where(source(at) == to, 1.0, 0.0).astype(BF)
    stat = jnp.broadcast_to(stat_ref[...][None], (rows // 8, 8, NE)).reshape(rows, NE).astype(BF)

    def step(i, carry):
        span = pl.ds(pl.multiple_of(i * rows, rows), rows)
        rest = dot(sort, x_ref[span, D:]).astype(BF)
        rest = jnp.concatenate([rest[:count], rest[count:]], axis=1)
        x = jnp.concatenate([x_ref[span, :D], rest], axis=0)
        gate = dot(x, gate_ref[0])
        hidden = (gate / (1.0 + jnp.exp(-gate)) * dot(x, up_ref[0])).astype(BF)
        y = dot(hidden, down_ref[0]).astype(BF)
        y_ref[span, :D] = y[:rows]
        rest = jnp.concatenate([y[rows:, :half], y[rows:, half:]], axis=0)
        y_ref[span, D:WIDE] = dot(back, rest).astype(BF)
        y_ref[span, WIDE:] = stat
        return carry

    lax.fori_loop(0, NE * 8 // rows, step, 0)


def expert_apply(x, w_gate, w_up, w_down, stat):
    return pl.pallas_call(
        expert_kernel,
        out_shape=pltpu.VMEM((NE * 8, WIDE + NE), BF),
        in_specs=[VM] * 5,
        out_specs=VM,
        compiler_params=params(16),
        cost_estimate=pl.CostEstimate(
            flops=6 * NE * CAP * D * FF, bytes_accessed=22 << 20, transcendentals=NE * CAP * FF
        ),
        name="experts",
    )(near_core(x), near_core(w_gate), near_core(w_up), near_core(w_down), near_core(stat))


def mix_kernel(mix1_ref, mix2_ref, y_ref, out_ref, load_ref, loss_ref):
    cols = 512
    for j in range(D // cols):
        at = j * cols
        side = (j // 2) * 2 * TOK
        rest = D + (j % 2) * cols
        both = dot(mix1_ref[...], y_ref[:, at : at + cols])
        both = both + dot(mix2_ref[side : side + 2 * TOK], y_ref[:, rest : rest + cols])
        out_ref[:, at : at + cols] = (both[:TOK] + both[TOK:]).astype(BF)
    stat = jnp.sum(y_ref[:, WIDE:].astype(F32).reshape(NE, 8, NE), axis=0)
    counts = stat[0:1]
    gates = stat[1:2] + stat[2:3]
    tokens = TOK * NE
    load = counts / (tokens * TOP)
    load_ref[...] = NE * load
    loss = NE * jnp.sum(load * (gates / tokens), axis=1, keepdims=True)
    loss_ref[...] = jnp.broadcast_to(loss, (1, NE))


def mix(mix1, mix2, y):
    return pl.pallas_call(
        mix_kernel,
        out_shape=(
            jax.ShapeDtypeStruct((TOK, D), BF),
            jax.ShapeDtypeStruct((1, NE), F32),
            jax.ShapeDtypeStruct((1, NE), F32),
        ),
        in_specs=[VM] * 3,
        out_specs=(VM,) * 3,
        compiler_params=params(12),
        cost_estimate=pl.CostEstimate(flops=2 << 30, bytes_accessed=8 << 20, transcendentals=0),
        name="mix",
    )(near_core(mix1), near_core(mix2), near_core(y))


def swap(x, axis, count, step):
    return lax.ppermute(x, axis, [(i, i ^ step) for i in range(count)])


def turn(x, step):
    return lax.ppermute(x, "ctx", [(i, (i + 2 * step) % CTX) for i in range(CTX)])


def exchange(x, axes, groups=None):
    return lax.all_to_all(
        x, axes, split_axis=0, concat_axis=0, tiled=True, axis_index_groups=groups
    )


def on_device(
    hidden_in, queries, keys, values, out_weight, norm_gain, routes, gates, w_gate, w_up, w_down
):
    place = lax.axis_index("ctx").astype(jnp.int32)
    half = (place % 2).reshape(1)
    core = (lax.axis_index("dp") % 2).astype(jnp.int32).reshape(1)
    place = jnp.concatenate([core, (place // 2).reshape(1)])
    partner_keys = swap(keys, "ctx", CTX, 1)
    partner_values = swap(values, "ctx", CTX, 1)
    sent = send_rows(queries, keys, values, partner_keys, partner_values)
    sent = exchange(sent, "ctx", Z_GROUPS)
    near = swap(send_weight(core, out_weight, partner_keys, partner_values), "ctx", CTX, 1)
    far = swap(near, "dp", 16, 1)
    pick1, pick2, mix1, mix2, stat = route_plan(routes, gates)
    heads = attend(half, sent)
    mine = project_mine(heads, out_weight)
    (two,) = project((2,), BF, place, heads, mine, near, far)
    two = turn(two, 2)
    one, three = project((1, 3), BF, place, heads, mine, near, far)
    one, three = turn(one, 1), turn(three, 3)
    (own,) = project((0,), F32, place, heads, mine, near, far)
    attended, x = residual((own, one, two, three), hidden_in, norm_gain, pick1, pick2)
    x = exchange(x.reshape(NE, 8, WIDE), ALL)
    y = expert_apply(x.reshape(NE * 8, WIDE), w_gate, w_up, w_down, stat)
    y = exchange(y.reshape(NE, 8, WIDE + NE), ALL)
    expert_mix, load, loss = mix(mix1, mix2, y.reshape(NE * 8, WIDE + NE))
    return attended, expert_mix, loss[0, 0], load[0]


def solution(mesh):
    rows = P(ALL, None)
    return jax.shard_map(
        on_device,
        mesh=mesh,
        in_specs=(
            rows,
            rows,
            rows,
            rows,
            P("ctx", None),
            P(),
            rows,
            rows,
            P(ALL, None, None),
            P(ALL, None, None),
            P(ALL, None, None),
        ),
        out_specs=(rows, rows, P(), P()),
        check_vma=False,
    )
```

time: 299 us -> 265 us (0.89)
  waiting for transfers between devices: 58.1 us -> 42.1 us
  Pallas kernels: 51.3 us -> 37.5 us
  local copies, waits for them, and re-layouts: 8.42 us -> 1.65 us
    all_to_all x3 -> x1, waiting for transfers between devices: 41.8 us -> 4 us  [exchange(): lax.all_to_all(x, axes, split_axis=0, concat_axis=0, tiled=True, axis_ind...]
    ppermute x0 -> x3, waiting for transfers between devices: none -> 16.1 us  [turn(): lax.ppermute(x, 'ctx', [(i, (i + 2 * step) % CTX) for i in range(CTX)])]
    pallas_call x6 -> x11, Pallas kernels: 51.3 us -> 37.5 us  [the longest x1 17.1 us: expert_apply(): pl.pallas_call(expert_kernel, out_shape=pltpu.VMEM((NE * 8, WIDE + NE), B...]
    all_to_all x3 -> x1, starting transfers between devices: 12.4 us -> 5.31 us  [exchange(): lax.all_to_all(x, axes, split_axis=0, concat_axis=0, tiled=True, axis_ind...]
    ppermute x2 -> x4, waiting for transfers between devices: 16.4 us -> 21.9 us  [swap(): return lax.ppermute(x, axis, [(i, i ^ step) for i in range(count)])]
    ppermute x0 -> x3, starting transfers between devices: none -> 3.96 us  [turn(): lax.ppermute(x, 'ctx', [(i, (i + 2 * step) % CTX) for i in range(CTX)])]
    ppermute x2 -> x4, starting transfers between devices: 3.19 us -> 6.77 us  [swap(): return lax.ppermute(x, axis, [(i, i ^ step) for i in range(count)])]
    reshape x3 -> x0, local copies, waits for them, and re-layouts: 3.2 us -> none  [the longest x1 1.32 us: on_device(): q = jnp.transpose(queries.reshape(TOK, KV, GH * DH), (1, 0, 2))]
  transfers between devices with their start and end apart: 5 -> 8, of which waited for: 4 -> 7; matrix products, arithmetic and copies ran while one was open for 2% -> 0% of each run, Pallas kernels for 3% -> 5%
where the time goes in v2:
time: 265 us
  blocking collectives  166 us (63%)
  waiting for transfers between devices  42.1 us (16%)
  Pallas kernels  37.5 us (14%)
  starting transfers between devices  16 us (6%)
    all_to_all x2, blocking collectives, exchange(): lax.all_to_all(x, axes, split_axis=0, concat_axis=0, tiled=True, axis_ind...  166 us
    ppermute x4, waiting for transfers between devices, swap(): return lax.ppermute(x, axis, [(i, i ^ step) for i in range(count)])  21.9 us
    pallas_call x1, Pallas kernels, expert_apply(): pl.pallas_call(expert_kernel, out_shape=pltpu.VMEM((NE * 8, WIDE + NE), B...  17.1 us
    ppermute x3, waiting for transfers between devices, turn(): lax.ppermute(x, 'ctx', [(i, (i + 2 * step) % CTX) for i in range(CTX)])  16.1 us
    ppermute x4, starting transfers between devices, swap(): return lax.ppermute(x, axis, [(i, i ^ step) for i in range(count)])  6.77 us
    pallas_call x1, Pallas kernels, attend(): pl.pallas_call(attend_kernel, out_shape=pltpu.VMEM((4, TOK, GH * DH), BF)...  6 us
    all_to_all x1, starting transfers between devices, exchange(): lax.all_to_all(x, axes, split_axis=0, concat_axis=0, tiled=True, axis_ind...  5.31 us
  transfers between devices with their start and end apart: 8, of which 7 were waited for; matrix products, arithmetic and copies ran while one was open for 0% of the time, Pallas kernels for 5%

profile of v2, /device:TPU:0, one launch (start us, length us, event | category | flops | bytes accessed | tf_op | source)
XLA Modules:
  0.0 264.6 jit_solution(883096618084189610)
XLA Ops:
  0.6 3.2 %collective-permute-start = (bf16[128,512]{1,0:T(8,128)(2,1)}, bf16[128,512]{1,0:T(8,128)(2,1)S(1)}, u32[]{:S(2)}, u32[]{:S(2)}) collective-permute-start(bf16[128,512]{1,0:T(8,128)(2,1)} %keys_ref.1), channel_id=1, source_target_pairs={{0,1},{1,0},{2,3},{3,2},{4,5},{5,4},{6,7},{7,6},{8,9},{9,8},{10,11... | collective-permute-start | bytes 393224 | tf_op jit(solution)/shard_map/ppermute | solution.py:393
  3.8 0.4 collective-permute-start.1
  4.2 3.8 %collective-permute-done.partner_keys_ref.first_ref = bf16[128,512]{1,0:T(8,128)(2,1)S(1)} collective-permute-done((bf16[128,512]{1,0:T(8,128)(2,1)}, bf16[128,512]{1,0:T(8,128)(2,1)S(1)}, u32[]{:S(2)}, u32[]{:S(2)}) %collective-permute-start) | collective-permute-done | bytes 131104 | tf_op jit(solution)/shard_map/ppermute | solution.py:393
  8.0 2.5 collective-permute-done.1.partner_values_ref.second_ref
  10.5 1.6 copy-done
  12.1 0.1 send_weight.1
  12.2 3.2 %collective-permute-start.2 = (bf16[256,2048]{1,0:T(8,128)(2,1)S(1)}, bf16[256,2048]{1,0:T(8,128)(2,1)S(1)}, u32[]{:S(2)}, u32[]{:S(2)}) collective-permute-start(bf16[256,2048]{1,0:T(8,128)(2,1)S(1)} %send_weight.1), channel_id=1, source_target_pairs={{0,1},{1,0},{2,3},{3,2},{4,5},{5,4},{6,7},{7,6},{8,9},{9,8},{10,11... | collective-permute-start | bytes 3145736 | tf_op jit(solution)/shard_map/ppermute | solution.py:393
  15.4 1.3 send_rows.1
  16.7 5.3 %all-to-all-start = ((bf16[4,128,1536]{2,1,0:T(8,128)(2,1)}), bf16[4,128,1536]{2,1,0:T(8,128)(2,1)}, u32[]{:S(2)}, u32[]{:S(2)}) async-start(bf16[4,128,1536]{2,1,0:T(8,128)(2,1)} %send_rows.1), calls=%async_computation | async-start | bytes 3145728 | tf_op jit(solution)/shard_map/all_to_all | solution.py:401
  22.0 15.7 %collective-permute-done.2.near_ref = bf16[256,2048]{1,0:T(8,128)(2,1)S(1)} collective-permute-done((bf16[256,2048]{1,0:T(8,128)(2,1)S(1)}, bf16[256,2048]{1,0:T(8,128)(2,1)S(1)}, u32[]{:S(2)}, u32[]{:S(2)}) %collective-permute-start.2) | collective-permute-done | bytes 1048608 | tf_op jit(solution)/shard_map/ppermute | solution.py:393
  37.6 0.1 pad_add_fusion.place_ref
  37.7 4.0 %all-to-all-done.sent_ref = bf16[4,128,1536]{2,1,0:T(8,128)(2,1)} async-done(((bf16[4,128,1536]{2,1,0:T(8,128)(2,1)}), bf16[4,128,1536]{2,1,0:T(8,128)(2,1)}, u32[]{:S(2)}, u32[]{:S(2)}) %all-to-all-start) | async-done | bytes 1572896 | tf_op jit(solution)/shard_map/all_to_all | solution.py:401
  41.7 6.0 %attend.1.heads_ref = bf16[4,128,1024]{2,1,0:T(8,128)(2,1)S(1)} custom-call(s32[1]{0:T(128)} %bitcast.2.half_ref, bf16[4,128,1536]{2,1,0:T(8,128)(2,1)} %all-to-all-done.sent_ref), custom_call_target="tpu_custom_call" | custom-call | flops 1342177280 | bytes 3145728 | tf_op jit(solution)/shard_map/attend/pallas_call | solution.py:194
  47.7 1.3 project_mine.1.mine_ref
  49.0 1.0 project.5
  50.0 0.0 copy-start.7
  50.0 0.0 copy-start.8
  50.0 0.5 collective-permute-start.5
  50.6 1.3 project.4
  51.8 1.6 collective-permute-start.4
  53.4 1.9 collective-permute-start.6
  55.3 2.2 route_plan.1
  57.4 1.0 project.3.own_ref
  58.4 8.1 %collective-permute-done.5.two_ref = bf16[128,2048]{1,0:T(8,128)(2,1)S(1)} collective-permute-done((bf16[128,2048]{1,0:T(8,128)(2,1)S(1)}, bf16[128,2048]{1,0:T(8,128)(2,1)S(1)}, u32[]{:S(2)}, u32[]{:S(2)}) %collective-permute-start.5) | collective-permute-done | bytes 524320 | tf_op jit(solution)/shard_map/ppermute | solution.py:397
  66.5 7.6 %collective-permute-done.4.one_ref = bf16[128,2048]{1,0:T(8,128)(2,1)S(1)} collective-permute-done((bf16[128,2048]{1,0:T(8,128)(2,1)S(1)}, bf16[128,2048]{1,0:T(8,128)(2,1)S(1)}, u32[]{:S(2)}, u32[]{:S(2)}) %collective-permute-start.4) | collective-permute-done | bytes 524320 | tf_op jit(solution)/shard_map/ppermute | solution.py:397
  74.1 0.5 collective-permute-done.6.three_ref
  74.6 3.2 %residual_norm_pick.1 = (bf16[128,2048]{1,0:T(8,128)(2,1)}, bf16[1024,3072]{1,0:T(8,128)(2,1)S(1)}) custom-call(f32[128,2048]{1,0:T(8,128)S(1)} %project.3.own_ref, bf16[128,2048]{1,0:T(8,128)(2,1)S(1)} %collective-permute-done.4.one_ref, bf16[128,2048]{1,0:T(8,128)(2,1)S(1)} %collective-permute-done.5.two_ref, ...), custom_call_target="tpu_custom_call" | custom-call | flops 1073741824 | bytes 10485760 | tf_op jit(solution)/shard_map/residual_norm_pick/pallas_call | solution.py:287
  77.8 0.0 copy-start.10
  77.9 84.0 %all_to_all.15 = bf16[128,8,3072]{2,1,0:T(8,128)(2,1)S(1)} all-to-all(bf16[128,8,3072]{2,1,0:T(8,128)(2,1)S(1)} %bitcast.15), channel_id=1, replica_groups=mesh['dp'=16,'ctx'=8] {'dp','ctx'}, dimensions={0} | all-to-all | bytes 12582912 | tf_op jit(solution)/shard_map/all_to_all | solution.py:401
  161.9 17.1 %experts.1 = bf16[1024,3200]{1,0:T(8,128)(2,1)S(1)} custom-call(bf16[1024,3072]{1,0:T(8,128)(2,1)S(1)} %bitcast.16, bf16[1,2048,768]{2,1,0:T(8,128)(2,1)S(1)} %copy-done.9, bf16[1,2048,768]{2,1,0:T(8,128)(2,1)S(1)} %copy-done.10, bf16[1,768,2048]{2,1,0:T(8,128)(2,1)S(1)} %copy-done.11, f32[8,128]{1,0:T(8,128)S(1)} %copy-done.13), custom_call_target="tpu_custom_call" | custom-call | flops 14495514624 | bytes 23068672 | tf_op jit(solution)/shard_map/experts/pallas_call | solution.py:344
  179.0 82.4 %all_to_all.16 = bf16[128,8,3200]{2,1,0:T(8,128)(2,1)S(1)} all-to-all(bf16[128,8,3200]{2,1,0:T(8,128)(2,1)S(1)} %bitcast.14), channel_id=1, replica_groups=mesh['dp'=16,'ctx'=8] {'dp','ctx'}, dimensions={0} | all-to-all | bytes 13107200 | tf_op jit(solution)/shard_map/all_to_all | solution.py:401
  261.4 3.1 %mix.1 = (bf16[128,2048]{1,0:T(8,128)(2,1)}, f32[1,128]{1,0:T(1,128)}, f32[1,128]{1,0:T(1,128)}) custom-call(bf16[256,1024]{1,0:T(8,128)(2,1)S(1)} %copy-done.4, bf16[512,1024]{1,0:T(8,128)(2,1)S(1)} %copy-done.3, bf16[1024,3200]{1,0:T(8,128)(2,1)S(1)} %bitcast.13), custom_call_target="tpu_custom_call" | custom-call | flops 2147483648 | bytes 8388608 | tf_op jit(solution)/shard_map/mix/pallas_call | solution.py:377
  (26 shorter events, 0.1 us)
Async XLA Ops:
  0.6 7.4 %collective-permute-start = (bf16[128,512]{1,0:T(8,128)(2,1)}, bf16[128,512]{1,0:T(8,128)(2,1)S(1)}, u32[]{:S(2)}, u32[]{:S(2)}) collective-permute-start(bf16[128,512]{1,0:T(8,128)(2,1)} %keys_ref.1), channel_id=1, source_target_pairs={{0,1},{1,0},{2,3},{3,2},{4,5},{5,4},{6,7},{7,6},{8,9},{9,8},{10,11... | collective-permute-start | bytes 393224 | tf_op jit(solution)/shard_map/ppermute | solution.py:393
  3.8 6.7 %collective-permute-start.1 = (bf16[128,512]{1,0:T(8,128)(2,1)}, bf16[128,512]{1,0:T(8,128)(2,1)S(1)}, u32[]{:S(2)}, u32[]{:S(2)}) collective-permute-start(bf16[128,512]{1,0:T(8,128)(2,1)} %values_ref.1), channel_id=1, source_target_pairs={{0,1},{1,0},{2,3},{3,2},{4,5},{5,4},{6,7},{7,6},{8,9},{9,8},{10,11... | collective-permute-start | bytes 393224 | tf_op jit(solution)/shard_map/ppermute | solution.py:393
  10.5 1.6 copy-start
  12.1 3.3 %copy-start.2 = (bf16[128,4096]{1,0:T(8,128)(2,1)S(1)}, bf16[128,4096]{1,0:T(8,128)(2,1)}, u32[]{:S(2)}) copy-start(bf16[128,4096]{1,0:T(8,128)(2,1)} %q_ref.1) | copy-start | bytes 3145732
  12.1 3.3 %copy-start.5 = (bf16[128,512]{1,0:T(8,128)(2,1)S(1)}, bf16[128,512]{1,0:T(8,128)(2,1)}, u32[]{:S(2)}) copy-start(bf16[128,512]{1,0:T(8,128)(2,1)} %keys_ref.1) | copy-start | bytes 393220
  12.1 3.3 %copy-start.6 = (bf16[128,512]{1,0:T(8,128)(2,1)S(1)}, bf16[128,512]{1,0:T(8,128)(2,1)}, u32[]{:S(2)}) copy-start(bf16[128,512]{1,0:T(8,128)(2,1)} %values_ref.1) | copy-start | bytes 393220
  12.2 25.4 %collective-permute-start.2 = (bf16[256,2048]{1,0:T(8,128)(2,1)S(1)}, bf16[256,2048]{1,0:T(8,128)(2,1)S(1)}, u32[]{:S(2)}, u32[]{:S(2)}) collective-permute-start(bf16[256,2048]{1,0:T(8,128)(2,1)S(1)} %send_weight.1), channel_id=1, source_target_pairs={{0,1},{1,0},{2,3},{3,2},{4,5},{5,4},{6,7},{7,6},{8,9},{9,8},{10,11... | collective-permute-start | bytes 3145736 | tf_op jit(solution)/shard_map/ppermute | solution.py:393
  16.7 25.1 %all-to-all-start = ((bf16[4,128,1536]{2,1,0:T(8,128)(2,1)}), bf16[4,128,1536]{2,1,0:T(8,128)(2,1)}, u32[]{:S(2)}, u32[]{:S(2)}) async-start(bf16[4,128,1536]{2,1,0:T(8,128)(2,1)} %send_rows.1), calls=%async_computation | async-start | bytes 3145728 | tf_op jit(solution)/shard_map/all_to_all | solution.py:401
  37.6 11.4 %collective-permute-start.3 = (bf16[256,2048]{1,0:T(8,128)(2,1)S(1)}, bf16[256,2048]{1,0:T(8,128)(2,1)S(1)}, u32[]{:S(2)}, u32[]{:S(2)}) collective-permute-start(bf16[256,2048]{1,0:T(8,128)(2,1)S(1)} %collective-permute-done.2.near_ref), channel_id=1, source_target_pairs={{0,8},{8,0},{16,24},{24,16},{32,40},{40,32},{48,56},{56,48},{64,72... | collective-permute-start | bytes 3145736 | tf_op jit(solution)/shard_map/ppermute | solution.py:393
  41.7 6.0 %copy-start.1 = (bf16[512,2048]{1,0:T(8,128)(2,1)S(1)}, bf16[512,2048]{1,0:T(8,128)(2,1)}, u32[]{:S(2)}) copy-start(bf16[512,2048]{1,0:T(8,128)(2,1)} %weight_ref.1) | copy-start | bytes 6291460
  50.0 5.3 %copy-start.7 = (s32[128,8]{0,1:T(8,128)S(1)}, s32[128,8]{0,1:T(8,128)}, u32[]{:S(2)}) copy-start(s32[128,8]{0,1:T(8,128)} %param.17) | copy-start | bytes 12292
  50.0 5.3 %copy-start.8 = (f32[128,8]{0,1:T(8,128)S(1)}, f32[128,8]{0,1:T(8,128)}, u32[]{:S(2)}) copy-start(f32[128,8]{0,1:T(8,128)} %param.18) | copy-start | bytes 12292
  50.0 16.5 %collective-permute-start.5 = (bf16[128,2048]{1,0:T(8,128)(2,1)S(1)}, bf16[128,2048]{1,0:T(8,128)(2,1)S(1)}, u32[]{:S(2)}, u32[]{:S(2)}) collective-permute-start(bf16[128,2048]{1,0:T(8,128)(2,1)S(1)} %project.5), channel_id=1, source_target_pairs={{0,4},{1,5},{2,6},{3,7},{4,0},{5,1},{6,2},{7,3},{8,12},{9,13},{10,... | collective-permute-start | bytes 1572872 | tf_op jit(solution)/shard_map/ppermute | solution.py:397
  51.8 22.3 %collective-permute-start.4 = (bf16[128,2048]{1,0:T(8,128)(2,1)S(1)}, bf16[128,2048]{1,0:T(8,128)(2,1)S(1)}, u32[]{:S(2)}, u32[]{:S(2)}) collective-permute-start(bf16[128,2048]{1,0:T(8,128)(2,1)S(1)} %get-tuple-element.16), channel_id=1, source_target_pairs={{0,2},{1,3},{2,4},{3,5},{4,6},{5,7},{6,0},{7,1},{8,10},{9,11},{10,... | collective-permute-start | bytes 1572872 | tf_op jit(solution)/shard_map/ppermute | solution.py:397
  53.4 21.2 %collective-permute-start.6 = (bf16[128,2048]{1,0:T(8,128)(2,1)S(1)}, bf16[128,2048]{1,0:T(8,128)(2,1)S(1)}, u32[]{:S(2)}, u32[]{:S(2)}) collective-permute-start(bf16[128,2048]{1,0:T(8,128)(2,1)S(1)} %get-tuple-element.17), channel_id=1, source_target_pairs={{0,6},{1,7},{2,0},{3,1},{4,2},{5,3},{6,4},{7,5},{8,14},{9,15},{10,... | collective-permute-start | bytes 1572872 | tf_op jit(solution)/shard_map/ppermute | solution.py:397
  57.4 17.1 %copy-start.12 = (f32[2048]{0:T(1024)S(1)}, f32[2048]{0:T(1024)}, u32[]{:S(2)}) copy-start(f32[2048]{0:T(1024)} %param.16) | copy-start | bytes 24580
  77.8 84.1 %copy-start.9 = (bf16[1,2048,768]{2,1,0:T(8,128)(2,1)S(1)}, bf16[1,2048,768]{2,1,0:T(8,128)(2,1)}, u32[]{:S(2)}) copy-start(bf16[1,2048,768]{2,1,0:T(8,128)(2,1)} %gate_ref.1) | copy-start | bytes 9437188
  77.8 84.1 %copy-start.10 = (bf16[1,2048,768]{2,1,0:T(8,128)(2,1)S(1)}, bf16[1,2048,768]{2,1,0:T(8,128)(2,1)}, u32[]{:S(2)}) copy-start(bf16[1,2048,768]{2,1,0:T(8,128)(2,1)} %up_ref.1) | copy-start | bytes 9437188
  77.8 84.1 %copy-start.11 = (bf16[1,768,2048]{2,1,0:T(8,128)(2,1)S(1)}, bf16[1,768,2048]{2,1,0:T(8,128)(2,1)}, u32[]{:S(2)}) copy-start(bf16[1,768,2048]{2,1,0:T(8,128)(2,1)} %down_ref.1) | copy-start | bytes 9437188
  77.8 84.1 %copy-start.13 = (f32[8,128]{1,0:T(8,128)S(1)}, f32[8,128]{1,0:T(8,128)}, u32[]{:S(2)}) copy-start(f32[8,128]{1,0:T(8,128)} %get-tuple-element.24.stat_ref) | copy-start | bytes 12292
  179.0 82.4 %copy-start.3 = (bf16[512,1024]{1,0:T(8,128)(2,1)S(1)}, bf16[512,1024]{1,0:T(8,128)(2,1)}, u32[]{:S(2)}) copy-start(bf16[512,1024]{1,0:T(8,128)(2,1)} %get-tuple-element.22.mix2_ref) | copy-start | bytes 3145732
  179.0 82.4 %copy-start.4 = (bf16[256,1024]{1,0:T(8,128)(2,1)S(1)}, bf16[256,1024]{1,0:T(8,128)(2,1)}, u32[]{:S(2)}) copy-start(bf16[256,1024]{1,0:T(8,128)(2,1)} %get-tuple-element.21.mix1_ref) | copy-start | bytes 1572868

commit v3 on v2

--- a/solution.py
+++ b/solution.py
@@ -18,14 +18,13 @@
 NE = 128
 CTX = 8
 GH = H // KV
-SENT = GH * DH + 4 * DH
+SENT = GH * DH + 2 * DH
 HALF = 512
 WHOLE = 8
 CAP = 12
 QUARTER = 256
 WIDE = 3072
 ALL = ("dp", "ctx")
-Z_GROUPS = [[0, 2, 4, 6], [1, 3, 5, 7]]
 BF = jnp.bfloat16
 F32 = jnp.float32
 def params(megabytes):
@@ -107,57 +106,83 @@
     )(routes.T, gates.T)
 
 
-def send_kernel(q_ref, keys_ref, values_ref, partner_keys_ref, partner_values_ref, out_ref):
-    parts = (keys_ref, values_ref, partner_keys_ref, partner_values_ref)
+def send_kernel(place_ref, q_ref, keys_ref, values_ref, weight_ref, *refs):
+    out_refs, weight_out, sems = refs[:4], refs[4], refs[5]
     wide = GH * DH
-    for group in range(KV):
-        out_ref[group, :, :wide] = q_ref[:, group * wide : (group + 1) * wide]
-        for i, ref in enumerate(parts):
-            first = wide + i * DH
-            out_ref[group, :, first : first + DH] = ref[:, group * DH : (group + 1) * DH]
-
-
-def send_rows(*arrays):
+    copies = []
+
+    def fetch(source, target):
+        copies.append(pltpu.make_async_copy(source, target, sems.at[len(copies)]))
+        copies[-1].start()
+
+    for step, out_ref in enumerate(out_refs):
+        group = (place_ref[1] + step) % 4
+        cols = pl.ds(pl.multiple_of(group * DH, DH), DH)
+        fetch(q_ref.at[:, pl.ds(pl.multiple_of(group * wide, wide), wide)], out_ref.at[:, :wide])
+        fetch(keys_ref.at[:, cols], out_ref.at[:, wide : wide + DH])
+        fetch(values_ref.at[:, cols], out_ref.at[:, wide + DH :])
+    rows = pl.ds(pl.multiple_of(place_ref[0] * QUARTER, QUARTER), QUARTER)
+    fetch(weight_ref.at[rows], weight_out)
+    for copy in copies:
+        copy.wait()
+
+
+def send_all(place, queries, keys, values, weight):
     return pl.pallas_call(
         send_kernel,
-        out_shape=jax.ShapeDtypeStruct((KV, TOK, SENT), BF),
-        in_specs=[VM] * 5,
+        out_shape=[pltpu.VMEM((TOK, SENT), BF)] * 4 + [pltpu.VMEM((QUARTER, D), BF)],
+        in_specs=[SM] + [ANY] * 4,
+        out_specs=[VM] * 5,
+        scratch_shapes=[pltpu.SemaphoreType.DMA((13,))],
+        compiler_params=params(4),
+        name="send_all",
+    )(place, *(far_memory(x) for x in (queries, keys, values, weight)))
+
+
+def own_keys_kernel(place_ref, *refs):
+    for step in range(4):
+        refs[4][(place_ref[1] + 4 - step) % 4] = refs[step][:, GH * DH :]
+
+
+def own_keys(place, blocks):
+    return pl.pallas_call(
+        own_keys_kernel,
+        out_shape=pltpu.VMEM((4, TOK, 2 * DH), BF),
+        in_specs=[SM] + [VM] * 4,
         out_specs=VM,
         compiler_params=params(4),
-        name="send_rows",
-    )(*(near_core(x) for x in arrays))
-
-
-def send_weight_kernel(core_ref, weight_ref, first_ref, second_ref, out_ref, sem):
-    del first_ref, second_ref
-    rows = pl.ds(pl.multiple_of(core_ref[0] * QUARTER, QUARTER), QUARTER)
-    copy = pltpu.make_async_copy(weight_ref.at[rows], out_ref, sem)
-    copy.start()
-    copy.wait()
-
-
-def send_weight(core, weight, first, second):
-    return pl.pallas_call(
-        send_weight_kernel,
-        out_shape=jax.ShapeDtypeStruct((QUARTER, D), BF),
-        in_specs=[SM, ANY, ANY, ANY],
+        name="own_keys",
+    )(place, *(near_core(x) for x in blocks))
+
+
+def later_kernel(x_ref, after_ref, out_ref):
+    del x_ref, after_ref, out_ref
+
+
+def later(x, after):
+    return pl.pallas_call(
+        later_kernel,
+        out_shape=jax.ShapeDtypeStruct(x.shape, x.dtype),
+        in_specs=[ANY, ANY],
         out_specs=ANY,
-        scratch_shapes=[pltpu.SemaphoreType.DMA],
+        input_output_aliases={0: 0},
         compiler_params=params(4),
-        name="send_weight",
-    )(core, weight, first, second)
-
-
-def attend_kernel(half_ref, sent_ref, out_ref):
-    half = half_ref[0]
-    one = jnp.ones((4 * TOK, DH), BF)
-
-    def piece(i):
-        first = GH * DH + i * DH
-        return jnp.concatenate([sent_ref[z, :, first : first + DH] for z in range(4)], axis=0)
-
-    keys = [piece(0), piece(2)]
-    values = [jnp.concatenate([piece(i), one], axis=1) for i in (1, 3)]
+        name="later",
+    )(x, after)
+
+
+def attend_kernel(place_ref, zero_ref, one_ref, two_ref, three_ref, own_ref, partner_ref, out_ref, q_ref):
+    half = place_ref[2]
+    first = pl.ds(pl.multiple_of(half * HALF, HALF), HALF)
+    second = pl.ds(pl.multiple_of((1 - half) * HALF, HALF), HALF)
+    for step, ref in enumerate((zero_ref, one_ref, two_ref, three_ref)):
+        at = (place_ref[1] + 4 - step) % 4
+        q_ref[at, :, :HALF] = ref[:, first]
+        q_ref[at, :, HALF:] = ref[:, second]
+    ones = jnp.ones((4 * TOK, DH), BF)
+    sides = [ref[...].reshape(4 * TOK, 2 * DH) for ref in (own_ref, partner_ref)]
+    keys = [side[:, :DH] for side in sides]
+    values = [jnp.concatenate([side[:, DH:], ones], axis=1) for side in sides]
     scale = math.log2(math.e) / math.sqrt(DH)
     below = lax.broadcasted_iota(jnp.int32, (TOK, TOK), 1) <= lax.broadcasted_iota(
         jnp.int32, (TOK, TOK), 0
@@ -165,9 +190,7 @@
     for block in range(4):
         upto = (block + 1) * TOK
         for head in range(GH):
-            part, inner = divmod(head, GH // 2)
-            first = (half if part == 0 else 1 - half) * HALF + inner * DH
-            q = sent_ref[block, :, pl.ds(pl.multiple_of(first, DH), DH)]
+            q = q_ref[block, :, head * DH : (head + 1) * DH]
             scores = []
             for side in range(2):
                 score = lax.dot_general(
@@ -190,18 +213,19 @@
             ).astype(BF)
 
 
-def attend(half, sent):
+def attend(place, blocks, own, partner):
     return pl.pallas_call(
         attend_kernel,
         out_shape=pltpu.VMEM((4, TOK, GH * DH), BF),
-        in_specs=[SM, VM],
+        in_specs=[SM] + [VM] * 6,
         out_specs=VM,
+        scratch_shapes=[pltpu.VMEM((4, TOK, GH * DH), BF)],
         compiler_params=params(16),
         cost_estimate=pl.CostEstimate(
             flops=2 * 2 * 512 * 8 * 640 * 128, bytes_accessed=3 << 20, transcendentals=512 * 8 * 640
         ),
         name="attend",
-    )(half, near_core(sent))
+    )(place, *(near_core(x) for x in (*blocks, own, partner)))
 
 
 def project_mine_kernel(heads_ref, mine_ref, out_ref):
@@ -226,7 +250,7 @@
     )(near_core(heads), near_core(mine))
 
 
-def project_kernel(steps, place_ref, heads_ref, mine_ref, near_ref, far_ref, *out_refs):
+def project_kernel(steps, wanted, place_ref, heads_ref, mine_ref, near_ref, far_ref, *out_refs):
     core = place_ref[0]
     blocks = [(place_ref[1] + step) % 4 for step in steps]
     near = pl.multiple_of(HALF + core * QUARTER, QUARTER)
@@ -240,17 +264,18 @@
     cols = 512
     for j in range(0, D, cols):
         total = dot(second, near_ref[:, j : j + cols]) + dot(third, far_ref[:, j : j + cols])
-        for i, block in enumerate(blocks):
-            out = total[i * TOK : (i + 1) * TOK] + mine_ref[block, :, j : j + cols]
-            out_refs[i][:, j : j + cols] = out.astype(out_refs[i].dtype)
-
-
-def project(steps, kind, place, heads, mine, near, far):
-    return pl.pallas_call(
-        functools.partial(project_kernel, steps),
-        out_shape=[pltpu.VMEM((TOK, D), kind)] * len(steps),
+        for (i, low, high, kind), out_ref in zip(wanted, out_refs):
+            if low <= j < high:
+                out = total[i * TOK : (i + 1) * TOK] + mine_ref[blocks[i], :, j : j + cols]
+                out_ref[:, j - low : j - low + cols] = out.astype(kind)
+
+
+def project(steps, wanted, place, heads, mine, near, far):
+    return pl.pallas_call(
+        functools.partial(project_kernel, steps, wanted),
+        out_shape=[pltpu.VMEM((TOK, high - low), kind) for _, low, high, kind in wanted],
         in_specs=[SM] + [VM] * 4,
-        out_specs=[VM] * len(steps),
+        out_specs=[VM] * len(wanted),
         compiler_params=params(8),
         cost_estimate=pl.CostEstimate(
             flops=2 * len(steps) * TOK * HALF * D, bytes_accessed=8 << 20, transcendentals=0
@@ -259,16 +284,46 @@
     )(place, near_core(heads), near_core(mine), near_core(near), near_core(far))
 
 
+def join_kernel(a_ref, b_ref, c_ref, d_ref, left_ref, right_ref):
+    left_ref[...] = (a_ref[...] + b_ref[...].astype(F32)).astype(BF)
+    right_ref[...] = (c_ref[...] + d_ref[...].astype(F32)).astype(BF)
+
+
+def join(*parts):
+    return pl.pallas_call(
+        join_kernel,
+        out_shape=[pltpu.VMEM((TOK, D // 2), BF)] * 2,
+        in_specs=[VM] * 4,
+        out_specs=[VM] * 2,
+        compiler_params=params(4),
+        name="join",
+    )(*(near_core(x) for x in parts))
+
+
+def sum_over_z(place, heads, mine, near, far):
+    half = D // 2
+    operands = (place, heads, mine, near, far)
+    left, right = project((2,), ((0, 0, half, BF), (0, half, D, BF)), *operands)
+    left, right = turn(left, 1), turn(right, 3)
+    wanted = ((0, half, D, BF), (1, 0, half, BF), (0, 0, half, F32), (1, half, D, F32))
+    up_right, down_left, up_left, down_right = project((1, 3), wanted, *operands)
+    up_right, down_left = turn(up_right, 1), turn(down_left, 3)
+    (own,) = project((0,), ((0, 0, D, F32),), *operands)
+    up_left, down_right = join(up_left, left, down_right, right)
+    return own, turn(up_left, 1), up_right, down_left, turn(down_right, 3)
+
+
 def residual_kernel(
-    own_ref, one_ref, two_ref, three_ref, hidden_any, gain_ref, pick1_any, pick2_any,
+    own_ref, up_left_ref, up_right_ref, down_left_ref, down_right_ref, hidden_any, gain_ref, pick1_any, pick2_any,
     att_ref, x_ref, hidden_ref, pick1_ref, pick2_ref, sems
 ):
     pairs = ((hidden_any, hidden_ref), (pick1_any, pick1_ref), (pick2_any, pick2_ref))
     copies = [pltpu.make_async_copy(a, b, sems.at[i]) for i, (a, b) in enumerate(pairs)]
     for copy in copies:
         copy.start()
-    total = own_ref[...] + one_ref[...].astype(F32)
-    total = total + (two_ref[...].astype(F32) + three_ref[...].astype(F32))
+    left = up_left_ref[...].astype(F32) + down_left_ref[...].astype(F32)
+    right = up_right_ref[...].astype(F32) + down_right_ref[...].astype(F32)
+    total = own_ref[...] + jnp.concatenate([left, right], axis=1)
     copies[0].wait()
     total = total + hidden_ref[...].astype(F32)
     att_ref[...] = total.astype(BF)
@@ -287,7 +342,7 @@
     return pl.pallas_call(
         residual_kernel,
         out_shape=(jax.ShapeDtypeStruct((TOK, D), BF), pltpu.VMEM((NE * 8, WIDE), BF)),
-        in_specs=[VM] * 4 + [ANY, VM, ANY, ANY],
+        in_specs=[VM] * 5 + [ANY, VM, ANY, ANY],
         out_specs=(VM, VM),
         scratch_shapes=[
             pltpu.VMEM(hidden.shape, BF),
@@ -308,11 +363,12 @@
 
 
 def expert_kernel(x_ref, gate_ref, up_ref, down_ref, stat_ref, y_ref):
-    rows = 256
-    count = rows // 2
+    rows = 512
+    piece = 256
+    count = piece // 2
     half = D // 2
-    to = lax.broadcasted_iota(jnp.int32, (rows, rows), 0)
-    at = lax.broadcasted_iota(jnp.int32, (rows, rows), 1)
+    to = lax.broadcasted_iota(jnp.int32, (piece, piece), 0)
+    at = lax.broadcasted_iota(jnp.int32, (piece, piece), 1)
 
     def source(i):
         side = (i >= count).astype(jnp.int32)
@@ -324,16 +380,22 @@
     stat = jnp.broadcast_to(stat_ref[...][None], (rows // 8, 8, NE)).reshape(rows, NE).astype(BF)
 
     def step(i, carry):
-        span = pl.ds(pl.multiple_of(i * rows, rows), rows)
-        rest = dot(sort, x_ref[span, D:]).astype(BF)
-        rest = jnp.concatenate([rest[:count], rest[count:]], axis=1)
-        x = jnp.concatenate([x_ref[span, :D], rest], axis=0)
+        base = i * rows
+        span = pl.ds(pl.multiple_of(base, rows), rows)
+        pieces = [pl.ds(pl.multiple_of(base + p, piece), piece) for p in range(0, rows, piece)]
+        parts = [x_ref[span, :D]]
+        for at in pieces:
+            rest = dot(sort, x_ref[at, D:]).astype(BF)
+            parts.append(jnp.concatenate([rest[:count], rest[count:]], axis=1))
+        x = jnp.concatenate(parts, axis=0)
         gate = dot(x, gate_ref[0])
         hidden = (gate / (1.0 + jnp.exp(-gate)) * dot(x, up_ref[0])).astype(BF)
         y = dot(hidden, down_ref[0]).astype(BF)
         y_ref[span, :D] = y[:rows]
-        rest = jnp.concatenate([y[rows:, :half], y[rows:, half:]], axis=0)
-        y_ref[span, D:WIDE] = dot(back, rest).astype(BF)
+        for p, at in enumerate(pieces):
+            rest = y[rows + p * count : rows + (p + 1) * count]
+            rest = jnp.concatenate([rest[:, :half], rest[:, half:]], axis=0)
+            y_ref[at, D:WIDE] = dot(back, rest).astype(BF)
         y_ref[span, WIDE:] = stat
         return carry
 
@@ -397,37 +459,31 @@
     return lax.ppermute(x, "ctx", [(i, (i + 2 * step) % CTX) for i in range(CTX)])
 
 
-def exchange(x, axes, groups=None):
-    return lax.all_to_all(
-        x, axes, split_axis=0, concat_axis=0, tiled=True, axis_index_groups=groups
-    )
+def exchange(x):
+    return lax.all_to_all(x, ALL, split_axis=0, concat_axis=0, tiled=True)
 
 
 def on_device(
     hidden_in, queries, keys, values, out_weight, norm_gain, routes, gates, w_gate, w_up, w_down
 ):
-    place = lax.axis_index("ctx").astype(jnp.int32)
-    half = (place % 2).reshape(1)
-    core = (lax.axis_index("dp") % 2).astype(jnp.int32).reshape(1)
-    place = jnp.concatenate([core, (place // 2).reshape(1)])
-    partner_keys = swap(keys, "ctx", CTX, 1)
-    partner_values = swap(values, "ctx", CTX, 1)
-    sent = send_rows(queries, keys, values, partner_keys, partner_values)
-    sent = exchange(sent, "ctx", Z_GROUPS)
-    near = swap(send_weight(core, out_weight, partner_keys, partner_values), "ctx", CTX, 1)
+    spot = lax.axis_index("ctx").astype(jnp.int32)
+    core = lax.axis_index("dp").astype(jnp.int32) % 2
+    place = jnp.stack([core, spot // 2, spot % 2])
+    *blocks, weight = send_all(place, queries, keys, values, out_weight)
+    near = swap(weight, "ctx", CTX, 1)
+    blocks = [blocks[0]] + [turn(blocks[step], step) for step in (1, 2, 3)]
+    own = own_keys(place, blocks)
+    partner = swap(own, "ctx", CTX, 1)
+    near = later(near, partner)
     far = swap(near, "dp", 16, 1)
     pick1, pick2, mix1, mix2, stat = route_plan(routes, gates)
-    heads = attend(half, sent)
+    heads = attend(place, blocks, own, partner)
     mine = project_mine(heads, out_weight)
-    (two,) = project((2,), BF, place, heads, mine, near, far)
-    two = turn(two, 2)
-    one, three = project((1, 3), BF, place, heads, mine, near, far)
-    one, three = turn(one, 1), turn(three, 3)
-    (own,) = project((0,), F32, place, heads, mine, near, far)
-    attended, x = residual((own, one, two, three), hidden_in, norm_gain, pick1, pick2)
-    x = exchange(x.reshape(NE, 8, WIDE), ALL)
+    sums = sum_over_z(place, heads, mine, near, far)
+    attended, x = residual(sums, hidden_in, norm_gain, pick1, pick2)
+    x = exchange(x.reshape(NE, 8, WIDE))
     y = expert_apply(x.reshape(NE * 8, WIDE), w_gate, w_up, w_down, stat)
-    y = exchange(y.reshape(NE, 8, WIDE + NE), ALL)
+    y = exchange(y.reshape(NE, 8, WIDE + NE))
     expert_mix, load, loss = mix(mix1, mix2, y.reshape(NE * 8, WIDE + NE))
     return attended, expert_mix, loss[0, 0], load[0]
 

time: 265 us -> 255 us (0.962)
  waiting for transfers between devices: 42.1 us -> 27.8 us
  starting transfers between devices: 16 us -> 21.6 us
    ppermute x4 -> x3, waiting for transfers between devices: 21.9 us -> 7.95 us  [swap(): return lax.ppermute(x, axis, [(i, i ^ step) for i in range(count)])]
    ppermute x3 -> x9, starting transfers between devices: 3.96 us -> 17.8 us  [turn(): lax.ppermute(x, 'ctx', [(i, (i + 2 * step) % CTX) for i in range(CTX)])]
    all_to_all x1 -> x0, starting transfers between devices: 5.31 us -> none  [exchange(): lax.all_to_all(x, axes, split_axis=0, concat_axis=0, tiled=True, axis_ind...]
    all_to_all x1 -> x0, waiting for transfers between devices: 4 us -> none  [exchange(): lax.all_to_all(x, axes, split_axis=0, concat_axis=0, tiled=True, axis_ind...]
    ppermute x3 -> x9, waiting for transfers between devices: 16.1 us -> 19.8 us  [turn(): lax.ppermute(x, 'ctx', [(i, (i + 2 * step) % CTX) for i in range(CTX)])]
    ppermute x4 -> x3, starting transfers between devices: 6.77 us -> 3.77 us  [swap(): return lax.ppermute(x, axis, [(i, i ^ step) for i in range(count)])]
    pallas_call x5 -> x7, Pallas kernels: 4.64 us -> 6.23 us  [the longest x3 3.23 us: project(): pl.pallas_call(functools.partial(project_kernel, steps, wanted), out_shap...]
  transfers between devices with their start and end apart: 8 -> 12, of which waited for: 7 -> 5; matrix products, arithmetic and copies ran while one was open for 0% -> 0% of each run, Pallas kernels for 5% -> 5%
where the time goes in v3:
time: 255 us
  blocking collectives  167 us (65%)
  Pallas kernels  37.6 us (15%)
  waiting for transfers between devices  27.8 us (11%)
  starting transfers between devices  21.6 us (8%)
    all_to_all x2, blocking collectives, exchange(): return lax.all_to_all(x, ALL, split_axis=0, concat_axis=0, tiled=True)  167 us
    ppermute x9, waiting for transfers between devices, turn(): lax.ppermute(x, 'ctx', [(i, (i + 2 * step) % CTX) for i in range(CTX)])  19.8 us
    ppermute x9, starting transfers between devices, turn(): lax.ppermute(x, 'ctx', [(i, (i + 2 * step) % CTX) for i in range(CTX)])  17.8 us
    pallas_call x1, Pallas kernels, expert_apply(): pl.pallas_call(expert_kernel, out_shape=pltpu.VMEM((NE * 8, WIDE + NE), B...  16.4 us
    ppermute x3, waiting for transfers between devices, swap(): return lax.ppermute(x, axis, [(i, i ^ step) for i in range(count)])  7.95 us
    pallas_call x1, Pallas kernels, attend(): pl.pallas_call(attend_kernel, out_shape=pltpu.VMEM((4, TOK, GH * DH), BF)...  5.23 us
  transfers between devices with their start and end apart: 12, of which 5 were waited for; matrix products, arithmetic and copies ran while one was open for 0% of the time, Pallas kernels for 5%

profile of v3, /device:TPU:0, one launch (start us, length us, event | category | flops | bytes accessed | tf_op | source)
XLA Modules:
  0.0 254.6 jit_solution(7526677192382732719)
XLA Ops:
  0.7 0.1 pad_add_fusion.place_ref
  0.7 2.3 send_all.1
  3.1 3.2 %collective-permute-start.4 = (bf16[256,2048]{1,0:T(8,128)(2,1)S(1)}, bf16[256,2048]{1,0:T(8,128)(2,1)S(1)}, u32[]{:S(2)}, u32[]{:S(2)}) collective-permute-start(bf16[256,2048]{1,0:T(8,128)(2,1)S(1)} %get-tuple-element.31), channel_id=1, source_target_pairs={{0,1},{1,0},{2,3},{3,2},{4,5},{5,4},{6,7},{7,6},{8,9},{9,8},{10,11... | collective-permute-start | bytes 3145736 | tf_op jit(solution)/shard_map/ppermute | solution.py:455
  6.3 1.9 collective-permute-start
  8.2 3.6 %collective-permute-start.1 = (bf16[128,1280]{1,0:T(8,128)(2,1)S(1)}, bf16[128,1280]{1,0:T(8,128)(2,1)S(1)}, u32[]{:S(2)}, u32[]{:S(2)}) collective-permute-start(bf16[128,1280]{1,0:T(8,128)(2,1)S(1)} %get-tuple-element.29), channel_id=1, source_target_pairs={{0,4},{1,5},{2,6},{3,7},{4,0},{5,1},{6,2},{7,3},{8,12},{9,13},{10,... | collective-permute-start | bytes 983048 | tf_op jit(solution)/shard_map/ppermute | solution.py:459
  11.8 1.0 collective-permute-start.2
  12.8 5.2 %collective-permute-done.refs_1_.one_ref = bf16[128,1280]{1,0:T(8,128)(2,1)S(1)} collective-permute-done((bf16[128,1280]{1,0:T(8,128)(2,1)S(1)}, bf16[128,1280]{1,0:T(8,128)(2,1)S(1)}, u32[]{:S(2)}, u32[]{:S(2)}) %collective-permute-start) | collective-permute-done | bytes 327712 | tf_op jit(solution)/shard_map/ppermute | solution.py:459
  18.0 7.9 %collective-permute-done.1.refs_2_.two_ref = bf16[128,1280]{1,0:T(8,128)(2,1)S(1)} collective-permute-done((bf16[128,1280]{1,0:T(8,128)(2,1)S(1)}, bf16[128,1280]{1,0:T(8,128)(2,1)S(1)}, u32[]{:S(2)}, u32[]{:S(2)}) %collective-permute-start.1) | collective-permute-done | bytes 327712 | tf_op jit(solution)/shard_map/ppermute | solution.py:459
  25.9 0.6 own_keys.1.own_ref
  26.5 0.6 collective-permute-start.3
  27.1 7.9 %collective-permute-done.3.partner_ref.after_ref = bf16[4,128,256]{2,1,0:T(8,128)(2,1)S(1)} collective-permute-done((bf16[4,128,256]{2,1,0:T(8,128)(2,1)S(1)}, bf16[4,128,256]{2,1,0:T(8,128)(2,1)S(1)}, u32[]{:S(2)}, u32[]{:S(2)}) %collective-permute-start.3) | collective-permute-done | bytes 262176 | tf_op jit(solution)/shard_map/ppermute | solution.py:455
  35.1 5.2 %attend.1.heads_ref = bf16[4,128,1024]{2,1,0:T(8,128)(2,1)S(1)} custom-call(s32[3]{0:T(128)S(1)} %pad_add_fusion.place_ref, bf16[128,1280]{1,0:T(8,128)(2,1)S(1)} %get-tuple-element.27.refs_0_.zero_ref, bf16[128,1280]{1,0:T(8,128)(2,1)S(1)} %collective-permute-done.refs_1_.one_ref, bf16[128,1280]{1,0:T(8,128)(2,1)S(1)} %collective-permute-done.1.refs_2_.two_ref, ...), custom_call_target="tpu_custom_call" | custom-call | flops 1342177280 | bytes 3145728 | tf_op jit(solution)/shard_map/attend/pallas_call | solution.py:217
  40.3 1.3 project_mine.1.mine_ref
  41.6 1.0 project.5
  42.6 2.2 collective-permute-start.6
  44.8 2.2 collective-permute-start.7
  47.0 1.3 project.4
  48.3 0.1 collective-permute-start.9
  48.4 3.2 %collective-permute-start.10 = (bf16[128,1024]{1,0:T(8,128)(2,1)S(1)}, bf16[128,1024]{1,0:T(8,128)(2,1)S(1)}, u32[]{:S(2)}, u32[]{:S(2)}) collective-permute-start(bf16[128,1024]{1,0:T(8,128)(2,1)S(1)} %get-tuple-element.38), channel_id=1, source_target_pairs={{0,6},{1,7},{2,0},{3,1},{4,2},{5,3},{6,4},{7,5},{8,14},{9,15},{10,... | collective-permute-start | bytes 786440 | tf_op jit(solution)/shard_map/ppermute | solution.py:459
  51.6 2.5 collective-permute-done.6.b_ref
  54.1 0.1 join.1
  54.1 1.9 collective-permute-start.8
  56.0 1.7 collective-permute-start.11
  57.7 2.2 route_plan.1
  59.9 1.0 project.3.own_ref
  60.9 4.2 %collective-permute-done.8.up_left_ref = bf16[128,1024]{1,0:T(8,128)(2,1)S(1)} collective-permute-done((bf16[128,1024]{1,0:T(8,128)(2,1)S(1)}, bf16[128,1024]{1,0:T(8,128)(2,1)S(1)}, u32[]{:S(2)}, u32[]{:S(2)}) %collective-permute-start.8) | collective-permute-done | bytes 262176 | tf_op jit(solution)/shard_map/ppermute | solution.py:459
  65.1 3.2 %residual_norm_pick.1 = (bf16[128,2048]{1,0:T(8,128)(2,1)}, bf16[1024,3072]{1,0:T(8,128)(2,1)S(1)}) custom-call(f32[128,2048]{1,0:T(8,128)S(1)} %project.3.own_ref, bf16[128,1024]{1,0:T(8,128)(2,1)S(1)} %collective-permute-done.8.up_left_ref, bf16[128,1024]{1,0:T(8,128)(2,1)S(1)} %collective-permute-done.9.up_right_ref, ...), custom_call_target="tpu_custom_call" | custom-call | flops 1073741824 | bytes 10485760 | tf_op jit(solution)/shard_map/residual_norm_pick/pallas_call | solution.py:342
  68.3 0.0 copy-start.5
  68.4 84.2 %all_to_all.10 = bf16[128,8,3072]{2,1,0:T(8,128)(2,1)S(1)} all-to-all(bf16[128,8,3072]{2,1,0:T(8,128)(2,1)S(1)} %bitcast.15), channel_id=1, replica_groups=mesh['dp'=16,'ctx'=8] {'dp','ctx'}, dimensions={0} | all-to-all | bytes 12582912 | tf_op jit(solution)/shard_map/all_to_all | solution.py:463
  152.6 16.4 %experts.1 = bf16[1024,3200]{1,0:T(8,128)(2,1)S(1)} custom-call(bf16[1024,3072]{1,0:T(8,128)(2,1)S(1)} %bitcast.16, bf16[1,2048,768]{2,1,0:T(8,128)(2,1)S(1)} %copy-done.5, bf16[1,2048,768]{2,1,0:T(8,128)(2,1)S(1)} %copy-done.6, bf16[1,768,2048]{2,1,0:T(8,128)(2,1)S(1)} %copy-done.7, f32[8,128]{1,0:T(8,128)S(1)} %copy-done.9), custom_call_target="tpu_custom_call" | custom-call | flops 14495514624 | bytes 23068672 | tf_op jit(solution)/shard_map/experts/pallas_call | solution.py:406
  169.0 82.4 %all_to_all.11 = bf16[128,8,3200]{2,1,0:T(8,128)(2,1)S(1)} all-to-all(bf16[128,8,3200]{2,1,0:T(8,128)(2,1)S(1)} %bitcast.14), channel_id=1, replica_groups=mesh['dp'=16,'ctx'=8] {'dp','ctx'}, dimensions={0} | all-to-all | bytes 13107200 | tf_op jit(solution)/shard_map/all_to_all | solution.py:463
  251.5 3.1 %mix.1 = (bf16[128,2048]{1,0:T(8,128)(2,1)}, f32[1,128]{1,0:T(1,128)}, f32[1,128]{1,0:T(1,128)}) custom-call(bf16[256,1024]{1,0:T(8,128)(2,1)S(1)} %copy-done.2, bf16[512,1024]{1,0:T(8,128)(2,1)S(1)} %copy-done.1, bf16[1024,3200]{1,0:T(8,128)(2,1)S(1)} %bitcast.13), custom_call_target="tpu_custom_call" | custom-call | flops 2147483648 | bytes 8388608 | tf_op jit(solution)/shard_map/mix/pallas_call | solution.py:439
  (28 shorter events, 0.1 us)
Async XLA Ops:
  3.1 32.0 %collective-permute-start.4 = (bf16[256,2048]{1,0:T(8,128)(2,1)S(1)}, bf16[256,2048]{1,0:T(8,128)(2,1)S(1)}, u32[]{:S(2)}, u32[]{:S(2)}) collective-permute-start(bf16[256,2048]{1,0:T(8,128)(2,1)S(1)} %get-tuple-element.31), channel_id=1, source_target_pairs={{0,1},{1,0},{2,3},{3,2},{4,5},{5,4},{6,7},{7,6},{8,9},{9,8},{10,11... | collective-permute-start | bytes 3145736 | tf_op jit(solution)/shard_map/ppermute | solution.py:455
  6.3 11.7 %collective-permute-start = (bf16[128,1280]{1,0:T(8,128)(2,1)S(1)}, bf16[128,1280]{1,0:T(8,128)(2,1)S(1)}, u32[]{:S(2)}, u32[]{:S(2)}) collective-permute-start(bf16[128,1280]{1,0:T(8,128)(2,1)S(1)} %get-tuple-element.28), channel_id=1, source_target_pairs={{0,2},{1,3},{2,4},{3,5},{4,6},{5,7},{6,0},{7,1},{8,10},{9,11},{10,... | collective-permute-start | bytes 983048 | tf_op jit(solution)/shard_map/ppermute | solution.py:459
  8.2 17.7 %collective-permute-start.1 = (bf16[128,1280]{1,0:T(8,128)(2,1)S(1)}, bf16[128,1280]{1,0:T(8,128)(2,1)S(1)}, u32[]{:S(2)}, u32[]{:S(2)}) collective-permute-start(bf16[128,1280]{1,0:T(8,128)(2,1)S(1)} %get-tuple-element.29), channel_id=1, source_target_pairs={{0,4},{1,5},{2,6},{3,7},{4,0},{5,1},{6,2},{7,3},{8,12},{9,13},{10,... | collective-permute-start | bytes 983048 | tf_op jit(solution)/shard_map/ppermute | solution.py:459
  11.8 14.2 %collective-permute-start.2 = (bf16[128,1280]{1,0:T(8,128)(2,1)S(1)}, bf16[128,1280]{1,0:T(8,128)(2,1)S(1)}, u32[]{:S(2)}, u32[]{:S(2)}) collective-permute-start(bf16[128,1280]{1,0:T(8,128)(2,1)S(1)} %get-tuple-element.30), channel_id=1, source_target_pairs={{0,6},{1,7},{2,0},{3,1},{4,2},{5,3},{6,4},{7,5},{8,14},{9,15},{10,... | collective-permute-start | bytes 983048 | tf_op jit(solution)/shard_map/ppermute | solution.py:459
  25.9 14.3 %copy-start = (bf16[512,2048]{1,0:T(8,128)(2,1)S(1)}, bf16[512,2048]{1,0:T(8,128)(2,1)}, u32[]{:S(2)}) copy-start(bf16[512,2048]{1,0:T(8,128)(2,1)} %mine_ref.1) | copy-start | bytes 6291460
  26.5 8.5 %collective-permute-start.3 = (bf16[4,128,256]{2,1,0:T(8,128)(2,1)S(1)}, bf16[4,128,256]{2,1,0:T(8,128)(2,1)S(1)}, u32[]{:S(2)}, u32[]{:S(2)}) collective-permute-start(bf16[4,128,256]{2,1,0:T(8,128)(2,1)S(1)} %own_keys.1.own_ref), channel_id=1, source_target_pairs={{0,1},{1,0},{2,3},{3,2},{4,5},{5,4},{6,7},{7,6},{8,9},{9,8},{10,11... | collective-permute-start | bytes 786440 | tf_op jit(solution)/shard_map/ppermute | solution.py:455
  35.1 6.5 %collective-permute-start.5 = (bf16[256,2048]{1,0:T(8,128)(2,1)S(1)}, bf16[256,2048]{1,0:T(8,128)(2,1)S(1)}, u32[]{:S(2)}, u32[]{:S(2)}) collective-permute-start(bf16[256,2048]{1,0:T(8,128)(2,1)S(1)} %later.1.near_ref), channel_id=1, source_target_pairs={{0,8},{8,0},{16,24},{24,16},{32,40},{40,32},{48,56},{56,48},{64,72... | collective-permute-start | bytes 3145736 | tf_op jit(solution)/shard_map/ppermute | solution.py:455
  42.6 11.5 %collective-permute-start.6 = (bf16[128,1024]{1,0:T(8,128)(2,1)S(1)}, bf16[128,1024]{1,0:T(8,128)(2,1)S(1)}, u32[]{:S(2)}, u32[]{:S(2)}) collective-permute-start(bf16[128,1024]{1,0:T(8,128)(2,1)S(1)} %get-tuple-element.33), channel_id=1, source_target_pairs={{0,2},{1,3},{2,4},{3,5},{4,6},{5,7},{6,0},{7,1},{8,10},{9,11},{10,... | collective-permute-start | bytes 786440 | tf_op jit(solution)/shard_map/ppermute | solution.py:459
  44.8 13.0 %copy-start.3 = (s32[128,8]{0,1:T(8,128)S(1)}, s32[128,8]{0,1:T(8,128)}, u32[]{:S(2)}) copy-start(s32[128,8]{0,1:T(8,128)} %param.17) | copy-start | bytes 12292
  44.8 13.0 %copy-start.4 = (f32[128,8]{0,1:T(8,128)S(1)}, f32[128,8]{0,1:T(8,128)}, u32[]{:S(2)}) copy-start(f32[128,8]{0,1:T(8,128)} %param.18) | copy-start | bytes 12292
  44.8 9.3 %collective-permute-start.7 = (bf16[128,1024]{1,0:T(8,128)(2,1)S(1)}, bf16[128,1024]{1,0:T(8,128)(2,1)S(1)}, u32[]{:S(2)}, u32[]{:S(2)}) collective-permute-start(bf16[128,1024]{1,0:T(8,128)(2,1)S(1)} %get-tuple-element.35), channel_id=1, source_target_pairs={{0,6},{1,7},{2,0},{3,1},{4,2},{5,3},{6,4},{7,5},{8,14},{9,15},{10,... | collective-permute-start | bytes 786440 | tf_op jit(solution)/shard_map/ppermute | solution.py:459
  48.3 12.6 %collective-permute-start.9 = (bf16[128,1024]{1,0:T(8,128)(2,1)S(1)}, bf16[128,1024]{1,0:T(8,128)(2,1)S(1)}, u32[]{:S(2)}, u32[]{:S(2)}) collective-permute-start(bf16[128,1024]{1,0:T(8,128)(2,1)S(1)} %get-tuple-element.37), channel_id=1, source_target_pairs={{0,2},{1,3},{2,4},{3,5},{4,6},{5,7},{6,0},{7,1},{8,10},{9,11},{10,... | collective-permute-start | bytes 786440 | tf_op jit(solution)/shard_map/ppermute | solution.py:459
  48.4 12.6 %collective-permute-start.10 = (bf16[128,1024]{1,0:T(8,128)(2,1)S(1)}, bf16[128,1024]{1,0:T(8,128)(2,1)S(1)}, u32[]{:S(2)}, u32[]{:S(2)}) collective-permute-start(bf16[128,1024]{1,0:T(8,128)(2,1)S(1)} %get-tuple-element.38), channel_id=1, source_target_pairs={{0,6},{1,7},{2,0},{3,1},{4,2},{5,3},{6,4},{7,5},{8,14},{9,15},{10,... | collective-permute-start | bytes 786440 | tf_op jit(solution)/shard_map/ppermute | solution.py:459
  54.1 11.0 %collective-permute-start.8 = (bf16[128,1024]{1,0:T(8,128)(2,1)S(1)}, bf16[128,1024]{1,0:T(8,128)(2,1)S(1)}, u32[]{:S(2)}, u32[]{:S(2)}) collective-permute-start(bf16[128,1024]{1,0:T(8,128)(2,1)S(1)} %get-tuple-element.36), channel_id=1, source_target_pairs={{0,2},{1,3},{2,4},{3,5},{4,6},{5,7},{6,0},{7,1},{8,10},{9,11},{10,... | collective-permute-start | bytes 786440 | tf_op jit(solution)/shard_map/ppermute | solution.py:459
  56.0 9.1 %collective-permute-start.11 = (bf16[128,1024]{1,0:T(8,128)(2,1)S(1)}, bf16[128,1024]{1,0:T(8,128)(2,1)S(1)}, u32[]{:S(2)}, u32[]{:S(2)}) collective-permute-start(bf16[128,1024]{1,0:T(8,128)(2,1)S(1)} %get-tuple-element.39), channel_id=1, source_target_pairs={{0,6},{1,7},{2,0},{3,1},{4,2},{5,3},{6,4},{7,5},{8,14},{9,15},{10,... | collective-permute-start | bytes 786440 | tf_op jit(solution)/shard_map/ppermute | solution.py:459
  59.9 5.2 %copy-start.8 = (f32[2048]{0:T(1024)S(1)}, f32[2048]{0:T(1024)}, u32[]{:S(2)}) copy-start(f32[2048]{0:T(1024)} %param.16) | copy-start | bytes 24580
  68.3 84.3 %copy-start.5 = (bf16[1,2048,768]{2,1,0:T(8,128)(2,1)S(1)}, bf16[1,2048,768]{2,1,0:T(8,128)(2,1)}, u32[]{:S(2)}) copy-start(bf16[1,2048,768]{2,1,0:T(8,128)(2,1)} %gate_ref.1) | copy-start | bytes 9437188
  68.3 84.3 %copy-start.6 = (bf16[1,2048,768]{2,1,0:T(8,128)(2,1)S(1)}, bf16[1,2048,768]{2,1,0:T(8,128)(2,1)}, u32[]{:S(2)}) copy-start(bf16[1,2048,768]{2,1,0:T(8,128)(2,1)} %up_ref.1) | copy-start | bytes 9437188
  68.3 84.3 %copy-start.7 = (bf16[1,768,2048]{2,1,0:T(8,128)(2,1)S(1)}, bf16[1,768,2048]{2,1,0:T(8,128)(2,1)}, u32[]{:S(2)}) copy-start(bf16[1,768,2048]{2,1,0:T(8,128)(2,1)} %down_ref.1) | copy-start | bytes 9437188
  68.4 84.3 %copy-start.9 = (f32[8,128]{1,0:T(8,128)S(1)}, f32[8,128]{1,0:T(8,128)}, u32[]{:S(2)}) copy-start(f32[8,128]{1,0:T(8,128)} %get-tuple-element.46.stat_ref) | copy-start | bytes 12292
  169.0 82.4 %copy-start.1 = (bf16[512,1024]{1,0:T(8,128)(2,1)S(1)}, bf16[512,1024]{1,0:T(8,128)(2,1)}, u32[]{:S(2)}) copy-start(bf16[512,1024]{1,0:T(8,128)(2,1)} %get-tuple-element.44.mix2_ref) | copy-start | bytes 3145732
  169.0 82.4 %copy-start.2 = (bf16[256,1024]{1,0:T(8,128)(2,1)S(1)}, bf16[256,1024]{1,0:T(8,128)(2,1)}, u32[]{:S(2)}) copy-start(bf16[256,1024]{1,0:T(8,128)(2,1)} %get-tuple-element.43.mix1_ref) | copy-start | bytes 1572868

commit v4 on v3

--- a/solution.py
+++ b/solution.py
@@ -18,11 +18,10 @@
 NE = 128
 CTX = 8
 GH = H // KV
-SENT = GH * DH + 2 * DH
 HALF = 512
 WHOLE = 8
 CAP = 12
-QUARTER = 256
+PIECE = 128
 WIDE = 3072
 ALL = ("dp", "ctx")
 BF = jnp.bfloat16
@@ -106,53 +105,58 @@
     )(routes.T, gates.T)
 
 
-def send_kernel(place_ref, q_ref, keys_ref, values_ref, weight_ref, *refs):
-    out_refs, weight_out, sems = refs[:4], refs[4], refs[5]
-    wide = GH * DH
-    copies = []
-
-    def fetch(source, target):
-        copies.append(pltpu.make_async_copy(source, target, sems.at[len(copies)]))
-        copies[-1].start()
-
-    for step, out_ref in enumerate(out_refs):
-        group = (place_ref[1] + step) % 4
-        cols = pl.ds(pl.multiple_of(group * DH, DH), DH)
-        fetch(q_ref.at[:, pl.ds(pl.multiple_of(group * wide, wide), wide)], out_ref.at[:, :wide])
-        fetch(keys_ref.at[:, cols], out_ref.at[:, wide : wide + DH])
-        fetch(values_ref.at[:, cols], out_ref.at[:, wide + DH :])
-    rows = pl.ds(pl.multiple_of(place_ref[0] * QUARTER, QUARTER), QUARTER)
-    fetch(weight_ref.at[rows], weight_out)
+def fetch_all(pairs, sems):
+    copies = [pltpu.make_async_copy(a, b, sems.at[i]) for i, (a, b) in enumerate(pairs)]
+    for copy in copies:
+        copy.start()
     for copy in copies:
         copy.wait()
 
 
-def send_all(place, queries, keys, values, weight):
+def group_cols(place_ref, step, size):
+    group = (place_ref[1] + step) % 4
+    return pl.ds(pl.multiple_of(group * size, size), size)
+
+
+def send_kernel(place_ref, keys_ref, values_ref, q_ref, weight_ref, *refs):
+    rows = pl.ds(pl.multiple_of((2 * place_ref[0] + place_ref[3]) * PIECE, PIECE), PIECE)
+    pairs = [(weight_ref.at[rows], refs[8])]
+    for step in range(4):
+        cols = group_cols(place_ref, step, DH)
+        pairs.append((keys_ref.at[:, cols], refs[step].at[:, :DH]))
+        pairs.append((values_ref.at[:, cols], refs[step].at[:, DH:]))
+        pairs.append((q_ref.at[:, group_cols(place_ref, step, GH * DH)], refs[4 + step]))
+    fetch_all(pairs, refs[9])
+
+
+def send_all(place, *arrays):
     return pl.pallas_call(
         send_kernel,
-        out_shape=[pltpu.VMEM((TOK, SENT), BF)] * 4 + [pltpu.VMEM((QUARTER, D), BF)],
+        out_shape=[pltpu.VMEM((TOK, 2 * DH), BF)] * 4
+        + [pltpu.VMEM((TOK, GH * DH), BF)] * 4
+        + [pltpu.VMEM((PIECE, D), BF)],
         in_specs=[SM] + [ANY] * 4,
-        out_specs=[VM] * 5,
+        out_specs=[VM] * 9,
         scratch_shapes=[pltpu.SemaphoreType.DMA((13,))],
         compiler_params=params(4),
         name="send_all",
-    )(place, *(far_memory(x) for x in (queries, keys, values, weight)))
+    )(place, *(far_memory(x) for x in arrays))
 
 
 def own_keys_kernel(place_ref, *refs):
     for step in range(4):
-        refs[4][(place_ref[1] + 4 - step) % 4] = refs[step][:, GH * DH :]
-
-
-def own_keys(place, blocks):
+        refs[5][(place_ref[1] + 4 - step) % 4] = refs[step][...]
+
+
+def own_keys(place, blocks, after):
     return pl.pallas_call(
         own_keys_kernel,
         out_shape=pltpu.VMEM((4, TOK, 2 * DH), BF),
-        in_specs=[SM] + [VM] * 4,
+        in_specs=[SM] + [VM] * 4 + [ANY],
         out_specs=VM,
         compiler_params=params(4),
         name="own_keys",
-    )(place, *(near_core(x) for x in blocks))
+    )(place, *(near_core(x) for x in blocks), after)
 
 
 def later_kernel(x_ref, after_ref, out_ref):
@@ -171,46 +175,56 @@
     )(x, after)
 
 
+SCALE = math.log2(math.e) / math.sqrt(DH)
+
+
+def scores_of(q, keys):
+    return lax.dot_general(q, keys, (((1,), (1,)), ((), ())), preferred_element_type=F32)
+
+
+def with_ones(values):
+    return jnp.concatenate([values, jnp.ones(values.shape, BF)], axis=1)
+
+
 def attend_kernel(place_ref, zero_ref, one_ref, two_ref, three_ref, own_ref, partner_ref, out_ref, q_ref):
-    half = place_ref[2]
-    first = pl.ds(pl.multiple_of(half * HALF, HALF), HALF)
-    second = pl.ds(pl.multiple_of((1 - half) * HALF, HALF), HALF)
+    core, half, turned = place_ref[0], place_ref[2], place_ref[3]
+    firsts = [half * HALF + i * DH for i in range(GH // 2)]
+    for c in (core, 1 - core):
+        for y in (turned, 1 - turned):
+            firsts.append((1 - half) * HALF + (2 * c + y) * DH)
     for step, ref in enumerate((zero_ref, one_ref, two_ref, three_ref)):
         at = (place_ref[1] + 4 - step) % 4
-        q_ref[at, :, :HALF] = ref[:, first]
-        q_ref[at, :, HALF:] = ref[:, second]
-    ones = jnp.ones((4 * TOK, DH), BF)
+        for head, first in enumerate(firsts):
+            q_ref[at, head * TOK : (head + 1) * TOK, :] = ref[:, pl.ds(pl.multiple_of(first, DH), DH)]
     sides = [ref[...].reshape(4 * TOK, 2 * DH) for ref in (own_ref, partner_ref)]
     keys = [side[:, :DH] for side in sides]
-    values = [jnp.concatenate([side[:, DH:], ones], axis=1) for side in sides]
-    scale = math.log2(math.e) / math.sqrt(DH)
-    below = lax.broadcasted_iota(jnp.int32, (TOK, TOK), 1) <= lax.broadcasted_iota(
-        jnp.int32, (TOK, TOK), 0
-    )
+    values = [with_ones(side[:, DH:]) for side in sides]
+    heads = 4
+    rows = heads * TOK
+    own_row = lax.broadcasted_iota(jnp.int32, (rows, TOK), 0) & (TOK - 1)
+    below = lax.broadcasted_iota(jnp.int32, (rows, TOK), 1) <= own_row
+    shown = jnp.full((rows, TOK), half, jnp.int32) == 1
     for block in range(4):
         upto = (block + 1) * TOK
-        for head in range(GH):
-            q = q_ref[block, :, head * DH : (head + 1) * DH]
-            scores = []
-            for side in range(2):
-                score = lax.dot_general(
-                    q, keys[side][:upto], (((1,), (1,)), ((), ())), preferred_element_type=F32
-                )
-                seen = below if side == 0 else jnp.full((TOK, TOK), half, jnp.int32) == 1
-                last = jnp.where(seen, score[:, upto - TOK :], -jnp.inf)
+        before = upto - TOK
+        key = jnp.concatenate([k[:upto] for k in keys], axis=0)
+        value = jnp.concatenate([v[:upto] for v in values], axis=0)
+        for head in range(0, GH, heads):
+            q = q_ref[block, head * TOK : (head + heads) * TOK, :]
+            score = scores_of(q, key)
+            parts = []
+            for side, seen in enumerate((below, shown)):
                 if block:
-                    last = jnp.concatenate([score[:, : upto - TOK], last], axis=1)
-                scores.append(last)
-            top = jnp.maximum(
-                jnp.max(scores[0], axis=1, keepdims=True), jnp.max(scores[1], axis=1, keepdims=True)
-            )
-            result = 0.0
-            for side in range(2):
-                expo = jnp.exp2((scores[side] - top) * scale).astype(BF)
-                result = result + dot(expo, values[side][:upto])
-            out_ref[block, :, head * DH : (head + 1) * DH] = (
-                result[:, :DH] / result[:, DH:]
-            ).astype(BF)
+                    parts.append(score[:, side * upto : side * upto + before])
+                last = score[:, side * upto + before : (side + 1) * upto]
+                parts.append(jnp.where(seen, last, -jnp.inf))
+            score = jnp.concatenate(parts, axis=1)
+            top = jnp.max(score, axis=1, keepdims=True)
+            result = dot(jnp.exp2((score - top) * SCALE).astype(BF), value)
+            result = (result[:, :DH] / result[:, DH:]).astype(BF)
+            for i in range(heads):
+                cols = slice((head + i) * DH, (head + i + 1) * DH)
+                out_ref[block, :, cols] = result[i * TOK : (i + 1) * TOK]
 
 
 def attend(place, blocks, own, partner):
@@ -219,10 +233,10 @@
         out_shape=pltpu.VMEM((4, TOK, GH * DH), BF),
         in_specs=[SM] + [VM] * 6,
         out_specs=VM,
-        scratch_shapes=[pltpu.VMEM((4, TOK, GH * DH), BF)],
+        scratch_shapes=[pltpu.VMEM((4, GH * TOK, DH), BF)],
         compiler_params=params(16),
         cost_estimate=pl.CostEstimate(
-            flops=2 * 2 * 512 * 8 * 640 * 128, bytes_accessed=3 << 20, transcendentals=512 * 8 * 640
+            flops=5 << 30, bytes_accessed=8 << 20, transcendentals=512 * 8 * 640
         ),
         name="attend",
     )(place, *(near_core(x) for x in (*blocks, own, partner)))
@@ -250,38 +264,33 @@
     )(near_core(heads), near_core(mine))
 
 
-def project_kernel(steps, wanted, place_ref, heads_ref, mine_ref, near_ref, far_ref, *out_refs):
-    core = place_ref[0]
+def project_kernel(steps, wanted, place_ref, heads_ref, mine_ref, *refs):
+    others, out_refs = refs[:4], refs[4:]
     blocks = [(place_ref[1] + step) % 4 for step in steps]
-    near = pl.multiple_of(HALF + core * QUARTER, QUARTER)
-    far = pl.multiple_of(HALF + (1 - core) * QUARTER, QUARTER)
-
-    def heads(first):
-        rows = [heads_ref[block, :, pl.ds(first, QUARTER)] for block in blocks]
-        return rows[0] if len(rows) == 1 else jnp.concatenate(rows, axis=0)
-
-    second, third = heads(near), heads(far)
+    rows = [heads_ref[block, :, HALF:] for block in blocks]
+    heads = rows[0] if len(rows) == 1 else jnp.concatenate(rows, axis=0)
     cols = 512
     for j in range(0, D, cols):
-        total = dot(second, near_ref[:, j : j + cols]) + dot(third, far_ref[:, j : j + cols])
+        other = jnp.concatenate([ref[:, j : j + cols] for ref in others], axis=0)
+        total = dot(heads, other)
         for (i, low, high, kind), out_ref in zip(wanted, out_refs):
             if low <= j < high:
                 out = total[i * TOK : (i + 1) * TOK] + mine_ref[blocks[i], :, j : j + cols]
                 out_ref[:, j - low : j - low + cols] = out.astype(kind)
 
 
-def project(steps, wanted, place, heads, mine, near, far):
+def project(steps, wanted, place, *arrays):
     return pl.pallas_call(
         functools.partial(project_kernel, steps, wanted),
         out_shape=[pltpu.VMEM((TOK, high - low), kind) for _, low, high, kind in wanted],
-        in_specs=[SM] + [VM] * 4,
+        in_specs=[SM] + [VM] * 6,
         out_specs=[VM] * len(wanted),
-        compiler_params=params(8),
+        compiler_params=params(12),
         cost_estimate=pl.CostEstimate(
-            flops=2 * len(steps) * TOK * HALF * D, bytes_accessed=8 << 20, transcendentals=0
+            flops=2 * len(steps) * TOK * 2 * HALF * D, bytes_accessed=8 << 20, transcendentals=0
         ),
         name="project",
-    )(place, near_core(heads), near_core(mine), near_core(near), near_core(far))
+    )(place, *(near_core(x) for x in arrays))
 
 
 def join_kernel(a_ref, b_ref, c_ref, d_ref, left_ref, right_ref):
@@ -300,9 +309,8 @@
     )(*(near_core(x) for x in parts))
 
 
-def sum_over_z(place, heads, mine, near, far):
+def sum_over_z(*operands):
     half = D // 2
-    operands = (place, heads, mine, near, far)
     left, right = project((2,), ((0, 0, half, BF), (0, half, D, BF)), *operands)
     left, right = turn(left, 1), turn(right, 3)
     wanted = ((0, half, D, BF), (1, 0, half, BF), (0, 0, half, F32), (1, half, D, F32))
@@ -459,6 +467,10 @@
     return lax.ppermute(x, "ctx", [(i, (i + 2 * step) % CTX) for i in range(CTX)])
 
 
+def turn_all(blocks):
+    return [blocks[0]] + [turn(blocks[step], step) for step in (1, 2, 3)]
+
+
 def exchange(x):
     return lax.all_to_all(x, ALL, split_axis=0, concat_axis=0, tiled=True)
 
@@ -467,19 +479,21 @@
     hidden_in, queries, keys, values, out_weight, norm_gain, routes, gates, w_gate, w_up, w_down
 ):
     spot = lax.axis_index("ctx").astype(jnp.int32)
-    core = lax.axis_index("dp").astype(jnp.int32) % 2
-    place = jnp.stack([core, spot // 2, spot % 2])
-    *blocks, weight = send_all(place, queries, keys, values, out_weight)
-    near = swap(weight, "ctx", CTX, 1)
-    blocks = [blocks[0]] + [turn(blocks[step], step) for step in (1, 2, 3)]
-    own = own_keys(place, blocks)
+    column = lax.axis_index("dp").astype(jnp.int32)
+    place = jnp.stack([column % 2, spot // 2, spot % 2, column // 2 % 2])
+    *sent, weight = send_all(place, keys, values, queries, out_weight)
+    first = lax.ppermute(weight, ALL, [(i, i ^ 65) for i in range(NE)])
+    sent, blocks = turn_all(sent[:4]), turn_all(sent[4:])
+    own = own_keys(place, sent, blocks[2])
     partner = swap(own, "ctx", CTX, 1)
-    near = later(near, partner)
-    far = swap(near, "dp", 16, 1)
+    first = later(first, own)
+    second = swap(first, "dp", 16, 2)
+    first, second = later(first, partner), later(second, partner)
+    third, fourth = swap(first, "dp", 16, 1), swap(second, "dp", 16, 1)
     pick1, pick2, mix1, mix2, stat = route_plan(routes, gates)
     heads = attend(place, blocks, own, partner)
     mine = project_mine(heads, out_weight)
-    sums = sum_over_z(place, heads, mine, near, far)
+    sums = sum_over_z(place, heads, mine, first, second, third, fourth)
     attended, x = residual(sums, hidden_in, norm_gain, pick1, pick2)
     x = exchange(x.reshape(NE, 8, WIDE))
     y = expert_apply(x.reshape(NE * 8, WIDE), w_gate, w_up, w_down, stat)

time: 255 us -> 250 us (0.980)
  waiting for transfers between devices: 27.8 us -> 19.1 us
  starting transfers between devices: 21.6 us -> 27.7 us
    ppermute x9 -> x12, waiting for transfers between devices: 19.8 us -> 12 us  [turn(): lax.ppermute(x, 'ctx', [(i, (i + 2 * step) % CTX) for i in range(CTX)])]
    ppermute x9 -> x12, starting transfers between devices: 17.8 us -> 21.8 us  [turn(): lax.ppermute(x, 'ctx', [(i, (i + 2 * step) % CTX) for i in range(CTX)])]
    ppermute x0 -> x1, starting transfers between devices: none -> 2.92 us  [on_device(): first = lax.ppermute(weight, ALL, [(i, i ^ 65) for i in range(NE)])]
    ppermute x3 -> x4, waiting for transfers between devices: 7.95 us -> 7.03 us  [swap(): return lax.ppermute(x, axis, [(i, i ^ step) for i in range(count)])]
  transfers between devices with their start and end apart: 12 -> 17, of which waited for: 5 -> 7; matrix products, arithmetic and copies ran while one was open for 0% -> 0% of each run, Pallas kernels for 5% -> 4%
where the time goes in v4:
time: 250 us; the launch traced here: 249 us
  blocking collectives  165 us (66%)
  Pallas kernels  37 us (15%)
  starting transfers between devices  27.7 us (11%)
  waiting for transfers between devices  19.1 us (8%)
    all_to_all x2, blocking collectives, exchange(): return lax.all_to_all(x, ALL, split_axis=0, concat_axis=0, tiled=True)  165 us
    ppermute x12, starting transfers between devices, turn(): lax.ppermute(x, 'ctx', [(i, (i + 2 * step) % CTX) for i in range(CTX)])  21.8 us
    pallas_call x1, Pallas kernels, expert_apply(): pl.pallas_call(expert_kernel, out_shape=pltpu.VMEM((NE * 8, WIDE + NE), B...  16.4 us
    ppermute x12, waiting for transfers between devices, turn(): lax.ppermute(x, 'ctx', [(i, (i + 2 * step) % CTX) for i in range(CTX)])  12 us
    ppermute x4, waiting for transfers between devices, swap(): return lax.ppermute(x, axis, [(i, i ^ step) for i in range(count)])  7.03 us
  transfers between devices with their start and end apart: 17, of which 7 were waited for; matrix products, arithmetic and copies ran while one was open for 0% of the time, Pallas kernels for 4%

profile of v4, /device:TPU:0, one launch (start us, length us, event | category | flops | bytes accessed | tf_op | source)
XLA Modules:
  0.0 249.5 jit_solution(584473305778058771)
XLA Ops:
  0.8 2.1 send_all.1
  2.9 2.9 %collective-permute-start.7 = (bf16[128,2048]{1,0:T(8,128)(2,1)S(1)}, bf16[128,2048]{1,0:T(8,128)(2,1)S(1)}, u32[]{:S(2)}, u32[]{:S(2)}) collective-permute-start(bf16[128,2048]{1,0:T(8,128)(2,1)S(1)} %get-tuple-element.39), channel_id=1, source_target_pairs={{0,65},{1,64},{2,67},{3,66},{4,69},{5,68},{6,71},{7,70},{8,73},{9,... | collective-permute-start | bytes 1572872 | tf_op jit(solution)/shard_map/ppermute | solution.py:485
  5.8 3.9 %collective-permute-start.1 = (bf16[128,1024]{1,0:T(8,128)(2,1)S(1)}, bf16[128,1024]{1,0:T(8,128)(2,1)S(1)}, u32[]{:S(2)}, u32[]{:S(2)}) collective-permute-start(bf16[128,1024]{1,0:T(8,128)(2,1)S(1)} %get-tuple-element.33), channel_id=1, source_target_pairs={{0,4},{1,5},{2,6},{3,7},{4,0},{5,1},{6,2},{7,3},{8,12},{9,13},{10,... | collective-permute-start | bytes 786440 | tf_op jit(solution)/shard_map/ppermute | solution.py:467
  9.7 1.0 collective-permute-start.3
  10.7 1.2 collective-permute-start.4
  11.9 1.5 collective-permute-start.5
  13.4 4.4 %collective-permute-done.3.refs_1_ = bf16[128,256]{1,0:T(8,128)(2,1)S(1)} collective-permute-done((bf16[128,256]{1,0:T(8,128)(2,1)S(1)}, bf16[128,256]{1,0:T(8,128)(2,1)S(1)}, u32[]{:S(2)}, u32[]{:S(2)}) %collective-permute-start.3) | collective-permute-done | bytes 65568 | tf_op jit(solution)/shard_map/ppermute | solution.py:467
  18.5 0.7 collective-permute-done.5.refs_3_
  19.9 1.7 collective-permute-start.8
  21.6 0.8 collective-permute-start.6
  22.4 0.9 collective-permute-start
  23.2 2.4 collective-permute-start.2
  25.6 4.2 %collective-permute-done.6.partner_ref.after_ref = bf16[4,128,256]{2,1,0:T(8,128)(2,1)S(1)} collective-permute-done((bf16[4,128,256]{2,1,0:T(8,128)(2,1)S(1)}, bf16[4,128,256]{2,1,0:T(8,128)(2,1)S(1)}, u32[]{:S(2)}, u32[]{:S(2)}) %collective-permute-start.6) | collective-permute-done | bytes 262176 | tf_op jit(solution)/shard_map/ppermute | solution.py:463
  29.8 2.8 %collective-permute-done.8.x_ref = bf16[128,2048]{1,0:T(8,128)(2,1)S(1)} collective-permute-done((bf16[128,2048]{1,0:T(8,128)(2,1)S(1)}, bf16[128,2048]{1,0:T(8,128)(2,1)S(1)}, u32[]{:S(2)}, u32[]{:S(2)}) %collective-permute-start.8) | collective-permute-done | bytes 524320 | tf_op jit(solution)/shard_map/ppermute | solution.py:463
  33.1 4.9 %attend.1.heads_ref = bf16[4,128,1024]{2,1,0:T(8,128)(2,1)S(1)} custom-call(s32[4]{0:T(128)S(1)} %pad_add_fusion.place_ref, bf16[128,1024]{1,0:T(8,128)(2,1)S(1)} %get-tuple-element.31.zero_ref, bf16[128,1024]{1,0:T(8,128)(2,1)S(1)} %collective-permute-done.one_ref, bf16[128,1024]{1,0:T(8,128)(2,1)S(1)} %collective-permute-done.1.refs_4_.two_ref, ...), custom_call_target="tpu_custom_call" | custom-call | flops 5368709120 | bytes 8388608 | tf_op jit(solution)/shard_map/attend/pallas_call | solution.py:231
  38.1 1.3 project_mine.1.mine_ref
  39.3 1.0 project.5
  40.3 1.7 collective-permute-start.11
  42.0 2.3 collective-permute-start.12
  44.3 1.3 project.4
  45.7 3.2 %collective-permute-start.15 = (bf16[128,1024]{1,0:T(8,128)(2,1)S(1)}, bf16[128,1024]{1,0:T(8,128)(2,1)S(1)}, u32[]{:S(2)}, u32[]{:S(2)}) collective-permute-start(bf16[128,1024]{1,0:T(8,128)(2,1)S(1)} %get-tuple-element.46), channel_id=1, source_target_pairs={{0,6},{1,7},{2,0},{3,1},{4,2},{5,3},{6,4},{7,5},{8,14},{9,15},{10,... | collective-permute-start | bytes 786440 | tf_op jit(solution)/shard_map/ppermute | solution.py:467
  48.9 2.4 collective-permute-done.11.b_ref
  51.4 1.5 collective-permute-start.13
  53.0 2.2 collective-permute-start.16
  55.2 2.1 route_plan.1
  57.3 1.0 project.3.own_ref
  58.3 3.7 %collective-permute-done.13.up_left_ref = bf16[128,1024]{1,0:T(8,128)(2,1)S(1)} collective-permute-done((bf16[128,1024]{1,0:T(8,128)(2,1)S(1)}, bf16[128,1024]{1,0:T(8,128)(2,1)S(1)}, u32[]{:S(2)}, u32[]{:S(2)}) %collective-permute-start.13) | collective-permute-done | bytes 262176 | tf_op jit(solution)/shard_map/ppermute | solution.py:467
  62.0 3.2 %residual_norm_pick.1 = (bf16[128,2048]{1,0:T(8,128)(2,1)}, bf16[1024,3072]{1,0:T(8,128)(2,1)S(1)}) custom-call(f32[128,2048]{1,0:T(8,128)S(1)} %project.3.own_ref, bf16[128,1024]{1,0:T(8,128)(2,1)S(1)} %collective-permute-done.13.up_left_ref, bf16[128,1024]{1,0:T(8,128)(2,1)S(1)} %collective-permute-done.14.up_right_ref, ...), custom_call_target="tpu_custom_call" | custom-call | flops 1073741824 | bytes 10485760 | tf_op jit(solution)/shard_map/residual_norm_pick/pallas_call | solution.py:350
  65.2 82.3 %all_to_all.10 = bf16[128,8,3072]{2,1,0:T(8,128)(2,1)S(1)} all-to-all(bf16[128,8,3072]{2,1,0:T(8,128)(2,1)S(1)} %bitcast.16), channel_id=1, replica_groups=mesh['dp'=16,'ctx'=8] {'dp','ctx'}, dimensions={0} | all-to-all | bytes 12582912 | tf_op jit(solution)/shard_map/all_to_all | solution.py:475
  147.5 16.4 %experts.1 = bf16[1024,3200]{1,0:T(8,128)(2,1)S(1)} custom-call(bf16[1024,3072]{1,0:T(8,128)(2,1)S(1)} %bitcast.17, bf16[1,2048,768]{2,1,0:T(8,128)(2,1)S(1)} %copy-done.5, bf16[1,2048,768]{2,1,0:T(8,128)(2,1)S(1)} %copy-done.6, bf16[1,768,2048]{2,1,0:T(8,128)(2,1)S(1)} %copy-done.7, f32[8,128]{1,0:T(8,128)S(1)} %copy-done.9), custom_call_target="tpu_custom_call" | custom-call | flops 14495514624 | bytes 23068672 | tf_op jit(solution)/shard_map/experts/pallas_call | solution.py:414
  163.9 82.4 %all_to_all.11 = bf16[128,8,3200]{2,1,0:T(8,128)(2,1)S(1)} all-to-all(bf16[128,8,3200]{2,1,0:T(8,128)(2,1)S(1)} %bitcast.15), channel_id=1, replica_groups=mesh['dp'=16,'ctx'=8] {'dp','ctx'}, dimensions={0} | all-to-all | bytes 13107200 | tf_op jit(solution)/shard_map/all_to_all | solution.py:475
  246.3 3.1 %mix.1 = (bf16[128,2048]{1,0:T(8,128)(2,1)}, f32[1,128]{1,0:T(1,128)}, f32[1,128]{1,0:T(1,128)}) custom-call(bf16[256,1024]{1,0:T(8,128)(2,1)S(1)} %copy-done.2, bf16[512,1024]{1,0:T(8,128)(2,1)S(1)} %copy-done.1, bf16[1024,3200]{1,0:T(8,128)(2,1)S(1)} %bitcast.14), custom_call_target="tpu_custom_call" | custom-call | flops 2147483648 | bytes 8388608 | tf_op jit(solution)/shard_map/mix/pallas_call | solution.py:447
  (40 shorter events, 2.1 us)
Async XLA Ops:
  2.9 17.0 %collective-permute-start.7 = (bf16[128,2048]{1,0:T(8,128)(2,1)S(1)}, bf16[128,2048]{1,0:T(8,128)(2,1)S(1)}, u32[]{:S(2)}, u32[]{:S(2)}) collective-permute-start(bf16[128,2048]{1,0:T(8,128)(2,1)S(1)} %get-tuple-element.39), channel_id=1, source_target_pairs={{0,65},{1,64},{2,67},{3,66},{4,69},{5,68},{6,71},{7,70},{8,73},{9,... | collective-permute-start | bytes 1572872 | tf_op jit(solution)/shard_map/ppermute | solution.py:485
  5.8 13.5 %collective-permute-start.1 = (bf16[128,1024]{1,0:T(8,128)(2,1)S(1)}, bf16[128,1024]{1,0:T(8,128)(2,1)S(1)}, u32[]{:S(2)}, u32[]{:S(2)}) collective-permute-start(bf16[128,1024]{1,0:T(8,128)(2,1)S(1)} %get-tuple-element.33), channel_id=1, source_target_pairs={{0,4},{1,5},{2,6},{3,7},{4,0},{5,1},{6,2},{7,3},{8,12},{9,13},{10,... | collective-permute-start | bytes 786440 | tf_op jit(solution)/shard_map/ppermute | solution.py:467
  9.7 8.1 %collective-permute-start.3 = (bf16[128,256]{1,0:T(8,128)(2,1)S(1)}, bf16[128,256]{1,0:T(8,128)(2,1)S(1)}, u32[]{:S(2)}, u32[]{:S(2)}) collective-permute-start(bf16[128,256]{1,0:T(8,128)(2,1)S(1)} %get-tuple-element.36), channel_id=1, source_target_pairs={{0,2},{1,3},{2,4},{3,5},{4,6},{5,7},{6,0},{7,1},{8,10},{9,11},{10,... | collective-permute-start | bytes 196616 | tf_op jit(solution)/shard_map/ppermute | solution.py:467
  10.7 7.8 %collective-permute-start.4 = (bf16[128,256]{1,0:T(8,128)(2,1)S(1)}, bf16[128,256]{1,0:T(8,128)(2,1)S(1)}, u32[]{:S(2)}, u32[]{:S(2)}) collective-permute-start(bf16[128,256]{1,0:T(8,128)(2,1)S(1)} %get-tuple-element.37), channel_id=1, source_target_pairs={{0,4},{1,5},{2,6},{3,7},{4,0},{5,1},{6,2},{7,3},{8,12},{9,13},{10,... | collective-permute-start | bytes 196616 | tf_op jit(solution)/shard_map/ppermute | solution.py:467
  11.9 7.4 %collective-permute-start.5 = (bf16[128,256]{1,0:T(8,128)(2,1)S(1)}, bf16[128,256]{1,0:T(8,128)(2,1)S(1)}, u32[]{:S(2)}, u32[]{:S(2)}) collective-permute-start(bf16[128,256]{1,0:T(8,128)(2,1)S(1)} %get-tuple-element.38), channel_id=1, source_target_pairs={{0,6},{1,7},{2,0},{3,1},{4,2},{5,3},{6,4},{7,5},{8,14},{9,15},{10,... | collective-permute-start | bytes 196616 | tf_op jit(solution)/shard_map/ppermute | solution.py:467
  19.9 12.7 %collective-permute-start.8 = (bf16[128,2048]{1,0:T(8,128)(2,1)S(1)}, bf16[128,2048]{1,0:T(8,128)(2,1)S(1)}, u32[]{:S(2)}, u32[]{:S(2)}) collective-permute-start(bf16[128,2048]{1,0:T(8,128)(2,1)S(1)} %later.3.x_ref), channel_id=1, source_target_pairs={{0,16},{8,24},{16,0},{24,8},{32,48},{40,56},{48,32},{56,40},{64,80... | collective-permute-start | bytes 1572872 | tf_op jit(solution)/shard_map/ppermute | solution.py:463
  21.6 8.2 %collective-permute-start.6 = (bf16[4,128,256]{2,1,0:T(8,128)(2,1)S(1)}, bf16[4,128,256]{2,1,0:T(8,128)(2,1)S(1)}, u32[]{:S(2)}, u32[]{:S(2)}) collective-permute-start(bf16[4,128,256]{2,1,0:T(8,128)(2,1)S(1)} %own_keys.1.own_ref.after_ref), channel_id=1, source_target_pairs={{0,1},{1,0},{2,3},{3,2},{4,5},{5,4},{6,7},{7,6},{8,9},{9,8},{10,11... | collective-permute-start | bytes 786440 | tf_op jit(solution)/shard_map/ppermute | solution.py:463
  22.4 10.8 %collective-permute-start = (bf16[128,1024]{1,0:T(8,128)(2,1)S(1)}, bf16[128,1024]{1,0:T(8,128)(2,1)S(1)}, u32[]{:S(2)}, u32[]{:S(2)}) collective-permute-start(bf16[128,1024]{1,0:T(8,128)(2,1)S(1)} %get-tuple-element.32), channel_id=1, source_target_pairs={{0,2},{1,3},{2,4},{3,5},{4,6},{5,7},{6,0},{7,1},{8,10},{9,11},{10,... | collective-permute-start | bytes 786440 | tf_op jit(solution)/shard_map/ppermute | solution.py:467
  23.2 9.9 %collective-permute-start.2 = (bf16[128,1024]{1,0:T(8,128)(2,1)S(1)}, bf16[128,1024]{1,0:T(8,128)(2,1)S(1)}, u32[]{:S(2)}, u32[]{:S(2)}) collective-permute-start(bf16[128,1024]{1,0:T(8,128)(2,1)S(1)} %get-tuple-element.34), channel_id=1, source_target_pairs={{0,6},{1,7},{2,0},{3,1},{4,2},{5,3},{6,4},{7,5},{8,14},{9,15},{10,... | collective-permute-start | bytes 786440 | tf_op jit(solution)/shard_map/ppermute | solution.py:467
  32.6 6.7 %collective-permute-start.10 = (bf16[128,2048]{1,0:T(8,128)(2,1)S(1)}, bf16[128,2048]{1,0:T(8,128)(2,1)S(1)}, u32[]{:S(2)}, u32[]{:S(2)}) collective-permute-start(bf16[128,2048]{1,0:T(8,128)(2,1)S(1)} %later.5.refs_1_), channel_id=1, source_target_pairs={{0,8},{8,0},{16,24},{24,16},{32,40},{40,32},{48,56},{56,48},{64,72... | collective-permute-start | bytes 1572872 | tf_op jit(solution)/shard_map/ppermute | solution.py:463
  32.6 6.7 %collective-permute-start.9 = (bf16[128,2048]{1,0:T(8,128)(2,1)S(1)}, bf16[128,2048]{1,0:T(8,128)(2,1)S(1)}, u32[]{:S(2)}, u32[]{:S(2)}) collective-permute-start(bf16[128,2048]{1,0:T(8,128)(2,1)S(1)} %later.4.refs_0_), channel_id=1, source_target_pairs={{0,8},{8,0},{16,24},{24,16},{32,40},{40,32},{48,56},{56,48},{64,72... | collective-permute-start | bytes 1572872 | tf_op jit(solution)/shard_map/ppermute | solution.py:463
  33.1 4.9 %copy-start = (bf16[512,2048]{1,0:T(8,128)(2,1)S(1)}, bf16[512,2048]{1,0:T(8,128)(2,1)}, u32[]{:S(2)}) copy-start(bf16[512,2048]{1,0:T(8,128)(2,1)} %mine_ref.1) | copy-start | bytes 6291460
  40.3 11.0 %collective-permute-start.11 = (bf16[128,1024]{1,0:T(8,128)(2,1)S(1)}, bf16[128,1024]{1,0:T(8,128)(2,1)S(1)}, u32[]{:S(2)}, u32[]{:S(2)}) collective-permute-start(bf16[128,1024]{1,0:T(8,128)(2,1)S(1)} %get-tuple-element.41), channel_id=1, source_target_pairs={{0,2},{1,3},{2,4},{3,5},{4,6},{5,7},{6,0},{7,1},{8,10},{9,11},{10,... | collective-permute-start | bytes 786440 | tf_op jit(solution)/shard_map/ppermute | solution.py:467
  42.0 13.2 %copy-start.3 = (s32[128,8]{0,1:T(8,128)S(1)}, s32[128,8]{0,1:T(8,128)}, u32[]{:S(2)}) copy-start(s32[128,8]{0,1:T(8,128)} %param.17) | copy-start | bytes 12292
  42.0 13.2 %copy-start.4 = (f32[128,8]{0,1:T(8,128)S(1)}, f32[128,8]{0,1:T(8,128)}, u32[]{:S(2)}) copy-start(f32[128,8]{0,1:T(8,128)} %param.18) | copy-start | bytes 12292
  42.0 9.4 %collective-permute-start.12 = (bf16[128,1024]{1,0:T(8,128)(2,1)S(1)}, bf16[128,1024]{1,0:T(8,128)(2,1)S(1)}, u32[]{:S(2)}, u32[]{:S(2)}) collective-permute-start(bf16[128,1024]{1,0:T(8,128)(2,1)S(1)} %get-tuple-element.43), channel_id=1, source_target_pairs={{0,6},{1,7},{2,0},{3,1},{4,2},{5,3},{6,4},{7,5},{8,14},{9,15},{10,... | collective-permute-start | bytes 786440 | tf_op jit(solution)/shard_map/ppermute | solution.py:467
  45.6 12.7 %collective-permute-start.14 = (bf16[128,1024]{1,0:T(8,128)(2,1)S(1)}, bf16[128,1024]{1,0:T(8,128)(2,1)S(1)}, u32[]{:S(2)}, u32[]{:S(2)}) collective-permute-start(bf16[128,1024]{1,0:T(8,128)(2,1)S(1)} %get-tuple-element.45), channel_id=1, source_target_pairs={{0,2},{1,3},{2,4},{3,5},{4,6},{5,7},{6,0},{7,1},{8,10},{9,11},{10,... | collective-permute-start | bytes 786440 | tf_op jit(solution)/shard_map/ppermute | solution.py:467
  45.7 12.6 %collective-permute-start.15 = (bf16[128,1024]{1,0:T(8,128)(2,1)S(1)}, bf16[128,1024]{1,0:T(8,128)(2,1)S(1)}, u32[]{:S(2)}, u32[]{:S(2)}) collective-permute-start(bf16[128,1024]{1,0:T(8,128)(2,1)S(1)} %get-tuple-element.46), channel_id=1, source_target_pairs={{0,6},{1,7},{2,0},{3,1},{4,2},{5,3},{6,4},{7,5},{8,14},{9,15},{10,... | collective-permute-start | bytes 786440 | tf_op jit(solution)/shard_map/ppermute | solution.py:467
  51.4 10.5 %collective-permute-start.13 = (bf16[128,1024]{1,0:T(8,128)(2,1)S(1)}, bf16[128,1024]{1,0:T(8,128)(2,1)S(1)}, u32[]{:S(2)}, u32[]{:S(2)}) collective-permute-start(bf16[128,1024]{1,0:T(8,128)(2,1)S(1)} %get-tuple-element.44), channel_id=1, source_target_pairs={{0,2},{1,3},{2,4},{3,5},{4,6},{5,7},{6,0},{7,1},{8,10},{9,11},{10,... | collective-permute-start | bytes 786440 | tf_op jit(solution)/shard_map/ppermute | solution.py:467
  53.0 9.0 %collective-permute-start.16 = (bf16[128,1024]{1,0:T(8,128)(2,1)S(1)}, bf16[128,1024]{1,0:T(8,128)(2,1)S(1)}, u32[]{:S(2)}, u32[]{:S(2)}) collective-permute-start(bf16[128,1024]{1,0:T(8,128)(2,1)S(1)} %get-tuple-element.47), channel_id=1, source_target_pairs={{0,6},{1,7},{2,0},{3,1},{4,2},{5,3},{6,4},{7,5},{8,14},{9,15},{10,... | collective-permute-start | bytes 786440 | tf_op jit(solution)/shard_map/ppermute | solution.py:467
  57.3 4.7 %copy-start.8 = (f32[2048]{0:T(1024)S(1)}, f32[2048]{0:T(1024)}, u32[]{:S(2)}) copy-start(f32[2048]{0:T(1024)} %param.16) | copy-start | bytes 24580
  65.2 82.3 %copy-start.5 = (bf16[1,2048,768]{2,1,0:T(8,128)(2,1)S(1)}, bf16[1,2048,768]{2,1,0:T(8,128)(2,1)}, u32[]{:S(2)}) copy-start(bf16[1,2048,768]{2,1,0:T(8,128)(2,1)} %gate_ref.1) | copy-start | bytes 9437188
  65.2 82.3 %copy-start.6 = (bf16[1,2048,768]{2,1,0:T(8,128)(2,1)S(1)}, bf16[1,2048,768]{2,1,0:T(8,128)(2,1)}, u32[]{:S(2)}) copy-start(bf16[1,2048,768]{2,1,0:T(8,128)(2,1)} %up_ref.1) | copy-start | bytes 9437188
  65.2 82.3 %copy-start.7 = (bf16[1,768,2048]{2,1,0:T(8,128)(2,1)S(1)}, bf16[1,768,2048]{2,1,0:T(8,128)(2,1)}, u32[]{:S(2)}) copy-start(bf16[1,768,2048]{2,1,0:T(8,128)(2,1)} %down_ref.1) | copy-start | bytes 9437188
  65.2 82.3 %copy-start.9 = (f32[8,128]{1,0:T(8,128)S(1)}, f32[8,128]{1,0:T(8,128)}, u32[]{:S(2)}) copy-start(f32[8,128]{1,0:T(8,128)} %get-tuple-element.54.stat_ref) | copy-start | bytes 12292
  163.9 82.4 %copy-start.1 = (bf16[512,1024]{1,0:T(8,128)(2,1)S(1)}, bf16[512,1024]{1,0:T(8,128)(2,1)}, u32[]{:S(2)}) copy-start(bf16[512,1024]{1,0:T(8,128)(2,1)} %get-tuple-element.52.mix2_ref) | copy-start | bytes 3145732
  163.9 82.4 %copy-start.2 = (bf16[256,1024]{1,0:T(8,128)(2,1)S(1)}, bf16[256,1024]{1,0:T(8,128)(2,1)}, u32[]{:S(2)}) copy-start(bf16[256,1024]{1,0:T(8,128)(2,1)} %get-tuple-element.51.mix1_ref) | copy-start | bytes 1572868

commit v5 on v4

--- a/solution.py
+++ b/solution.py
@@ -92,8 +92,8 @@
     return pl.pallas_call(
         route_kernel,
         out_shape=(
-            pltpu.HBM((NE * 8, TOK), BF),
-            pltpu.HBM((NE * 8, 2 * TOK), BF),
+            pltpu.VMEM((NE * 8, TOK), BF),
+            pltpu.VMEM((NE * 8, 2 * TOK), BF),
             pltpu.HBM((2 * TOK, NE * 8), BF),
             pltpu.HBM((4 * TOK, NE * 8), BF),
             pltpu.HBM((8, NE), F32),
@@ -242,48 +242,28 @@
     )(place, *(near_core(x) for x in (*blocks, own, partner)))
 
 
-def project_mine_kernel(heads_ref, mine_ref, out_ref):
-    heads = heads_ref[:, :, :HALF].reshape(4 * TOK, HALF)
-    cols = 512
-    for j in range(0, D, cols):
-        total = dot(heads, mine_ref[:, j : j + cols])
-        out_ref[:, :, j : j + cols] = total.reshape(4, TOK, cols)
-
-
-def project_mine(heads, mine):
-    return pl.pallas_call(
-        project_mine_kernel,
-        out_shape=pltpu.VMEM((4, TOK, D), F32),
-        in_specs=[VM] * 2,
-        out_specs=VM,
-        compiler_params=params(8),
-        cost_estimate=pl.CostEstimate(
-            flops=2 * 4 * TOK * HALF * D, bytes_accessed=8 << 20, transcendentals=0
-        ),
-        name="project_mine",
-    )(near_core(heads), near_core(mine))
-
-
-def project_kernel(steps, wanted, place_ref, heads_ref, mine_ref, *refs):
-    others, out_refs = refs[:4], refs[4:]
-    blocks = [(place_ref[1] + step) % 4 for step in steps]
-    rows = [heads_ref[block, :, HALF:] for block in blocks]
+def project_kernel(steps, wanted, more, place_ref, heads_ref, mine_ref, *refs):
+    others, added, out_refs = refs[:4], refs[4 : 4 + more], refs[4 + more :]
+    rows = [heads_ref[(place_ref[1] + step) % 4] for step in steps]
     heads = rows[0] if len(rows) == 1 else jnp.concatenate(rows, axis=0)
     cols = 512
     for j in range(0, D, cols):
-        other = jnp.concatenate([ref[:, j : j + cols] for ref in others], axis=0)
-        total = dot(heads, other)
+        span = slice(j, j + cols)
+        weight = jnp.concatenate([mine_ref[:, span]] + [ref[:, span] for ref in others], axis=0)
+        total = dot(heads, weight)
         for (i, low, high, kind), out_ref in zip(wanted, out_refs):
             if low <= j < high:
-                out = total[i * TOK : (i + 1) * TOK] + mine_ref[blocks[i], :, j : j + cols]
+                out = total[i * TOK : (i + 1) * TOK]
+                for ref in added:
+                    out = out + ref[:, span].astype(F32)
                 out_ref[:, j - low : j - low + cols] = out.astype(kind)
 
 
 def project(steps, wanted, place, *arrays):
     return pl.pallas_call(
-        functools.partial(project_kernel, steps, wanted),
+        functools.partial(project_kernel, steps, wanted, len(arrays) - 6),
         out_shape=[pltpu.VMEM((TOK, high - low), kind) for _, low, high, kind in wanted],
-        in_specs=[SM] + [VM] * 6,
+        in_specs=[SM] + [VM] * len(arrays),
         out_specs=[VM] * len(wanted),
         compiler_params=params(12),
         cost_estimate=pl.CostEstimate(
@@ -309,65 +289,44 @@
     )(*(near_core(x) for x in parts))
 
 
-def sum_over_z(*operands):
+def sum_over_z(hidden, *operands):
     half = D // 2
     left, right = project((2,), ((0, 0, half, BF), (0, half, D, BF)), *operands)
     left, right = turn(left, 1), turn(right, 3)
     wanted = ((0, half, D, BF), (1, 0, half, BF), (0, 0, half, F32), (1, half, D, F32))
     up_right, down_left, up_left, down_right = project((1, 3), wanted, *operands)
     up_right, down_left = turn(up_right, 1), turn(down_left, 3)
-    (own,) = project((0,), ((0, 0, D, F32),), *operands)
+    (own,) = project((0,), ((0, 0, D, F32),), *operands, hidden)
     up_left, down_right = join(up_left, left, down_right, right)
     return own, turn(up_left, 1), up_right, down_left, turn(down_right, 3)
 
 
 def residual_kernel(
-    own_ref, up_left_ref, up_right_ref, down_left_ref, down_right_ref, hidden_any, gain_ref, pick1_any, pick2_any,
-    att_ref, x_ref, hidden_ref, pick1_ref, pick2_ref, sems
+    own_ref, up_left_ref, up_right_ref, down_left_ref, down_right_ref, gain_ref, pick1_ref, pick2_ref, att_ref, x_ref
 ):
-    pairs = ((hidden_any, hidden_ref), (pick1_any, pick1_ref), (pick2_any, pick2_ref))
-    copies = [pltpu.make_async_copy(a, b, sems.at[i]) for i, (a, b) in enumerate(pairs)]
-    for copy in copies:
-        copy.start()
     left = up_left_ref[...].astype(F32) + down_left_ref[...].astype(F32)
     right = up_right_ref[...].astype(F32) + down_right_ref[...].astype(F32)
     total = own_ref[...] + jnp.concatenate([left, right], axis=1)
-    copies[0].wait()
-    total = total + hidden_ref[...].astype(F32)
     att_ref[...] = total.astype(BF)
     square = jnp.mean(total * total, axis=1, keepdims=True)
     normed = (total / jnp.sqrt(square + 1e-06) * gain_ref[...]).astype(BF)
     stack = jnp.concatenate([normed[:, : D // 2], normed[:, D // 2 :]], axis=0)
-    copies[1].wait()
-    copies[2].wait()
     rows = 256
     for first in range(0, NE * 8, rows):
         x_ref[first : first + rows, :D] = dot(pick1_ref[first : first + rows], normed).astype(BF)
         x_ref[first : first + rows, D:] = dot(pick2_ref[first : first + rows], stack).astype(BF)
 
 
-def residual(sums, hidden, gain, pick1, pick2):
+def residual(sums, gain, pick1, pick2):
     return pl.pallas_call(
         residual_kernel,
         out_shape=(jax.ShapeDtypeStruct((TOK, D), BF), pltpu.VMEM((NE * 8, WIDE), BF)),
-        in_specs=[VM] * 5 + [ANY, VM, ANY, ANY],
+        in_specs=[VM] * 8,
         out_specs=(VM, VM),
-        scratch_shapes=[
-            pltpu.VMEM(hidden.shape, BF),
-            pltpu.VMEM(pick1.shape, BF),
-            pltpu.VMEM(pick2.shape, BF),
-            pltpu.SemaphoreType.DMA((3,)),
-        ],
         compiler_params=params(12),
         cost_estimate=pl.CostEstimate(flops=1 << 30, bytes_accessed=10 << 20, transcendentals=128),
         name="residual_norm_pick",
-    )(
-        *(near_core(x) for x in sums),
-        far_memory(hidden),
-        gain.reshape(1, D),
-        far_memory(pick1),
-        far_memory(pick2),
-    )
+    )(*(near_core(x) for x in sums), gain.reshape(1, D), near_core(pick1), near_core(pick2))
 
 
 def expert_kernel(x_ref, gate_ref, up_ref, down_ref, stat_ref, y_ref):
@@ -492,9 +451,8 @@
     third, fourth = swap(first, "dp", 16, 1), swap(second, "dp", 16, 1)
     pick1, pick2, mix1, mix2, stat = route_plan(routes, gates)
     heads = attend(place, blocks, own, partner)
-    mine = project_mine(heads, out_weight)
-    sums = sum_over_z(place, heads, mine, first, second, third, fourth)
-    attended, x = residual(sums, hidden_in, norm_gain, pick1, pick2)
+    sums = sum_over_z(hidden_in, place, heads, out_weight, first, second, third, fourth)
+    attended, x = residual(sums, norm_gain, pick1, pick2)
     x = exchange(x.reshape(NE, 8, WIDE))
     y = expert_apply(x.reshape(NE * 8, WIDE), w_gate, w_up, w_down, stat)
     y = exchange(y.reshape(NE, 8, WIDE + NE))

time: 250 us -> 248 us (level)
    pallas_call x5 -> x4, Pallas kernels: 6.61 us -> 6.2 us  [the longest x3 4.33 us: project(): pl.pallas_call(functools.partial(project_kernel, steps, wanted, len(array...]
where the time goes in v5:
time: 248 us; the launch traced here: 247 us
  blocking collectives  165 us (67%)
  Pallas kernels  35.5 us (14%)
  starting transfers between devices  27.7 us (11%)
  waiting for transfers between devices  18.5 us (7%)
    all_to_all x2, blocking collectives, exchange(): return lax.all_to_all(x, ALL, split_axis=0, concat_axis=0, tiled=True)  165 us
    ppermute x12, starting transfers between devices, turn(): lax.ppermute(x, 'ctx', [(i, (i + 2 * step) % CTX) for i in range(CTX)])  21.8 us
    pallas_call x1, Pallas kernels, expert_apply(): pl.pallas_call(expert_kernel, out_shape=pltpu.VMEM((NE * 8, WIDE + NE), B...  16.4 us
    ppermute x12, waiting for transfers between devices, turn(): lax.ppermute(x, 'ctx', [(i, (i + 2 * step) % CTX) for i in range(CTX)])  11.5 us
    ppermute x4, waiting for transfers between devices, swap(): return lax.ppermute(x, axis, [(i, i ^ step) for i in range(count)])  7.03 us
  transfers between devices with their start and end apart: 17, of which 7 were waited for; matrix products, arithmetic and copies ran while one was open for 0% of the time, Pallas kernels for 4%

profile of v5, /device:TPU:0, one launch (start us, length us, event | category | flops | bytes accessed | tf_op | source)
XLA Modules:
  0.0 247.4 jit_solution(9862470661635318672)
XLA Ops:
  0.8 2.1 send_all.1
  2.9 2.9 %collective-permute-start.7 = (bf16[128,2048]{1,0:T(8,128)(2,1)S(1)}, bf16[128,2048]{1,0:T(8,128)(2,1)S(1)}, u32[]{:S(2)}, u32[]{:S(2)}) collective-permute-start(bf16[128,2048]{1,0:T(8,128)(2,1)S(1)} %get-tuple-element.39), channel_id=1, source_target_pairs={{0,65},{1,64},{2,67},{3,66},{4,69},{5,68},{6,71},{7,70},{8,73},{9,... | collective-permute-start | bytes 1572872 | tf_op jit(solution)/shard_map/ppermute | solution.py:444
  5.8 3.9 %collective-permute-start.1 = (bf16[128,1024]{1,0:T(8,128)(2,1)S(1)}, bf16[128,1024]{1,0:T(8,128)(2,1)S(1)}, u32[]{:S(2)}, u32[]{:S(2)}) collective-permute-start(bf16[128,1024]{1,0:T(8,128)(2,1)S(1)} %get-tuple-element.33), channel_id=1, source_target_pairs={{0,4},{1,5},{2,6},{3,7},{4,0},{5,1},{6,2},{7,3},{8,12},{9,13},{10,... | collective-permute-start | bytes 786440 | tf_op jit(solution)/shard_map/ppermute | solution.py:426
  9.7 1.0 collective-permute-start.3
  10.7 1.2 collective-permute-start.4
  11.9 1.5 collective-permute-start.5
  13.4 4.4 %collective-permute-done.3.refs_1_ = bf16[128,256]{1,0:T(8,128)(2,1)S(1)} collective-permute-done((bf16[128,256]{1,0:T(8,128)(2,1)S(1)}, bf16[128,256]{1,0:T(8,128)(2,1)S(1)}, u32[]{:S(2)}, u32[]{:S(2)}) %collective-permute-start.3) | collective-permute-done | bytes 65568 | tf_op jit(solution)/shard_map/ppermute | solution.py:426
  17.8 0.7 collective-permute-done.4.refs_2_
  18.5 0.7 collective-permute-done.5.refs_3_
  19.9 1.7 collective-permute-start.8
  21.6 0.8 collective-permute-start.6
  22.4 0.9 collective-permute-start
  23.2 2.4 collective-permute-start.2
  25.6 4.2 %collective-permute-done.6.partner_ref.after_ref = bf16[4,128,256]{2,1,0:T(8,128)(2,1)S(1)} collective-permute-done((bf16[4,128,256]{2,1,0:T(8,128)(2,1)S(1)}, bf16[4,128,256]{2,1,0:T(8,128)(2,1)S(1)}, u32[]{:S(2)}, u32[]{:S(2)}) %collective-permute-start.6) | collective-permute-done | bytes 262176 | tf_op jit(solution)/shard_map/ppermute | solution.py:422
  29.8 2.8 %collective-permute-done.8.x_ref = bf16[128,2048]{1,0:T(8,128)(2,1)S(1)} collective-permute-done((bf16[128,2048]{1,0:T(8,128)(2,1)S(1)}, bf16[128,2048]{1,0:T(8,128)(2,1)S(1)}, u32[]{:S(2)}, u32[]{:S(2)}) %collective-permute-start.8) | collective-permute-done | bytes 524320 | tf_op jit(solution)/shard_map/ppermute | solution.py:422
  33.1 4.9 %attend.1.heads_ref = bf16[4,128,1024]{2,1,0:T(8,128)(2,1)S(1)} custom-call(s32[4]{0:T(128)S(1)} %pad_add_fusion.place_ref, bf16[128,1024]{1,0:T(8,128)(2,1)S(1)} %get-tuple-element.31.zero_ref, bf16[128,1024]{1,0:T(8,128)(2,1)S(1)} %collective-permute-done.one_ref, bf16[128,1024]{1,0:T(8,128)(2,1)S(1)} %collective-permute-done.1.refs_4_.two_ref, ...), custom_call_target="tpu_custom_call" | custom-call | flops 5368709120 | bytes 8388608 | tf_op jit(solution)/shard_map/attend/pallas_call | solution.py:231
  38.1 1.3 project.5
  39.4 1.7 collective-permute-start.11
  41.1 2.3 collective-permute-start.12
  43.4 1.8 project.4
  45.3 3.2 %collective-permute-start.15 = (bf16[128,1024]{1,0:T(8,128)(2,1)S(1)}, bf16[128,1024]{1,0:T(8,128)(2,1)S(1)}, u32[]{:S(2)}, u32[]{:S(2)}) collective-permute-start(bf16[128,1024]{1,0:T(8,128)(2,1)S(1)} %get-tuple-element.46), channel_id=1, source_target_pairs={{0,6},{1,7},{2,0},{3,1},{4,2},{5,3},{6,4},{7,5},{8,14},{9,15},{10,... | collective-permute-start | bytes 786440 | tf_op jit(solution)/shard_map/ppermute | solution.py:426
  48.5 1.9 collective-permute-done.11.b_ref
  50.5 1.5 collective-permute-start.13
  52.0 2.2 collective-permute-start.16
  54.2 1.9 route_plan.1
  56.1 1.3 project.3.own_ref
  57.4 3.6 %collective-permute-done.13.up_left_ref = bf16[128,1024]{1,0:T(8,128)(2,1)S(1)} collective-permute-done((bf16[128,1024]{1,0:T(8,128)(2,1)S(1)}, bf16[128,1024]{1,0:T(8,128)(2,1)S(1)}, u32[]{:S(2)}, u32[]{:S(2)}) %collective-permute-start.13) | collective-permute-done | bytes 262176 | tf_op jit(solution)/shard_map/ppermute | solution.py:426
  61.0 2.1 residual_norm_pick.1
  63.2 82.3 %all_to_all.10 = bf16[128,8,3072]{2,1,0:T(8,128)(2,1)S(1)} all-to-all(bf16[128,8,3072]{2,1,0:T(8,128)(2,1)S(1)} %bitcast.16), channel_id=1, replica_groups=mesh['dp'=16,'ctx'=8] {'dp','ctx'}, dimensions={0} | all-to-all | bytes 12582912 | tf_op jit(solution)/shard_map/all_to_all | solution.py:434
  145.5 16.4 %experts.1 = bf16[1024,3200]{1,0:T(8,128)(2,1)S(1)} custom-call(bf16[1024,3072]{1,0:T(8,128)(2,1)S(1)} %bitcast.17, bf16[1,2048,768]{2,1,0:T(8,128)(2,1)S(1)} %copy-done.6, bf16[1,2048,768]{2,1,0:T(8,128)(2,1)S(1)} %copy-done.7, bf16[1,768,2048]{2,1,0:T(8,128)(2,1)S(1)} %copy-done.8, f32[8,128]{1,0:T(8,128)S(1)} %copy-done.10), custom_call_target="tpu_custom_call" | custom-call | flops 14495514624 | bytes 23068672 | tf_op jit(solution)/shard_map/experts/pallas_call | solution.py:373
  161.9 82.4 %all_to_all.11 = bf16[128,8,3200]{2,1,0:T(8,128)(2,1)S(1)} all-to-all(bf16[128,8,3200]{2,1,0:T(8,128)(2,1)S(1)} %bitcast.15), channel_id=1, replica_groups=mesh['dp'=16,'ctx'=8] {'dp','ctx'}, dimensions={0} | all-to-all | bytes 13107200 | tf_op jit(solution)/shard_map/all_to_all | solution.py:434
  244.3 3.1 %mix.1 = (bf16[128,2048]{1,0:T(8,128)(2,1)}, f32[1,128]{1,0:T(1,128)}, f32[1,128]{1,0:T(1,128)}) custom-call(bf16[256,1024]{1,0:T(8,128)(2,1)S(1)} %copy-done.2, bf16[512,1024]{1,0:T(8,128)(2,1)S(1)} %copy-done.1, bf16[1024,3200]{1,0:T(8,128)(2,1)S(1)} %bitcast.14), custom_call_target="tpu_custom_call" | custom-call | flops 2147483648 | bytes 8388608 | tf_op jit(solution)/shard_map/mix/pallas_call | solution.py:406
  (41 shorter events, 1.4 us)
Async XLA Ops:
  2.9 17.0 %collective-permute-start.7 = (bf16[128,2048]{1,0:T(8,128)(2,1)S(1)}, bf16[128,2048]{1,0:T(8,128)(2,1)S(1)}, u32[]{:S(2)}, u32[]{:S(2)}) collective-permute-start(bf16[128,2048]{1,0:T(8,128)(2,1)S(1)} %get-tuple-element.39), channel_id=1, source_target_pairs={{0,65},{1,64},{2,67},{3,66},{4,69},{5,68},{6,71},{7,70},{8,73},{9,... | collective-permute-start | bytes 1572872 | tf_op jit(solution)/shard_map/ppermute | solution.py:444
  5.8 13.5 %collective-permute-start.1 = (bf16[128,1024]{1,0:T(8,128)(2,1)S(1)}, bf16[128,1024]{1,0:T(8,128)(2,1)S(1)}, u32[]{:S(2)}, u32[]{:S(2)}) collective-permute-start(bf16[128,1024]{1,0:T(8,128)(2,1)S(1)} %get-tuple-element.33), channel_id=1, source_target_pairs={{0,4},{1,5},{2,6},{3,7},{4,0},{5,1},{6,2},{7,3},{8,12},{9,13},{10,... | collective-permute-start | bytes 786440 | tf_op jit(solution)/shard_map/ppermute | solution.py:426
  9.7 8.1 %collective-permute-start.3 = (bf16[128,256]{1,0:T(8,128)(2,1)S(1)}, bf16[128,256]{1,0:T(8,128)(2,1)S(1)}, u32[]{:S(2)}, u32[]{:S(2)}) collective-permute-start(bf16[128,256]{1,0:T(8,128)(2,1)S(1)} %get-tuple-element.36), channel_id=1, source_target_pairs={{0,2},{1,3},{2,4},{3,5},{4,6},{5,7},{6,0},{7,1},{8,10},{9,11},{10,... | collective-permute-start | bytes 196616 | tf_op jit(solution)/shard_map/ppermute | solution.py:426
  10.7 7.8 %collective-permute-start.4 = (bf16[128,256]{1,0:T(8,128)(2,1)S(1)}, bf16[128,256]{1,0:T(8,128)(2,1)S(1)}, u32[]{:S(2)}, u32[]{:S(2)}) collective-permute-start(bf16[128,256]{1,0:T(8,128)(2,1)S(1)} %get-tuple-element.37), channel_id=1, source_target_pairs={{0,4},{1,5},{2,6},{3,7},{4,0},{5,1},{6,2},{7,3},{8,12},{9,13},{10,... | collective-permute-start | bytes 196616 | tf_op jit(solution)/shard_map/ppermute | solution.py:426
  11.9 7.4 %collective-permute-start.5 = (bf16[128,256]{1,0:T(8,128)(2,1)S(1)}, bf16[128,256]{1,0:T(8,128)(2,1)S(1)}, u32[]{:S(2)}, u32[]{:S(2)}) collective-permute-start(bf16[128,256]{1,0:T(8,128)(2,1)S(1)} %get-tuple-element.38), channel_id=1, source_target_pairs={{0,6},{1,7},{2,0},{3,1},{4,2},{5,3},{6,4},{7,5},{8,14},{9,15},{10,... | collective-permute-start | bytes 196616 | tf_op jit(solution)/shard_map/ppermute | solution.py:426
  19.9 12.7 %collective-permute-start.8 = (bf16[128,2048]{1,0:T(8,128)(2,1)S(1)}, bf16[128,2048]{1,0:T(8,128)(2,1)S(1)}, u32[]{:S(2)}, u32[]{:S(2)}) collective-permute-start(bf16[128,2048]{1,0:T(8,128)(2,1)S(1)} %later.3.x_ref), channel_id=1, source_target_pairs={{0,16},{8,24},{16,0},{24,8},{32,48},{40,56},{48,32},{56,40},{64,80... | collective-permute-start | bytes 1572872 | tf_op jit(solution)/shard_map/ppermute | solution.py:422
  21.6 8.2 %collective-permute-start.6 = (bf16[4,128,256]{2,1,0:T(8,128)(2,1)S(1)}, bf16[4,128,256]{2,1,0:T(8,128)(2,1)S(1)}, u32[]{:S(2)}, u32[]{:S(2)}) collective-permute-start(bf16[4,128,256]{2,1,0:T(8,128)(2,1)S(1)} %own_keys.1.own_ref.after_ref), channel_id=1, source_target_pairs={{0,1},{1,0},{2,3},{3,2},{4,5},{5,4},{6,7},{7,6},{8,9},{9,8},{10,11... | collective-permute-start | bytes 786440 | tf_op jit(solution)/shard_map/ppermute | solution.py:422
  22.4 10.8 %collective-permute-start = (bf16[128,1024]{1,0:T(8,128)(2,1)S(1)}, bf16[128,1024]{1,0:T(8,128)(2,1)S(1)}, u32[]{:S(2)}, u32[]{:S(2)}) collective-permute-start(bf16[128,1024]{1,0:T(8,128)(2,1)S(1)} %get-tuple-element.32), channel_id=1, source_target_pairs={{0,2},{1,3},{2,4},{3,5},{4,6},{5,7},{6,0},{7,1},{8,10},{9,11},{10,... | collective-permute-start | bytes 786440 | tf_op jit(solution)/shard_map/ppermute | solution.py:426
  23.2 9.9 %collective-permute-start.2 = (bf16[128,1024]{1,0:T(8,128)(2,1)S(1)}, bf16[128,1024]{1,0:T(8,128)(2,1)S(1)}, u32[]{:S(2)}, u32[]{:S(2)}) collective-permute-start(bf16[128,1024]{1,0:T(8,128)(2,1)S(1)} %get-tuple-element.34), channel_id=1, source_target_pairs={{0,6},{1,7},{2,0},{3,1},{4,2},{5,3},{6,4},{7,5},{8,14},{9,15},{10,... | collective-permute-start | bytes 786440 | tf_op jit(solution)/shard_map/ppermute | solution.py:426
  32.6 5.5 %collective-permute-start.10 = (bf16[128,2048]{1,0:T(8,128)(2,1)S(1)}, bf16[128,2048]{1,0:T(8,128)(2,1)S(1)}, u32[]{:S(2)}, u32[]{:S(2)}) collective-permute-start(bf16[128,2048]{1,0:T(8,128)(2,1)S(1)} %later.5.refs_1_), channel_id=1, source_target_pairs={{0,8},{8,0},{16,24},{24,16},{32,40},{40,32},{48,56},{56,48},{64,72... | collective-permute-start | bytes 1572872 | tf_op jit(solution)/shard_map/ppermute | solution.py:422
  32.6 5.5 %collective-permute-start.9 = (bf16[128,2048]{1,0:T(8,128)(2,1)S(1)}, bf16[128,2048]{1,0:T(8,128)(2,1)S(1)}, u32[]{:S(2)}, u32[]{:S(2)}) collective-permute-start(bf16[128,2048]{1,0:T(8,128)(2,1)S(1)} %later.4.refs_0_), channel_id=1, source_target_pairs={{0,8},{8,0},{16,24},{24,16},{32,40},{40,32},{48,56},{56,48},{64,72... | collective-permute-start | bytes 1572872 | tf_op jit(solution)/shard_map/ppermute | solution.py:422
  33.1 5.0 %copy-start = (bf16[512,2048]{1,0:T(8,128)(2,1)S(1)}, bf16[512,2048]{1,0:T(8,128)(2,1)}, u32[]{:S(2)}) copy-start(bf16[512,2048]{1,0:T(8,128)(2,1)} %mine_ref.5) | copy-start | bytes 6291460
  38.1 16.1 %copy-start.4 = (s32[128,8]{0,1:T(8,128)S(1)}, s32[128,8]{0,1:T(8,128)}, u32[]{:S(2)}) copy-start(s32[128,8]{0,1:T(8,128)} %param.17) | copy-start | bytes 12292
  38.1 16.1 %copy-start.5 = (f32[128,8]{0,1:T(8,128)S(1)}, f32[128,8]{0,1:T(8,128)}, u32[]{:S(2)}) copy-start(f32[128,8]{0,1:T(8,128)} %param.18) | copy-start | bytes 12292
  38.1 18.0 %copy-start.3 = (bf16[128,2048]{1,0:T(8,128)(2,1)S(1)}, bf16[128,2048]{1,0:T(8,128)(2,1)}, u32[]{:S(2)}) copy-start(bf16[128,2048]{1,0:T(8,128)(2,1)} %refs_4_.1) | copy-start | bytes 1572868
  39.4 11.0 %collective-permute-start.11 = (bf16[128,1024]{1,0:T(8,128)(2,1)S(1)}, bf16[128,1024]{1,0:T(8,128)(2,1)S(1)}, u32[]{:S(2)}, u32[]{:S(2)}) collective-permute-start(bf16[128,1024]{1,0:T(8,128)(2,1)S(1)} %get-tuple-element.41), channel_id=1, source_target_pairs={{0,2},{1,3},{2,4},{3,5},{4,6},{5,7},{6,0},{7,1},{8,10},{9,11},{10,... | collective-permute-start | bytes 786440 | tf_op jit(solution)/shard_map/ppermute | solution.py:426
  41.1 20.0 %copy-start.9 = (f32[2048]{0:T(1024)S(1)}, f32[2048]{0:T(1024)}, u32[]{:S(2)}) copy-start(f32[2048]{0:T(1024)} %param.16) | copy-start | bytes 24580
  41.1 9.4 %collective-permute-start.12 = (bf16[128,1024]{1,0:T(8,128)(2,1)S(1)}, bf16[128,1024]{1,0:T(8,128)(2,1)S(1)}, u32[]{:S(2)}, u32[]{:S(2)}) collective-permute-start(bf16[128,1024]{1,0:T(8,128)(2,1)S(1)} %get-tuple-element.43), channel_id=1, source_target_pairs={{0,6},{1,7},{2,0},{3,1},{4,2},{5,3},{6,4},{7,5},{8,14},{9,15},{10,... | collective-permute-start | bytes 786440 | tf_op jit(solution)/shard_map/ppermute | solution.py:426
  45.2 12.2 %collective-permute-start.14 = (bf16[128,1024]{1,0:T(8,128)(2,1)S(1)}, bf16[128,1024]{1,0:T(8,128)(2,1)S(1)}, u32[]{:S(2)}, u32[]{:S(2)}) collective-permute-start(bf16[128,1024]{1,0:T(8,128)(2,1)S(1)} %get-tuple-element.45), channel_id=1, source_target_pairs={{0,2},{1,3},{2,4},{3,5},{4,6},{5,7},{6,0},{7,1},{8,10},{9,11},{10,... | collective-permute-start | bytes 786440 | tf_op jit(solution)/shard_map/ppermute | solution.py:426
  45.3 12.1 %collective-permute-start.15 = (bf16[128,1024]{1,0:T(8,128)(2,1)S(1)}, bf16[128,1024]{1,0:T(8,128)(2,1)S(1)}, u32[]{:S(2)}, u32[]{:S(2)}) collective-permute-start(bf16[128,1024]{1,0:T(8,128)(2,1)S(1)} %get-tuple-element.46), channel_id=1, source_target_pairs={{0,6},{1,7},{2,0},{3,1},{4,2},{5,3},{6,4},{7,5},{8,14},{9,15},{10,... | collective-permute-start | bytes 786440 | tf_op jit(solution)/shard_map/ppermute | solution.py:426
  50.5 10.5 %collective-permute-start.13 = (bf16[128,1024]{1,0:T(8,128)(2,1)S(1)}, bf16[128,1024]{1,0:T(8,128)(2,1)S(1)}, u32[]{:S(2)}, u32[]{:S(2)}) collective-permute-start(bf16[128,1024]{1,0:T(8,128)(2,1)S(1)} %get-tuple-element.44), channel_id=1, source_target_pairs={{0,2},{1,3},{2,4},{3,5},{4,6},{5,7},{6,0},{7,1},{8,10},{9,11},{10,... | collective-permute-start | bytes 786440 | tf_op jit(solution)/shard_map/ppermute | solution.py:426
  52.0 9.0 %collective-permute-start.16 = (bf16[128,1024]{1,0:T(8,128)(2,1)S(1)}, bf16[128,1024]{1,0:T(8,128)(2,1)S(1)}, u32[]{:S(2)}, u32[]{:S(2)}) collective-permute-start(bf16[128,1024]{1,0:T(8,128)(2,1)S(1)} %get-tuple-element.47), channel_id=1, source_target_pairs={{0,6},{1,7},{2,0},{3,1},{4,2},{5,3},{6,4},{7,5},{8,14},{9,15},{10,... | collective-permute-start | bytes 786440 | tf_op jit(solution)/shard_map/ppermute | solution.py:426
  63.1 82.3 %copy-start.6 = (bf16[1,2048,768]{2,1,0:T(8,128)(2,1)S(1)}, bf16[1,2048,768]{2,1,0:T(8,128)(2,1)}, u32[]{:S(2)}) copy-start(bf16[1,2048,768]{2,1,0:T(8,128)(2,1)} %gate_ref.1) | copy-start | bytes 9437188
  63.1 82.3 %copy-start.7 = (bf16[1,2048,768]{2,1,0:T(8,128)(2,1)S(1)}, bf16[1,2048,768]{2,1,0:T(8,128)(2,1)}, u32[]{:S(2)}) copy-start(bf16[1,2048,768]{2,1,0:T(8,128)(2,1)} %up_ref.1) | copy-start | bytes 9437188
  63.2 82.3 %copy-start.8 = (bf16[1,768,2048]{2,1,0:T(8,128)(2,1)S(1)}, bf16[1,768,2048]{2,1,0:T(8,128)(2,1)}, u32[]{:S(2)}) copy-start(bf16[1,768,2048]{2,1,0:T(8,128)(2,1)} %down_ref.1) | copy-start | bytes 9437188
  63.2 82.3 %copy-start.10 = (f32[8,128]{1,0:T(8,128)S(1)}, f32[8,128]{1,0:T(8,128)}, u32[]{:S(2)}) copy-start(f32[8,128]{1,0:T(8,128)} %get-tuple-element.54.stat_ref) | copy-start | bytes 12292
  161.9 82.4 %copy-start.1 = (bf16[512,1024]{1,0:T(8,128)(2,1)S(1)}, bf16[512,1024]{1,0:T(8,128)(2,1)}, u32[]{:S(2)}) copy-start(bf16[512,1024]{1,0:T(8,128)(2,1)} %get-tuple-element.52.mix2_ref) | copy-start | bytes 3145732
  161.9 82.4 %copy-start.2 = (bf16[256,1024]{1,0:T(8,128)(2,1)S(1)}, bf16[256,1024]{1,0:T(8,128)(2,1)}, u32[]{:S(2)}) copy-start(bf16[256,1024]{1,0:T(8,128)(2,1)} %get-tuple-element.51.mix1_ref) | copy-start | bytes 1572868

commit v6 on v5

--- a/solution.py
+++ b/solution.py
@@ -73,13 +73,11 @@
 
     def put(ref, first, chosen):
         mix = jnp.transpose(jnp.where(chosen, weights, 0.0))
-        high = mix.astype(BF)
-        ref[first : first + TOK, :] = high
-        ref[first + TOK : first + 2 * TOK, :] = (mix - high.astype(F32)).astype(BF)
+        ref[first : first + TOK, :] = mix.astype(BF)
 
     put(mix1_ref, 0, pick1)
     put(mix2_ref, 0, left)
-    put(mix2_ref, 2 * TOK, right)
+    put(mix2_ref, TOK, right)
     stat_ref[...] = jnp.zeros((8, NE), F32)
     stat_ref[0:1, :] = jnp.sum(jnp.transpose(named), axis=0, keepdims=True)
     total = jnp.sum(jnp.transpose(weight), axis=0, keepdims=True)
@@ -94,8 +92,8 @@
         out_shape=(
             pltpu.VMEM((NE * 8, TOK), BF),
             pltpu.VMEM((NE * 8, 2 * TOK), BF),
+            pltpu.HBM((TOK, NE * 8), BF),
             pltpu.HBM((2 * TOK, NE * 8), BF),
-            pltpu.HBM((4 * TOK, NE * 8), BF),
             pltpu.HBM((8, NE), F32),
         ),
         in_specs=[VM] * 2,
@@ -120,23 +118,26 @@
 
 def send_kernel(place_ref, keys_ref, values_ref, q_ref, weight_ref, *refs):
     rows = pl.ds(pl.multiple_of((2 * place_ref[0] + place_ref[3]) * PIECE, PIECE), PIECE)
-    pairs = [(weight_ref.at[rows], refs[8])]
-    for step in range(4):
+    pairs = [(weight_ref.at[rows], refs[6])]
+    wide = GH * DH
+    for step, (kv_ref, base, query_ref) in enumerate(
+        ((refs[0], 0, refs[3]), (refs[1], 0, refs[4]), (refs[5], wide, refs[5]), (refs[2], 0, refs[7]))
+    ):
         cols = group_cols(place_ref, step, DH)
-        pairs.append((keys_ref.at[:, cols], refs[step].at[:, :DH]))
-        pairs.append((values_ref.at[:, cols], refs[step].at[:, DH:]))
-        pairs.append((q_ref.at[:, group_cols(place_ref, step, GH * DH)], refs[4 + step]))
-    fetch_all(pairs, refs[9])
+        pairs.append((keys_ref.at[:, cols], kv_ref.at[:, base : base + DH]))
+        pairs.append((values_ref.at[:, cols], kv_ref.at[:, base + DH : base + 2 * DH]))
+        pairs.append((q_ref.at[:, group_cols(place_ref, step, wide)], query_ref.at[:, :wide]))
+    fetch_all(pairs, refs[8])
 
 
 def send_all(place, *arrays):
+    pair, block = pltpu.VMEM((TOK, 2 * DH), BF), pltpu.VMEM((TOK, GH * DH), BF)
+    both = pltpu.VMEM((TOK, GH * DH + 2 * DH), BF)
     return pl.pallas_call(
         send_kernel,
-        out_shape=[pltpu.VMEM((TOK, 2 * DH), BF)] * 4
-        + [pltpu.VMEM((TOK, GH * DH), BF)] * 4
-        + [pltpu.VMEM((PIECE, D), BF)],
+        out_shape=[pair, pair, pair, block, block, both, pltpu.VMEM((PIECE, D), BF), block],
         in_specs=[SM] + [ANY] * 4,
-        out_specs=[VM] * 9,
+        out_specs=[VM] * 8,
         scratch_shapes=[pltpu.SemaphoreType.DMA((13,))],
         compiler_params=params(4),
         name="send_all",
@@ -145,18 +146,18 @@
 
 def own_keys_kernel(place_ref, *refs):
     for step in range(4):
-        refs[5][(place_ref[1] + 4 - step) % 4] = refs[step][...]
-
-
-def own_keys(place, blocks, after):
+        refs[4][(place_ref[1] + 4 - step) % 4] = refs[step][:, -2 * DH :]
+
+
+def own_keys(place, blocks):
     return pl.pallas_call(
         own_keys_kernel,
         out_shape=pltpu.VMEM((4, TOK, 2 * DH), BF),
-        in_specs=[SM] + [VM] * 4 + [ANY],
+        in_specs=[SM] + [VM] * 4,
         out_specs=VM,
         compiler_params=params(4),
         name="own_keys",
-    )(place, *(near_core(x) for x in blocks), after)
+    )(place, *(near_core(x) for x in blocks))
 
 
 def later_kernel(x_ref, after_ref, out_ref):
@@ -173,6 +174,44 @@
         compiler_params=params(4),
         name="later",
     )(x, after)
+
+
+def cut_kernel(x_ref, after_ref, top_ref, bottom_ref):
+    del after_ref
+    half = x_ref.shape[0] // 2
+    top_ref[...] = x_ref[:half]
+    bottom_ref[...] = x_ref[half:]
+
+
+def cut(x, after):
+    rows, cols = x.shape
+    return pl.pallas_call(
+        cut_kernel,
+        out_shape=[pltpu.VMEM((rows // 2, cols), x.dtype)] * 2,
+        in_specs=[VM, ANY],
+        out_specs=[VM] * 2,
+        compiler_params=params(4),
+        name="cut",
+    )(near_core(x), after)
+
+
+def stack_kernel(top_ref, bottom_ref, after_ref, out_ref):
+    del after_ref
+    half = top_ref.shape[0]
+    out_ref[:half] = top_ref[...]
+    out_ref[half:] = bottom_ref[...]
+
+
+def stack(top, bottom, after):
+    rows, cols = top.shape
+    return pl.pallas_call(
+        stack_kernel,
+        out_shape=pltpu.VMEM((2 * rows, cols), top.dtype),
+        in_specs=[VM, VM, ANY],
+        out_specs=VM,
+        compiler_params=params(4),
+        name="stack",
+    )(near_core(top), near_core(bottom), after)
 
 
 SCALE = math.log2(math.e) / math.sqrt(DH)
@@ -387,11 +426,11 @@
     cols = 512
     for j in range(D // cols):
         at = j * cols
-        side = (j // 2) * 2 * TOK
+        side = (j // 2) * TOK
         rest = D + (j % 2) * cols
         both = dot(mix1_ref[...], y_ref[:, at : at + cols])
-        both = both + dot(mix2_ref[side : side + 2 * TOK], y_ref[:, rest : rest + cols])
-        out_ref[:, at : at + cols] = (both[:TOK] + both[TOK:]).astype(BF)
+        both = both + dot(mix2_ref[side : side + TOK], y_ref[:, rest : rest + cols])
+        out_ref[:, at : at + cols] = both.astype(BF)
     stat = jnp.sum(y_ref[:, WIDE:].astype(F32).reshape(NE, 8, NE), axis=0)
     counts = stat[0:1]
     gates = stat[1:2] + stat[2:3]
@@ -426,8 +465,8 @@
     return lax.ppermute(x, "ctx", [(i, (i + 2 * step) % CTX) for i in range(CTX)])
 
 
-def turn_all(blocks):
-    return [blocks[0]] + [turn(blocks[step], step) for step in (1, 2, 3)]
+def along_y(x, step):
+    return lax.ppermute(x, "dp", [(i, i // 8 * 8 + (i + 2 * step) % 8) for i in range(16)])
 
 
 def exchange(x):
@@ -440,14 +479,15 @@
     spot = lax.axis_index("ctx").astype(jnp.int32)
     column = lax.axis_index("dp").astype(jnp.int32)
     place = jnp.stack([column % 2, spot // 2, spot % 2, column // 2 % 2])
-    *sent, weight = send_all(place, keys, values, queries, out_weight)
+    k0, k1, k3, q0, q1, both, weight, q3 = send_all(place, keys, values, queries, out_weight)
     first = lax.ppermute(weight, ALL, [(i, i ^ 65) for i in range(NE)])
-    sent, blocks = turn_all(sent[:4]), turn_all(sent[4:])
-    own = own_keys(place, sent, blocks[2])
+    both = turn(both, 2)
+    own = own_keys(place, (k0, turn(k1, 1), both, turn(k3, 3)))
+    blocks = (q0, turn(q1, 1), both, turn(q3, 3))
     partner = swap(own, "ctx", CTX, 1)
-    first = later(first, own)
-    second = swap(first, "dp", 16, 2)
-    first, second = later(first, partner), later(second, partner)
+    top, bottom = cut(first, own)
+    second = stack(along_y(top, 1), along_y(bottom, 3), partner)
+    first = later(first, partner)
     third, fourth = swap(first, "dp", 16, 1), swap(second, "dp", 16, 1)
     pick1, pick2, mix1, mix2, stat = route_plan(routes, gates)
     heads = attend(place, blocks, own, partner)

time: 248 us -> 244 us (0.984)
  waiting for transfers between devices: 18.5 us -> 15.6 us
    ppermute x4 -> x3, waiting for transfers between devices: 7.03 us -> 1.58 us  [swap(): return lax.ppermute(x, axis, [(i, i ^ step) for i in range(count)])]
    ppermute x0 -> x2, starting transfers between devices: none -> 3.31 us  [along_y(): lax.ppermute(x, 'dp', [(i, i // 8 * 8 + (i + 2 * step) % 8) for i in rang...]
    ppermute x12 -> x11, waiting for transfers between devices: 11.5 us -> 13.6 us  [turn(): lax.ppermute(x, 'ctx', [(i, (i + 2 * step) % CTX) for i in range(CTX)])]
    ppermute x12 -> x11, starting transfers between devices: 21.8 us -> 20.3 us  [turn(): lax.ppermute(x, 'ctx', [(i, (i + 2 * step) % CTX) for i in range(CTX)])]
  transfers between devices with their start and end apart: 17 -> 17, of which waited for: 7 -> 8; matrix products, arithmetic and copies ran while one was open for 0% -> 0% of each run, Pallas kernels for 4% -> 4%
where the time goes in v6:
time: 244 us
  blocking collectives  166 us (68%)
  Pallas kernels  34.1 us (14%)
  starting transfers between devices  27.5 us (11%)
  waiting for transfers between devices  15.6 us (6%)
    all_to_all x2, blocking collectives, exchange(): return lax.all_to_all(x, ALL, split_axis=0, concat_axis=0, tiled=True)  166 us
    ppermute x11, starting transfers between devices, turn(): lax.ppermute(x, 'ctx', [(i, (i + 2 * step) % CTX) for i in range(CTX)])  20.3 us
    pallas_call x1, Pallas kernels, expert_apply(): pl.pallas_call(expert_kernel, out_shape=pltpu.VMEM((NE * 8, WIDE + NE), B...  16.4 us
    ppermute x11, waiting for transfers between devices, turn(): lax.ppermute(x, 'ctx', [(i, (i + 2 * step) % CTX) for i in range(CTX)])  13.6 us
  transfers between devices with their start and end apart: 17, of which 8 were waited for; matrix products, arithmetic and copies ran while one was open for 0% of the time, Pallas kernels for 4%

profile of v6, /device:TPU:0, one launch (start us, length us, event | category | flops | bytes accessed | tf_op | source)
XLA Modules:
  0.0 244.2 jit_solution(3426920796907458147)
XLA Ops:
  0.8 2.1 send_all.1
  2.9 2.9 %collective-permute-start.6 = (bf16[128,2048]{1,0:T(8,128)(2,1)S(1)}, bf16[128,2048]{1,0:T(8,128)(2,1)S(1)}, u32[]{:S(2)}, u32[]{:S(2)}) collective-permute-start(bf16[128,2048]{1,0:T(8,128)(2,1)S(1)} %get-tuple-element.39), channel_id=1, source_target_pairs={{0,65},{1,64},{2,67},{3,66},{4,69},{5,68},{6,71},{7,70},{8,73},{9,... | collective-permute-start | bytes 1572872 | tf_op jit(solution)/shard_map/ppermute | solution.py:483
  5.8 3.9 %collective-permute-start.1 = (bf16[128,1280]{1,0:T(8,128)(2,1)S(1)}, bf16[128,1280]{1,0:T(8,128)(2,1)S(1)}, u32[]{:S(2)}, u32[]{:S(2)}) collective-permute-start(bf16[128,1280]{1,0:T(8,128)(2,1)S(1)} %get-tuple-element.34), channel_id=1, source_target_pairs={{0,4},{1,5},{2,6},{3,7},{4,0},{5,1},{6,2},{7,3},{8,12},{9,13},{10,... | collective-permute-start | bytes 983048 | tf_op jit(solution)/shard_map/ppermute | solution.py:465
  9.7 1.0 collective-permute-start.3
  10.7 2.2 collective-permute-start.4
  12.9 5.6 %collective-permute-done.3.refs_1_ = bf16[128,256]{1,0:T(8,128)(2,1)S(1)} collective-permute-done((bf16[128,256]{1,0:T(8,128)(2,1)S(1)}, bf16[128,256]{1,0:T(8,128)(2,1)S(1)}, u32[]{:S(2)}, u32[]{:S(2)}) %collective-permute-start.3) | collective-permute-done | bytes 65568 | tf_op jit(solution)/shard_map/ppermute | solution.py:465
  18.5 0.8 collective-permute-done.4.refs_3_
  19.3 0.6 own_keys.1.own_ref.after_ref
  19.9 0.9 collective-permute-start.5
  20.8 1.6 collective-permute-start.7
  22.4 1.7 collective-permute-start.8
  24.1 1.0 collective-permute-start
  25.1 2.2 collective-permute-start.2
  27.3 1.6 collective-permute-done.5.partner_ref.after_ref
  29.5 3.0 %collective-permute-done.one_ref = bf16[128,1024]{1,0:T(8,128)(2,1)S(1)} collective-permute-done((bf16[128,1024]{1,0:T(8,128)(2,1)S(1)}, bf16[128,1024]{1,0:T(8,128)(2,1)S(1)}, u32[]{:S(2)}, u32[]{:S(2)}) %collective-permute-start) | collective-permute-done | bytes 262176 | tf_op jit(solution)/shard_map/ppermute | solution.py:465
  32.5 4.9 %attend.1.heads_ref = bf16[4,128,1024]{2,1,0:T(8,128)(2,1)S(1)} custom-call(s32[4]{0:T(128)S(1)} %pad_add_fusion.place_ref, bf16[128,1024]{1,0:T(8,128)(2,1)S(1)} %get-tuple-element.32.zero_ref, bf16[128,1024]{1,0:T(8,128)(2,1)S(1)} %collective-permute-done.one_ref, bf16[128,1280]{1,0:T(8,128)(2,1)S(1)} %collective-permute-done.1.refs_2_.two_ref, ...), custom_call_target="tpu_custom_call" | custom-call | flops 5368709120 | bytes 8388608 | tf_op jit(solution)/shard_map/attend/pallas_call | solution.py:270
  37.5 1.3 project.5
  38.7 1.2 collective-permute-start.11
  40.0 2.1 collective-permute-start.12
  42.1 1.8 project.4
  43.9 3.2 %collective-permute-start.15 = (bf16[128,1024]{1,0:T(8,128)(2,1)S(1)}, bf16[128,1024]{1,0:T(8,128)(2,1)S(1)}, u32[]{:S(2)}, u32[]{:S(2)}) collective-permute-start(bf16[128,1024]{1,0:T(8,128)(2,1)S(1)} %get-tuple-element.48), channel_id=1, source_target_pairs={{0,6},{1,7},{2,0},{3,1},{4,2},{5,3},{6,4},{7,5},{8,14},{9,15},{10,... | collective-permute-start | bytes 786440 | tf_op jit(solution)/shard_map/ppermute | solution.py:465
  47.5 1.1 collective-permute-done.12.d_ref
  48.7 2.1 collective-permute-start.13
  50.8 1.2 collective-permute-start.16
  52.0 1.5 route_plan.1
  53.5 1.3 project.3.own_ref
  54.8 2.8 %collective-permute-done.13.up_left_ref = bf16[128,1024]{1,0:T(8,128)(2,1)S(1)} collective-permute-done((bf16[128,1024]{1,0:T(8,128)(2,1)S(1)}, bf16[128,1024]{1,0:T(8,128)(2,1)S(1)}, u32[]{:S(2)}, u32[]{:S(2)}) %collective-permute-start.13) | collective-permute-done | bytes 262176 | tf_op jit(solution)/shard_map/ppermute | solution.py:465
  57.6 2.1 residual_norm_pick.1
  59.8 83.5 %all_to_all.10 = bf16[128,8,3072]{2,1,0:T(8,128)(2,1)S(1)} all-to-all(bf16[128,8,3072]{2,1,0:T(8,128)(2,1)S(1)} %bitcast.16), channel_id=1, replica_groups=mesh['dp'=16,'ctx'=8] {'dp','ctx'}, dimensions={0} | all-to-all | bytes 12582912 | tf_op jit(solution)/shard_map/all_to_all | solution.py:473
  143.3 16.4 %experts.1 = bf16[1024,3200]{1,0:T(8,128)(2,1)S(1)} custom-call(bf16[1024,3072]{1,0:T(8,128)(2,1)S(1)} %bitcast.17, bf16[1,2048,768]{2,1,0:T(8,128)(2,1)S(1)} %copy-done.4, bf16[1,2048,768]{2,1,0:T(8,128)(2,1)S(1)} %copy-done.5, bf16[1,768,2048]{2,1,0:T(8,128)(2,1)S(1)} %copy-done.6, f32[8,128]{1,0:T(8,128)S(1)} %copy-done.10), custom_call_target="tpu_custom_call" | custom-call | flops 14495514624 | bytes 23068672 | tf_op jit(solution)/shard_map/experts/pallas_call | solution.py:412
  159.7 82.4 %all_to_all.11 = bf16[128,8,3200]{2,1,0:T(8,128)(2,1)S(1)} all-to-all(bf16[128,8,3200]{2,1,0:T(8,128)(2,1)S(1)} %bitcast.15), channel_id=1, replica_groups=mesh['dp'=16,'ctx'=8] {'dp','ctx'}, dimensions={0} | all-to-all | bytes 13107200 | tf_op jit(solution)/shard_map/all_to_all | solution.py:473
  242.1 2.1 mix.1
  (41 shorter events, 1.3 us)
Async XLA Ops:
  2.9 17.9 %collective-permute-start.6 = (bf16[128,2048]{1,0:T(8,128)(2,1)S(1)}, bf16[128,2048]{1,0:T(8,128)(2,1)S(1)}, u32[]{:S(2)}, u32[]{:S(2)}) collective-permute-start(bf16[128,2048]{1,0:T(8,128)(2,1)S(1)} %get-tuple-element.39), channel_id=1, source_target_pairs={{0,65},{1,64},{2,67},{3,66},{4,69},{5,68},{6,71},{7,70},{8,73},{9,... | collective-permute-start | bytes 1572872 | tf_op jit(solution)/shard_map/ppermute | solution.py:483
  5.8 13.5 %collective-permute-start.1 = (bf16[128,1280]{1,0:T(8,128)(2,1)S(1)}, bf16[128,1280]{1,0:T(8,128)(2,1)S(1)}, u32[]{:S(2)}, u32[]{:S(2)}) collective-permute-start(bf16[128,1280]{1,0:T(8,128)(2,1)S(1)} %get-tuple-element.34), channel_id=1, source_target_pairs={{0,4},{1,5},{2,6},{3,7},{4,0},{5,1},{6,2},{7,3},{8,12},{9,13},{10,... | collective-permute-start | bytes 983048 | tf_op jit(solution)/shard_map/ppermute | solution.py:465
  9.7 8.8 %collective-permute-start.3 = (bf16[128,256]{1,0:T(8,128)(2,1)S(1)}, bf16[128,256]{1,0:T(8,128)(2,1)S(1)}, u32[]{:S(2)}, u32[]{:S(2)}) collective-permute-start(bf16[128,256]{1,0:T(8,128)(2,1)S(1)} %get-tuple-element.37), channel_id=1, source_target_pairs={{0,2},{1,3},{2,4},{3,5},{4,6},{5,7},{6,0},{7,1},{8,10},{9,11},{10,... | collective-permute-start | bytes 196616 | tf_op jit(solution)/shard_map/ppermute | solution.py:465
  10.7 8.6 %collective-permute-start.4 = (bf16[128,256]{1,0:T(8,128)(2,1)S(1)}, bf16[128,256]{1,0:T(8,128)(2,1)S(1)}, u32[]{:S(2)}, u32[]{:S(2)}) collective-permute-start(bf16[128,256]{1,0:T(8,128)(2,1)S(1)} %get-tuple-element.38), channel_id=1, source_target_pairs={{0,6},{1,7},{2,0},{3,1},{4,2},{5,3},{6,4},{7,5},{8,14},{9,15},{10,... | collective-permute-start | bytes 196616 | tf_op jit(solution)/shard_map/ppermute | solution.py:465
  19.9 9.0 %collective-permute-start.5 = (bf16[4,128,256]{2,1,0:T(8,128)(2,1)S(1)}, bf16[4,128,256]{2,1,0:T(8,128)(2,1)S(1)}, u32[]{:S(2)}, u32[]{:S(2)}) collective-permute-start(bf16[4,128,256]{2,1,0:T(8,128)(2,1)S(1)} %own_keys.1.own_ref.after_ref), channel_id=1, source_target_pairs={{0,1},{1,0},{2,3},{3,2},{4,5},{5,4},{6,7},{7,6},{8,9},{9,8},{10,11... | collective-permute-start | bytes 786440 | tf_op jit(solution)/shard_map/ppermute | solution.py:461
  20.8 8.5 %collective-permute-start.7 = (bf16[64,2048]{1,0:T(8,128)(2,1)S(1)}, bf16[64,2048]{1,0:T(8,128)(2,1)S(1)}, u32[]{:S(2)}, u32[]{:S(2)}) collective-permute-start(bf16[64,2048]{1,0:T(8,128)(2,1)S(1)} %get-tuple-element.40), channel_id=1, source_target_pairs={{0,16},{8,24},{16,32},{24,40},{32,48},{40,56},{48,0},{56,8},{64,80... | collective-permute-start | bytes 786440 | tf_op jit(solution)/shard_map/ppermute | solution.py:469
  22.4 6.9 %collective-permute-start.8 = (bf16[64,2048]{1,0:T(8,128)(2,1)S(1)}, bf16[64,2048]{1,0:T(8,128)(2,1)S(1)}, u32[]{:S(2)}, u32[]{:S(2)}) collective-permute-start(bf16[64,2048]{1,0:T(8,128)(2,1)S(1)} %get-tuple-element.41), channel_id=1, source_target_pairs={{0,48},{8,56},{16,0},{24,8},{32,16},{40,24},{48,32},{56,40},{64,11... | collective-permute-start | bytes 786440 | tf_op jit(solution)/shard_map/ppermute | solution.py:469
  24.1 8.4 %collective-permute-start = (bf16[128,1024]{1,0:T(8,128)(2,1)S(1)}, bf16[128,1024]{1,0:T(8,128)(2,1)S(1)}, u32[]{:S(2)}, u32[]{:S(2)}) collective-permute-start(bf16[128,1024]{1,0:T(8,128)(2,1)S(1)} %get-tuple-element.33), channel_id=1, source_target_pairs={{0,2},{1,3},{2,4},{3,5},{4,6},{5,7},{6,0},{7,1},{8,10},{9,11},{10,... | collective-permute-start | bytes 786440 | tf_op jit(solution)/shard_map/ppermute | solution.py:465
  25.1 7.4 %collective-permute-start.2 = (bf16[128,1024]{1,0:T(8,128)(2,1)S(1)}, bf16[128,1024]{1,0:T(8,128)(2,1)S(1)}, u32[]{:S(2)}, u32[]{:S(2)}) collective-permute-start(bf16[128,1024]{1,0:T(8,128)(2,1)S(1)} %get-tuple-element.35), channel_id=1, source_target_pairs={{0,6},{1,7},{2,0},{3,1},{4,2},{5,3},{6,4},{7,5},{8,14},{9,15},{10,... | collective-permute-start | bytes 786440 | tf_op jit(solution)/shard_map/ppermute | solution.py:465
  28.9 8.5 %collective-permute-start.9 = (bf16[128,2048]{1,0:T(8,128)(2,1)S(1)}, bf16[128,2048]{1,0:T(8,128)(2,1)S(1)}, u32[]{:S(2)}, u32[]{:S(2)}) collective-permute-start(bf16[128,2048]{1,0:T(8,128)(2,1)S(1)} %later.1.refs_0_), channel_id=1, source_target_pairs={{0,8},{8,0},{16,24},{24,16},{32,40},{40,32},{48,56},{56,48},{64,72... | collective-permute-start | bytes 1572872 | tf_op jit(solution)/shard_map/ppermute | solution.py:461
  29.4 8.1 %collective-permute-start.10 = (bf16[128,2048]{1,0:T(8,128)(2,1)S(1)}, bf16[128,2048]{1,0:T(8,128)(2,1)S(1)}, u32[]{:S(2)}, u32[]{:S(2)}) collective-permute-start(bf16[128,2048]{1,0:T(8,128)(2,1)S(1)} %stack.21.refs_1_), channel_id=1, source_target_pairs={{0,8},{8,0},{16,24},{24,16},{32,40},{40,32},{48,56},{56,48},{64,72... | collective-permute-start | bytes 1572872 | tf_op jit(solution)/shard_map/ppermute | solution.py:461
  32.5 4.9 %copy-start = (bf16[512,2048]{1,0:T(8,128)(2,1)S(1)}, bf16[512,2048]{1,0:T(8,128)(2,1)}, u32[]{:S(2)}) copy-start(bf16[512,2048]{1,0:T(8,128)(2,1)} %mine_ref.5) | copy-start | bytes 6291460
  37.4 14.6 %copy-start.2 = (s32[128,8]{0,1:T(8,128)S(1)}, s32[128,8]{0,1:T(8,128)}, u32[]{:S(2)}) copy-start(s32[128,8]{0,1:T(8,128)} %param.17) | copy-start | bytes 12292
  37.4 14.6 %copy-start.3 = (f32[128,8]{0,1:T(8,128)S(1)}, f32[128,8]{0,1:T(8,128)}, u32[]{:S(2)}) copy-start(f32[128,8]{0,1:T(8,128)} %param.18) | copy-start | bytes 12292
  37.4 16.1 %copy-start.1 = (bf16[128,2048]{1,0:T(8,128)(2,1)S(1)}, bf16[128,2048]{1,0:T(8,128)(2,1)}, u32[]{:S(2)}) copy-start(bf16[128,2048]{1,0:T(8,128)(2,1)} %refs_4_.1) | copy-start | bytes 1572868
  38.7 8.7 %collective-permute-start.11 = (bf16[128,1024]{1,0:T(8,128)(2,1)S(1)}, bf16[128,1024]{1,0:T(8,128)(2,1)S(1)}, u32[]{:S(2)}, u32[]{:S(2)}) collective-permute-start(bf16[128,1024]{1,0:T(8,128)(2,1)S(1)} %get-tuple-element.43), channel_id=1, source_target_pairs={{0,2},{1,3},{2,4},{3,5},{4,6},{5,7},{6,0},{7,1},{8,10},{9,11},{10,... | collective-permute-start | bytes 786440 | tf_op jit(solution)/shard_map/ppermute | solution.py:465
  40.0 17.7 %copy-start.9 = (f32[2048]{0:T(1024)S(1)}, f32[2048]{0:T(1024)}, u32[]{:S(2)}) copy-start(f32[2048]{0:T(1024)} %param.16) | copy-start | bytes 24580
  40.0 8.6 %collective-permute-start.12 = (bf16[128,1024]{1,0:T(8,128)(2,1)S(1)}, bf16[128,1024]{1,0:T(8,128)(2,1)S(1)}, u32[]{:S(2)}, u32[]{:S(2)}) collective-permute-start(bf16[128,1024]{1,0:T(8,128)(2,1)S(1)} %get-tuple-element.45), channel_id=1, source_target_pairs={{0,6},{1,7},{2,0},{3,1},{4,2},{5,3},{6,4},{7,5},{8,14},{9,15},{10,... | collective-permute-start | bytes 786440 | tf_op jit(solution)/shard_map/ppermute | solution.py:465
  43.9 11.0 %collective-permute-start.14 = (bf16[128,1024]{1,0:T(8,128)(2,1)S(1)}, bf16[128,1024]{1,0:T(8,128)(2,1)S(1)}, u32[]{:S(2)}, u32[]{:S(2)}) collective-permute-start(bf16[128,1024]{1,0:T(8,128)(2,1)S(1)} %get-tuple-element.47), channel_id=1, source_target_pairs={{0,2},{1,3},{2,4},{3,5},{4,6},{5,7},{6,0},{7,1},{8,10},{9,11},{10,... | collective-permute-start | bytes 786440 | tf_op jit(solution)/shard_map/ppermute | solution.py:465
  43.9 10.9 %collective-permute-start.15 = (bf16[128,1024]{1,0:T(8,128)(2,1)S(1)}, bf16[128,1024]{1,0:T(8,128)(2,1)S(1)}, u32[]{:S(2)}, u32[]{:S(2)}) collective-permute-start(bf16[128,1024]{1,0:T(8,128)(2,1)S(1)} %get-tuple-element.48), channel_id=1, source_target_pairs={{0,6},{1,7},{2,0},{3,1},{4,2},{5,3},{6,4},{7,5},{8,14},{9,15},{10,... | collective-permute-start | bytes 786440 | tf_op jit(solution)/shard_map/ppermute | solution.py:465
  48.7 8.9 %collective-permute-start.13 = (bf16[128,1024]{1,0:T(8,128)(2,1)S(1)}, bf16[128,1024]{1,0:T(8,128)(2,1)S(1)}, u32[]{:S(2)}, u32[]{:S(2)}) collective-permute-start(bf16[128,1024]{1,0:T(8,128)(2,1)S(1)} %get-tuple-element.46), channel_id=1, source_target_pairs={{0,2},{1,3},{2,4},{3,5},{4,6},{5,7},{6,0},{7,1},{8,10},{9,11},{10,... | collective-permute-start | bytes 786440 | tf_op jit(solution)/shard_map/ppermute | solution.py:465
  50.8 6.8 %collective-permute-start.16 = (bf16[128,1024]{1,0:T(8,128)(2,1)S(1)}, bf16[128,1024]{1,0:T(8,128)(2,1)S(1)}, u32[]{:S(2)}, u32[]{:S(2)}) collective-permute-start(bf16[128,1024]{1,0:T(8,128)(2,1)S(1)} %get-tuple-element.49), channel_id=1, source_target_pairs={{0,6},{1,7},{2,0},{3,1},{4,2},{5,3},{6,4},{7,5},{8,14},{9,15},{10,... | collective-permute-start | bytes 786440 | tf_op jit(solution)/shard_map/ppermute | solution.py:465
  59.8 83.6 %copy-start.4 = (bf16[1,2048,768]{2,1,0:T(8,128)(2,1)S(1)}, bf16[1,2048,768]{2,1,0:T(8,128)(2,1)}, u32[]{:S(2)}) copy-start(bf16[1,2048,768]{2,1,0:T(8,128)(2,1)} %gate_ref.1) | copy-start | bytes 9437188
  59.8 83.5 %copy-start.5 = (bf16[1,2048,768]{2,1,0:T(8,128)(2,1)S(1)}, bf16[1,2048,768]{2,1,0:T(8,128)(2,1)}, u32[]{:S(2)}) copy-start(bf16[1,2048,768]{2,1,0:T(8,128)(2,1)} %up_ref.1) | copy-start | bytes 9437188
  59.8 83.5 %copy-start.6 = (bf16[1,768,2048]{2,1,0:T(8,128)(2,1)S(1)}, bf16[1,768,2048]{2,1,0:T(8,128)(2,1)}, u32[]{:S(2)}) copy-start(bf16[1,768,2048]{2,1,0:T(8,128)(2,1)} %down_ref.1) | copy-start | bytes 9437188
  59.8 83.5 %copy-start.10 = (f32[8,128]{1,0:T(8,128)S(1)}, f32[8,128]{1,0:T(8,128)}, u32[]{:S(2)}) copy-start(f32[8,128]{1,0:T(8,128)} %get-tuple-element.56.stat_ref) | copy-start | bytes 12292
  159.7 82.4 %copy-start.7 = (bf16[256,1024]{1,0:T(8,128)(2,1)S(1)}, bf16[256,1024]{1,0:T(8,128)(2,1)}, u32[]{:S(2)}) copy-start(bf16[256,1024]{1,0:T(8,128)(2,1)} %get-tuple-element.54.mix2_ref) | copy-start | bytes 1572868
  159.7 82.4 %copy-start.8 = (bf16[128,1024]{1,0:T(8,128)(2,1)S(1)}, bf16[128,1024]{1,0:T(8,128)(2,1)}, u32[]{:S(2)}) copy-start(bf16[128,1024]{1,0:T(8,128)(2,1)} %get-tuple-element.53.mix1_ref) | copy-start | bytes 786436

commit v7 on v6

--- a/solution.py
+++ b/solution.py
@@ -486,8 +486,8 @@
     blocks = (q0, turn(q1, 1), both, turn(q3, 3))
     partner = swap(own, "ctx", CTX, 1)
     top, bottom = cut(first, own)
-    second = stack(along_y(top, 1), along_y(bottom, 3), partner)
-    first = later(first, partner)
+    second = stack(along_y(top, 1), along_y(bottom, 3), blocks[1])
+    first = later(first, blocks[3])
     third, fourth = swap(first, "dp", 16, 1), swap(second, "dp", 16, 1)
     pick1, pick2, mix1, mix2, stat = route_plan(routes, gates)
     heads = attend(place, blocks, own, partner)

time: 244 us -> 242 us (level)
  transfers between devices with their start and end apart: 17 -> 17, of which waited for: 8 -> 9; matrix products, arithmetic and copies ran while one was open for 0% -> 0% of each run, Pallas kernels for 4% -> 4%
where the time goes in v7:
time: 242 us
  blocking collectives  164 us (68%)
  Pallas kernels  34.1 us (14%)
  starting transfers between devices  25.2 us (10%)
  waiting for transfers between devices  17.8 us (7%)
    all_to_all x2, blocking collectives, exchange(): return lax.all_to_all(x, ALL, split_axis=0, concat_axis=0, tiled=True)  164 us
    ppermute x11, starting transfers between devices, turn(): lax.ppermute(x, 'ctx', [(i, (i + 2 * step) % CTX) for i in range(CTX)])  18.1 us
    pallas_call x1, Pallas kernels, expert_apply(): pl.pallas_call(expert_kernel, out_shape=pltpu.VMEM((NE * 8, WIDE + NE), B...  16.4 us
    ppermute x11, waiting for transfers between devices, turn(): lax.ppermute(x, 'ctx', [(i, (i + 2 * step) % CTX) for i in range(CTX)])  12.6 us
    pallas_call x1, Pallas kernels, attend(): pl.pallas_call(attend_kernel, out_shape=pltpu.VMEM((4, TOK, GH * DH), BF)...  4.88 us
  transfers between devices with their start and end apart: 17, of which 9 were waited for; matrix products, arithmetic and copies ran while one was open for 0% of the time, Pallas kernels for 4%

profile of v7, /device:TPU:0, one launch (start us, length us, event | category | flops | bytes accessed | tf_op | source)
XLA Modules:
  0.0 242.0 jit_solution(502971011576823706)
XLA Ops:
  0.8 2.1 send_all.1
  2.9 2.9 %collective-permute-start.6 = (bf16[128,2048]{1,0:T(8,128)(2,1)S(1)}, bf16[128,2048]{1,0:T(8,128)(2,1)S(1)}, u32[]{:S(2)}, u32[]{:S(2)}) collective-permute-start(bf16[128,2048]{1,0:T(8,128)(2,1)S(1)} %get-tuple-element.39), channel_id=1, source_target_pairs={{0,65},{1,64},{2,67},{3,66},{4,69},{5,68},{6,71},{7,70},{8,73},{9,... | collective-permute-start | bytes 1572872 | tf_op jit(solution)/shard_map/ppermute | solution.py:483
  5.8 3.9 %collective-permute-start.1 = (bf16[128,1280]{1,0:T(8,128)(2,1)S(1)}, bf16[128,1280]{1,0:T(8,128)(2,1)S(1)}, u32[]{:S(2)}, u32[]{:S(2)}) collective-permute-start(bf16[128,1280]{1,0:T(8,128)(2,1)S(1)} %get-tuple-element.34), channel_id=1, source_target_pairs={{0,4},{1,5},{2,6},{3,7},{4,0},{5,1},{6,2},{7,3},{8,12},{9,13},{10,... | collective-permute-start | bytes 983048 | tf_op jit(solution)/shard_map/ppermute | solution.py:465
  9.7 1.0 collective-permute-start.3
  10.7 2.2 collective-permute-start.4
  12.9 6.3 %collective-permute-done.3.refs_1_ = bf16[128,256]{1,0:T(8,128)(2,1)S(1)} collective-permute-done((bf16[128,256]{1,0:T(8,128)(2,1)S(1)}, bf16[128,256]{1,0:T(8,128)(2,1)S(1)}, u32[]{:S(2)}, u32[]{:S(2)}) %collective-permute-start.3) | collective-permute-done | bytes 65568 | tf_op jit(solution)/shard_map/ppermute | solution.py:465
  19.2 1.0 collective-permute-start.2
  20.3 0.6 own_keys.1.own_ref.after_ref
  20.9 1.6 collective-permute-start.7
  22.6 1.7 collective-permute-start.8
  24.2 0.8 collective-permute-start.5
  25.0 1.7 collective-permute-done.2.three_ref.after_ref
  26.8 2.0 collective-permute-done.7.top_ref
  29.1 3.0 %collective-permute-done.5.partner_ref = bf16[4,128,256]{2,1,0:T(8,128)(2,1)S(1)} collective-permute-done((bf16[4,128,256]{2,1,0:T(8,128)(2,1)S(1)}, bf16[4,128,256]{2,1,0:T(8,128)(2,1)S(1)}, u32[]{:S(2)}, u32[]{:S(2)}) %collective-permute-start.5) | collective-permute-done | bytes 262176 | tf_op jit(solution)/shard_map/ppermute | solution.py:461
  32.1 4.9 %attend.1.heads_ref = bf16[4,128,1024]{2,1,0:T(8,128)(2,1)S(1)} custom-call(s32[4]{0:T(128)S(1)} %pad_add_fusion.place_ref, bf16[128,1024]{1,0:T(8,128)(2,1)S(1)} %get-tuple-element.32.zero_ref, bf16[128,1024]{1,0:T(8,128)(2,1)S(1)} %collective-permute-done.one_ref.after_ref, bf16[128,1280]{1,0:T(8,128)(2,1)S(1)} %collective-permute-done.1.refs_2_.two_ref, ...), custom_call_target="tpu_custom_call" | custom-call | flops 5368709120 | bytes 8388608 | tf_op jit(solution)/shard_map/attend/pallas_call | solution.py:270
  37.0 1.3 project.5
  38.3 1.5 collective-permute-start.11
  39.9 1.8 collective-permute-start.12
  41.6 1.8 project.4
  43.4 0.3 collective-permute-start.14
  43.7 3.0 %collective-permute-start.15 = (bf16[128,1024]{1,0:T(8,128)(2,1)S(1)}, bf16[128,1024]{1,0:T(8,128)(2,1)S(1)}, u32[]{:S(2)}, u32[]{:S(2)}) collective-permute-start(bf16[128,1024]{1,0:T(8,128)(2,1)S(1)} %get-tuple-element.48), channel_id=1, source_target_pairs={{0,6},{1,7},{2,0},{3,1},{4,2},{5,3},{6,4},{7,5},{8,14},{9,15},{10,... | collective-permute-start | bytes 786440 | tf_op jit(solution)/shard_map/ppermute | solution.py:465
  47.0 1.6 collective-permute-done.12.d_ref
  48.7 2.5 %collective-permute-start.13 = (bf16[128,1024]{1,0:T(8,128)(2,1)S(1)}, bf16[128,1024]{1,0:T(8,128)(2,1)S(1)}, u32[]{:S(2)}, u32[]{:S(2)}) collective-permute-start(bf16[128,1024]{1,0:T(8,128)(2,1)S(1)} %get-tuple-element.46), channel_id=1, source_target_pairs={{0,2},{1,3},{2,4},{3,5},{4,6},{5,7},{6,0},{7,1},{8,10},{9,11},{10,... | collective-permute-start | bytes 786440 | tf_op jit(solution)/shard_map/ppermute | solution.py:465
  51.1 0.8 collective-permute-start.16
  52.0 1.5 route_plan.1
  53.5 1.3 project.3.own_ref
  54.8 2.5 %collective-permute-done.13.up_left_ref = bf16[128,1024]{1,0:T(8,128)(2,1)S(1)} collective-permute-done((bf16[128,1024]{1,0:T(8,128)(2,1)S(1)}, bf16[128,1024]{1,0:T(8,128)(2,1)S(1)}, u32[]{:S(2)}, u32[]{:S(2)}) %collective-permute-start.13) | collective-permute-done | bytes 262176 | tf_op jit(solution)/shard_map/ppermute | solution.py:465
  57.5 2.1 residual_norm_pick.1
  59.7 81.5 %all_to_all.10 = bf16[128,8,3072]{2,1,0:T(8,128)(2,1)S(1)} all-to-all(bf16[128,8,3072]{2,1,0:T(8,128)(2,1)S(1)} %bitcast.16), channel_id=1, replica_groups=mesh['dp'=16,'ctx'=8] {'dp','ctx'}, dimensions={0} | all-to-all | bytes 12582912 | tf_op jit(solution)/shard_map/all_to_all | solution.py:473
  141.1 16.4 %experts.1 = bf16[1024,3200]{1,0:T(8,128)(2,1)S(1)} custom-call(bf16[1024,3072]{1,0:T(8,128)(2,1)S(1)} %bitcast.17, bf16[1,2048,768]{2,1,0:T(8,128)(2,1)S(1)} %copy-done.4, bf16[1,2048,768]{2,1,0:T(8,128)(2,1)S(1)} %copy-done.5, bf16[1,768,2048]{2,1,0:T(8,128)(2,1)S(1)} %copy-done.6, f32[8,128]{1,0:T(8,128)S(1)} %copy-done.10), custom_call_target="tpu_custom_call" | custom-call | flops 14495514624 | bytes 23068672 | tf_op jit(solution)/shard_map/experts/pallas_call | solution.py:412
  157.6 82.4 %all_to_all.11 = bf16[128,8,3200]{2,1,0:T(8,128)(2,1)S(1)} all-to-all(bf16[128,8,3200]{2,1,0:T(8,128)(2,1)S(1)} %bitcast.15), channel_id=1, replica_groups=mesh['dp'=16,'ctx'=8] {'dp','ctx'}, dimensions={0} | all-to-all | bytes 13107200 | tf_op jit(solution)/shard_map/all_to_all | solution.py:473
  240.0 2.1 mix.1
  (41 shorter events, 1.1 us)
Async XLA Ops:
  2.9 18.0 %collective-permute-start.6 = (bf16[128,2048]{1,0:T(8,128)(2,1)S(1)}, bf16[128,2048]{1,0:T(8,128)(2,1)S(1)}, u32[]{:S(2)}, u32[]{:S(2)}) collective-permute-start(bf16[128,2048]{1,0:T(8,128)(2,1)S(1)} %get-tuple-element.39), channel_id=1, source_target_pairs={{0,65},{1,64},{2,67},{3,66},{4,69},{5,68},{6,71},{7,70},{8,73},{9,... | collective-permute-start | bytes 1572872 | tf_op jit(solution)/shard_map/ppermute | solution.py:483
  5.8 14.5 %collective-permute-start.1 = (bf16[128,1280]{1,0:T(8,128)(2,1)S(1)}, bf16[128,1280]{1,0:T(8,128)(2,1)S(1)}, u32[]{:S(2)}, u32[]{:S(2)}) collective-permute-start(bf16[128,1280]{1,0:T(8,128)(2,1)S(1)} %get-tuple-element.34), channel_id=1, source_target_pairs={{0,4},{1,5},{2,6},{3,7},{4,0},{5,1},{6,2},{7,3},{8,12},{9,13},{10,... | collective-permute-start | bytes 983048 | tf_op jit(solution)/shard_map/ppermute | solution.py:465
  9.7 9.6 %collective-permute-start.3 = (bf16[128,256]{1,0:T(8,128)(2,1)S(1)}, bf16[128,256]{1,0:T(8,128)(2,1)S(1)}, u32[]{:S(2)}, u32[]{:S(2)}) collective-permute-start(bf16[128,256]{1,0:T(8,128)(2,1)S(1)} %get-tuple-element.37), channel_id=1, source_target_pairs={{0,2},{1,3},{2,4},{3,5},{4,6},{5,7},{6,0},{7,1},{8,10},{9,11},{10,... | collective-permute-start | bytes 196616 | tf_op jit(solution)/shard_map/ppermute | solution.py:465
  10.7 9.6 %collective-permute-start.4 = (bf16[128,256]{1,0:T(8,128)(2,1)S(1)}, bf16[128,256]{1,0:T(8,128)(2,1)S(1)}, u32[]{:S(2)}, u32[]{:S(2)}) collective-permute-start(bf16[128,256]{1,0:T(8,128)(2,1)S(1)} %get-tuple-element.38), channel_id=1, source_target_pairs={{0,6},{1,7},{2,0},{3,1},{4,2},{5,3},{6,4},{7,5},{8,14},{9,15},{10,... | collective-permute-start | bytes 196616 | tf_op jit(solution)/shard_map/ppermute | solution.py:465
  12.9 13.8 %collective-permute-start = (bf16[128,1024]{1,0:T(8,128)(2,1)S(1)}, bf16[128,1024]{1,0:T(8,128)(2,1)S(1)}, u32[]{:S(2)}, u32[]{:S(2)}) collective-permute-start(bf16[128,1024]{1,0:T(8,128)(2,1)S(1)} %get-tuple-element.33), channel_id=1, source_target_pairs={{0,2},{1,3},{2,4},{3,5},{4,6},{5,7},{6,0},{7,1},{8,10},{9,11},{10,... | collective-permute-start | bytes 786440 | tf_op jit(solution)/shard_map/ppermute | solution.py:465
  19.2 7.5 %collective-permute-start.2 = (bf16[128,1024]{1,0:T(8,128)(2,1)S(1)}, bf16[128,1024]{1,0:T(8,128)(2,1)S(1)}, u32[]{:S(2)}, u32[]{:S(2)}) collective-permute-start(bf16[128,1024]{1,0:T(8,128)(2,1)S(1)} %get-tuple-element.35), channel_id=1, source_target_pairs={{0,6},{1,7},{2,0},{3,1},{4,2},{5,3},{6,4},{7,5},{8,14},{9,15},{10,... | collective-permute-start | bytes 786440 | tf_op jit(solution)/shard_map/ppermute | solution.py:465
  20.9 7.8 %collective-permute-start.7 = (bf16[64,2048]{1,0:T(8,128)(2,1)S(1)}, bf16[64,2048]{1,0:T(8,128)(2,1)S(1)}, u32[]{:S(2)}, u32[]{:S(2)}) collective-permute-start(bf16[64,2048]{1,0:T(8,128)(2,1)S(1)} %get-tuple-element.40), channel_id=1, source_target_pairs={{0,16},{8,24},{16,32},{24,40},{32,48},{40,56},{48,0},{56,8},{64,80... | collective-permute-start | bytes 786440 | tf_op jit(solution)/shard_map/ppermute | solution.py:469
  22.6 6.4 %collective-permute-start.8 = (bf16[64,2048]{1,0:T(8,128)(2,1)S(1)}, bf16[64,2048]{1,0:T(8,128)(2,1)S(1)}, u32[]{:S(2)}, u32[]{:S(2)}) collective-permute-start(bf16[64,2048]{1,0:T(8,128)(2,1)S(1)} %get-tuple-element.41), channel_id=1, source_target_pairs={{0,48},{8,56},{16,0},{24,8},{32,16},{40,24},{48,32},{56,40},{64,11... | collective-permute-start | bytes 786440 | tf_op jit(solution)/shard_map/ppermute | solution.py:469
  24.2 7.9 %collective-permute-start.5 = (bf16[4,128,256]{2,1,0:T(8,128)(2,1)S(1)}, bf16[4,128,256]{2,1,0:T(8,128)(2,1)S(1)}, u32[]{:S(2)}, u32[]{:S(2)}) collective-permute-start(bf16[4,128,256]{2,1,0:T(8,128)(2,1)S(1)} %own_keys.1.own_ref.after_ref), channel_id=1, source_target_pairs={{0,1},{1,0},{2,3},{3,2},{4,5},{5,4},{6,7},{7,6},{8,9},{9,8},{10,11... | collective-permute-start | bytes 786440 | tf_op jit(solution)/shard_map/ppermute | solution.py:461
  26.7 10.3 %collective-permute-start.9 = (bf16[128,2048]{1,0:T(8,128)(2,1)S(1)}, bf16[128,2048]{1,0:T(8,128)(2,1)S(1)}, u32[]{:S(2)}, u32[]{:S(2)}) collective-permute-start(bf16[128,2048]{1,0:T(8,128)(2,1)S(1)} %later.1.refs_0_), channel_id=1, source_target_pairs={{0,8},{8,0},{16,24},{24,16},{32,40},{40,32},{48,56},{56,48},{64,72... | collective-permute-start | bytes 1572872 | tf_op jit(solution)/shard_map/ppermute | solution.py:461
  29.0 8.1 %collective-permute-start.10 = (bf16[128,2048]{1,0:T(8,128)(2,1)S(1)}, bf16[128,2048]{1,0:T(8,128)(2,1)S(1)}, u32[]{:S(2)}, u32[]{:S(2)}) collective-permute-start(bf16[128,2048]{1,0:T(8,128)(2,1)S(1)} %stack.21.refs_1_), channel_id=1, source_target_pairs={{0,8},{8,0},{16,24},{24,16},{32,40},{40,32},{48,56},{56,48},{64,72... | collective-permute-start | bytes 1572872 | tf_op jit(solution)/shard_map/ppermute | solution.py:461
  32.1 4.9 %copy-start = (bf16[512,2048]{1,0:T(8,128)(2,1)S(1)}, bf16[512,2048]{1,0:T(8,128)(2,1)}, u32[]{:S(2)}) copy-start(bf16[512,2048]{1,0:T(8,128)(2,1)} %mine_ref.5) | copy-start | bytes 6291460
  37.0 15.0 %copy-start.2 = (s32[128,8]{0,1:T(8,128)S(1)}, s32[128,8]{0,1:T(8,128)}, u32[]{:S(2)}) copy-start(s32[128,8]{0,1:T(8,128)} %param.17) | copy-start | bytes 12292
  37.0 15.0 %copy-start.3 = (f32[128,8]{0,1:T(8,128)S(1)}, f32[128,8]{0,1:T(8,128)}, u32[]{:S(2)}) copy-start(f32[128,8]{0,1:T(8,128)} %param.18) | copy-start | bytes 12292
  37.0 16.5 %copy-start.1 = (bf16[128,2048]{1,0:T(8,128)(2,1)S(1)}, bf16[128,2048]{1,0:T(8,128)(2,1)}, u32[]{:S(2)}) copy-start(bf16[128,2048]{1,0:T(8,128)(2,1)} %refs_4_.1) | copy-start | bytes 1572868
  38.3 8.7 %collective-permute-start.11 = (bf16[128,1024]{1,0:T(8,128)(2,1)S(1)}, bf16[128,1024]{1,0:T(8,128)(2,1)S(1)}, u32[]{:S(2)}, u32[]{:S(2)}) collective-permute-start(bf16[128,1024]{1,0:T(8,128)(2,1)S(1)} %get-tuple-element.43), channel_id=1, source_target_pairs={{0,2},{1,3},{2,4},{3,5},{4,6},{5,7},{6,0},{7,1},{8,10},{9,11},{10,... | collective-permute-start | bytes 786440 | tf_op jit(solution)/shard_map/ppermute | solution.py:465
  39.9 17.7 %copy-start.9 = (f32[2048]{0:T(1024)S(1)}, f32[2048]{0:T(1024)}, u32[]{:S(2)}) copy-start(f32[2048]{0:T(1024)} %param.16) | copy-start | bytes 24580
  39.9 8.7 %collective-permute-start.12 = (bf16[128,1024]{1,0:T(8,128)(2,1)S(1)}, bf16[128,1024]{1,0:T(8,128)(2,1)S(1)}, u32[]{:S(2)}, u32[]{:S(2)}) collective-permute-start(bf16[128,1024]{1,0:T(8,128)(2,1)S(1)} %get-tuple-element.45), channel_id=1, source_target_pairs={{0,6},{1,7},{2,0},{3,1},{4,2},{5,3},{6,4},{7,5},{8,14},{9,15},{10,... | collective-permute-start | bytes 786440 | tf_op jit(solution)/shard_map/ppermute | solution.py:465
  43.4 11.4 %collective-permute-start.14 = (bf16[128,1024]{1,0:T(8,128)(2,1)S(1)}, bf16[128,1024]{1,0:T(8,128)(2,1)S(1)}, u32[]{:S(2)}, u32[]{:S(2)}) collective-permute-start(bf16[128,1024]{1,0:T(8,128)(2,1)S(1)} %get-tuple-element.47), channel_id=1, source_target_pairs={{0,2},{1,3},{2,4},{3,5},{4,6},{5,7},{6,0},{7,1},{8,10},{9,11},{10,... | collective-permute-start | bytes 786440 | tf_op jit(solution)/shard_map/ppermute | solution.py:465
  43.7 11.0 %collective-permute-start.15 = (bf16[128,1024]{1,0:T(8,128)(2,1)S(1)}, bf16[128,1024]{1,0:T(8,128)(2,1)S(1)}, u32[]{:S(2)}, u32[]{:S(2)}) collective-permute-start(bf16[128,1024]{1,0:T(8,128)(2,1)S(1)} %get-tuple-element.48), channel_id=1, source_target_pairs={{0,6},{1,7},{2,0},{3,1},{4,2},{5,3},{6,4},{7,5},{8,14},{9,15},{10,... | collective-permute-start | bytes 786440 | tf_op jit(solution)/shard_map/ppermute | solution.py:465
  48.7 8.6 %collective-permute-start.13 = (bf16[128,1024]{1,0:T(8,128)(2,1)S(1)}, bf16[128,1024]{1,0:T(8,128)(2,1)S(1)}, u32[]{:S(2)}, u32[]{:S(2)}) collective-permute-start(bf16[128,1024]{1,0:T(8,128)(2,1)S(1)} %get-tuple-element.46), channel_id=1, source_target_pairs={{0,2},{1,3},{2,4},{3,5},{4,6},{5,7},{6,0},{7,1},{8,10},{9,11},{10,... | collective-permute-start | bytes 786440 | tf_op jit(solution)/shard_map/ppermute | solution.py:465
  51.1 6.4 %collective-permute-start.16 = (bf16[128,1024]{1,0:T(8,128)(2,1)S(1)}, bf16[128,1024]{1,0:T(8,128)(2,1)S(1)}, u32[]{:S(2)}, u32[]{:S(2)}) collective-permute-start(bf16[128,1024]{1,0:T(8,128)(2,1)S(1)} %get-tuple-element.49), channel_id=1, source_target_pairs={{0,6},{1,7},{2,0},{3,1},{4,2},{5,3},{6,4},{7,5},{8,14},{9,15},{10,... | collective-permute-start | bytes 786440 | tf_op jit(solution)/shard_map/ppermute | solution.py:465
  59.6 81.5 %copy-start.4 = (bf16[1,2048,768]{2,1,0:T(8,128)(2,1)S(1)}, bf16[1,2048,768]{2,1,0:T(8,128)(2,1)}, u32[]{:S(2)}) copy-start(bf16[1,2048,768]{2,1,0:T(8,128)(2,1)} %gate_ref.1) | copy-start | bytes 9437188
  59.6 81.5 %copy-start.5 = (bf16[1,2048,768]{2,1,0:T(8,128)(2,1)S(1)}, bf16[1,2048,768]{2,1,0:T(8,128)(2,1)}, u32[]{:S(2)}) copy-start(bf16[1,2048,768]{2,1,0:T(8,128)(2,1)} %up_ref.1) | copy-start | bytes 9437188
  59.6 81.5 %copy-start.6 = (bf16[1,768,2048]{2,1,0:T(8,128)(2,1)S(1)}, bf16[1,768,2048]{2,1,0:T(8,128)(2,1)}, u32[]{:S(2)}) copy-start(bf16[1,768,2048]{2,1,0:T(8,128)(2,1)} %down_ref.1) | copy-start | bytes 9437188
  59.7 81.5 %copy-start.10 = (f32[8,128]{1,0:T(8,128)S(1)}, f32[8,128]{1,0:T(8,128)}, u32[]{:S(2)}) copy-start(f32[8,128]{1,0:T(8,128)} %get-tuple-element.56.stat_ref) | copy-start | bytes 12292
  157.5 82.4 %copy-start.7 = (bf16[256,1024]{1,0:T(8,128)(2,1)S(1)}, bf16[256,1024]{1,0:T(8,128)(2,1)}, u32[]{:S(2)}) copy-start(bf16[256,1024]{1,0:T(8,128)(2,1)} %get-tuple-element.54.mix2_ref) | copy-start | bytes 1572868
  157.6 82.4 %copy-start.8 = (bf16[128,1024]{1,0:T(8,128)(2,1)S(1)}, bf16[128,1024]{1,0:T(8,128)(2,1)}, u32[]{:S(2)}) copy-start(bf16[128,1024]{1,0:T(8,128)(2,1)} %get-tuple-element.53.mix1_ref) | copy-start | bytes 786436

commit v8 on v7

--- a/solution.py
+++ b/solution.py
@@ -348,7 +348,7 @@
     total = own_ref[...] + jnp.concatenate([left, right], axis=1)
     att_ref[...] = total.astype(BF)
     square = jnp.mean(total * total, axis=1, keepdims=True)
-    normed = (total / jnp.sqrt(square + 1e-06) * gain_ref[...]).astype(BF)
+    normed = (total * (1.0 / jnp.sqrt(square + 1e-06)) * gain_ref[...]).astype(BF)
     stack = jnp.concatenate([normed[:, : D // 2], normed[:, D // 2 :]], axis=0)
     rows = 256
     for first in range(0, NE * 8, rows):

time: 242 us -> 242 us (level)
  no operation moved by 1% of the time
where the time goes in v8:
time: 242 us
  blocking collectives  164 us (68%)
  Pallas kernels  34.1 us (14%)
  starting transfers between devices  25.2 us (10%)
  waiting for transfers between devices  17.8 us (7%)
    all_to_all x2, blocking collectives, exchange(): return lax.all_to_all(x, ALL, split_axis=0, concat_axis=0, tiled=True)  164 us
    ppermute x11, starting transfers between devices, turn(): lax.ppermute(x, 'ctx', [(i, (i + 2 * step) % CTX) for i in range(CTX)])  18.1 us
    pallas_call x1, Pallas kernels, expert_apply(): pl.pallas_call(expert_kernel, out_shape=pltpu.VMEM((NE * 8, WIDE + NE), B...  16.4 us
    ppermute x11, waiting for transfers between devices, turn(): lax.ppermute(x, 'ctx', [(i, (i + 2 * step) % CTX) for i in range(CTX)])  12.6 us
    pallas_call x1, Pallas kernels, attend(): pl.pallas_call(attend_kernel, out_shape=pltpu.VMEM((4, TOK, GH * DH), BF)...  4.88 us
  transfers between devices with their start and end apart: 17, of which 9 were waited for; matrix products, arithmetic and copies ran while one was open for 0% of the time, Pallas kernels for 4%

profile of v8, /device:TPU:0, one launch (start us, length us, event | category | flops | bytes accessed | tf_op | source)
XLA Modules:
  0.0 242.0 jit_solution(502971011576823706)
XLA Ops:
  0.8 2.1 send_all.1
  2.9 2.9 %collective-permute-start.6 = (bf16[128,2048]{1,0:T(8,128)(2,1)S(1)}, bf16[128,2048]{1,0:T(8,128)(2,1)S(1)}, u32[]{:S(2)}, u32[]{:S(2)}) collective-permute-start(bf16[128,2048]{1,0:T(8,128)(2,1)S(1)} %get-tuple-element.39), channel_id=1, source_target_pairs={{0,65},{1,64},{2,67},{3,66},{4,69},{5,68},{6,71},{7,70},{8,73},{9,... | collective-permute-start | bytes 1572872 | tf_op jit(solution)/shard_map/ppermute | solution.py:483
  5.8 3.9 %collective-permute-start.1 = (bf16[128,1280]{1,0:T(8,128)(2,1)S(1)}, bf16[128,1280]{1,0:T(8,128)(2,1)S(1)}, u32[]{:S(2)}, u32[]{:S(2)}) collective-permute-start(bf16[128,1280]{1,0:T(8,128)(2,1)S(1)} %get-tuple-element.34), channel_id=1, source_target_pairs={{0,4},{1,5},{2,6},{3,7},{4,0},{5,1},{6,2},{7,3},{8,12},{9,13},{10,... | collective-permute-start | bytes 983048 | tf_op jit(solution)/shard_map/ppermute | solution.py:465
  9.7 1.0 collective-permute-start.3
  10.7 2.2 collective-permute-start.4
  12.9 6.3 %collective-permute-done.3.refs_1_ = bf16[128,256]{1,0:T(8,128)(2,1)S(1)} collective-permute-done((bf16[128,256]{1,0:T(8,128)(2,1)S(1)}, bf16[128,256]{1,0:T(8,128)(2,1)S(1)}, u32[]{:S(2)}, u32[]{:S(2)}) %collective-permute-start.3) | collective-permute-done | bytes 65568 | tf_op jit(solution)/shard_map/ppermute | solution.py:465
  19.2 1.0 collective-permute-start.2
  20.3 0.6 own_keys.1.own_ref.after_ref
  20.9 1.6 collective-permute-start.7
  22.6 1.7 collective-permute-start.8
  24.2 0.8 collective-permute-start.5
  25.0 1.7 collective-permute-done.2.three_ref.after_ref
  26.8 2.0 collective-permute-done.7.top_ref
  29.1 3.0 %collective-permute-done.5.partner_ref = bf16[4,128,256]{2,1,0:T(8,128)(2,1)S(1)} collective-permute-done((bf16[4,128,256]{2,1,0:T(8,128)(2,1)S(1)}, bf16[4,128,256]{2,1,0:T(8,128)(2,1)S(1)}, u32[]{:S(2)}, u32[]{:S(2)}) %collective-permute-start.5) | collective-permute-done | bytes 262176 | tf_op jit(solution)/shard_map/ppermute | solution.py:461
  32.1 4.9 %attend.1.heads_ref = bf16[4,128,1024]{2,1,0:T(8,128)(2,1)S(1)} custom-call(s32[4]{0:T(128)S(1)} %pad_add_fusion.place_ref, bf16[128,1024]{1,0:T(8,128)(2,1)S(1)} %get-tuple-element.32.zero_ref, bf16[128,1024]{1,0:T(8,128)(2,1)S(1)} %collective-permute-done.one_ref.after_ref, bf16[128,1280]{1,0:T(8,128)(2,1)S(1)} %collective-permute-done.1.refs_2_.two_ref, ...), custom_call_target="tpu_custom_call" | custom-call | flops 5368709120 | bytes 8388608 | tf_op jit(solution)/shard_map/attend/pallas_call | solution.py:270
  37.0 1.3 project.5
  38.3 1.5 collective-permute-start.11
  39.9 1.8 collective-permute-start.12
  41.6 1.8 project.4
  43.4 0.3 collective-permute-start.14
  43.7 3.0 %collective-permute-start.15 = (bf16[128,1024]{1,0:T(8,128)(2,1)S(1)}, bf16[128,1024]{1,0:T(8,128)(2,1)S(1)}, u32[]{:S(2)}, u32[]{:S(2)}) collective-permute-start(bf16[128,1024]{1,0:T(8,128)(2,1)S(1)} %get-tuple-element.48), channel_id=1, source_target_pairs={{0,6},{1,7},{2,0},{3,1},{4,2},{5,3},{6,4},{7,5},{8,14},{9,15},{10,... | collective-permute-start | bytes 786440 | tf_op jit(solution)/shard_map/ppermute | solution.py:465
  47.0 1.6 collective-permute-done.12.d_ref
  48.7 2.5 %collective-permute-start.13 = (bf16[128,1024]{1,0:T(8,128)(2,1)S(1)}, bf16[128,1024]{1,0:T(8,128)(2,1)S(1)}, u32[]{:S(2)}, u32[]{:S(2)}) collective-permute-start(bf16[128,1024]{1,0:T(8,128)(2,1)S(1)} %get-tuple-element.46), channel_id=1, source_target_pairs={{0,2},{1,3},{2,4},{3,5},{4,6},{5,7},{6,0},{7,1},{8,10},{9,11},{10,... | collective-permute-start | bytes 786440 | tf_op jit(solution)/shard_map/ppermute | solution.py:465
  51.1 0.8 collective-permute-start.16
  52.0 1.5 route_plan.1
  53.5 1.3 project.3.own_ref
  54.8 2.5 %collective-permute-done.13.up_left_ref = bf16[128,1024]{1,0:T(8,128)(2,1)S(1)} collective-permute-done((bf16[128,1024]{1,0:T(8,128)(2,1)S(1)}, bf16[128,1024]{1,0:T(8,128)(2,1)S(1)}, u32[]{:S(2)}, u32[]{:S(2)}) %collective-permute-start.13) | collective-permute-done | bytes 262176 | tf_op jit(solution)/shard_map/ppermute | solution.py:465
  57.5 2.1 residual_norm_pick.1
  59.7 81.5 %all_to_all.10 = bf16[128,8,3072]{2,1,0:T(8,128)(2,1)S(1)} all-to-all(bf16[128,8,3072]{2,1,0:T(8,128)(2,1)S(1)} %bitcast.16), channel_id=1, replica_groups=mesh['dp'=16,'ctx'=8] {'dp','ctx'}, dimensions={0} | all-to-all | bytes 12582912 | tf_op jit(solution)/shard_map/all_to_all | solution.py:473
  141.1 16.4 %experts.1 = bf16[1024,3200]{1,0:T(8,128)(2,1)S(1)} custom-call(bf16[1024,3072]{1,0:T(8,128)(2,1)S(1)} %bitcast.17, bf16[1,2048,768]{2,1,0:T(8,128)(2,1)S(1)} %copy-done.4, bf16[1,2048,768]{2,1,0:T(8,128)(2,1)S(1)} %copy-done.5, bf16[1,768,2048]{2,1,0:T(8,128)(2,1)S(1)} %copy-done.6, f32[8,128]{1,0:T(8,128)S(1)} %copy-done.10), custom_call_target="tpu_custom_call" | custom-call | flops 14495514624 | bytes 23068672 | tf_op jit(solution)/shard_map/experts/pallas_call | solution.py:412
  157.6 82.4 %all_to_all.11 = bf16[128,8,3200]{2,1,0:T(8,128)(2,1)S(1)} all-to-all(bf16[128,8,3200]{2,1,0:T(8,128)(2,1)S(1)} %bitcast.15), channel_id=1, replica_groups=mesh['dp'=16,'ctx'=8] {'dp','ctx'}, dimensions={0} | all-to-all | bytes 13107200 | tf_op jit(solution)/shard_map/all_to_all | solution.py:473
  240.0 2.1 mix.1
  (41 shorter events, 1.1 us)
Async XLA Ops:
  2.9 18.0 %collective-permute-start.6 = (bf16[128,2048]{1,0:T(8,128)(2,1)S(1)}, bf16[128,2048]{1,0:T(8,128)(2,1)S(1)}, u32[]{:S(2)}, u32[]{:S(2)}) collective-permute-start(bf16[128,2048]{1,0:T(8,128)(2,1)S(1)} %get-tuple-element.39), channel_id=1, source_target_pairs={{0,65},{1,64},{2,67},{3,66},{4,69},{5,68},{6,71},{7,70},{8,73},{9,... | collective-permute-start | bytes 1572872 | tf_op jit(solution)/shard_map/ppermute | solution.py:483
  5.8 14.5 %collective-permute-start.1 = (bf16[128,1280]{1,0:T(8,128)(2,1)S(1)}, bf16[128,1280]{1,0:T(8,128)(2,1)S(1)}, u32[]{:S(2)}, u32[]{:S(2)}) collective-permute-start(bf16[128,1280]{1,0:T(8,128)(2,1)S(1)} %get-tuple-element.34), channel_id=1, source_target_pairs={{0,4},{1,5},{2,6},{3,7},{4,0},{5,1},{6,2},{7,3},{8,12},{9,13},{10,... | collective-permute-start | bytes 983048 | tf_op jit(solution)/shard_map/ppermute | solution.py:465
  9.7 9.6 %collective-permute-start.3 = (bf16[128,256]{1,0:T(8,128)(2,1)S(1)}, bf16[128,256]{1,0:T(8,128)(2,1)S(1)}, u32[]{:S(2)}, u32[]{:S(2)}) collective-permute-start(bf16[128,256]{1,0:T(8,128)(2,1)S(1)} %get-tuple-element.37), channel_id=1, source_target_pairs={{0,2},{1,3},{2,4},{3,5},{4,6},{5,7},{6,0},{7,1},{8,10},{9,11},{10,... | collective-permute-start | bytes 196616 | tf_op jit(solution)/shard_map/ppermute | solution.py:465
  10.7 9.6 %collective-permute-start.4 = (bf16[128,256]{1,0:T(8,128)(2,1)S(1)}, bf16[128,256]{1,0:T(8,128)(2,1)S(1)}, u32[]{:S(2)}, u32[]{:S(2)}) collective-permute-start(bf16[128,256]{1,0:T(8,128)(2,1)S(1)} %get-tuple-element.38), channel_id=1, source_target_pairs={{0,6},{1,7},{2,0},{3,1},{4,2},{5,3},{6,4},{7,5},{8,14},{9,15},{10,... | collective-permute-start | bytes 196616 | tf_op jit(solution)/shard_map/ppermute | solution.py:465
  12.9 13.8 %collective-permute-start = (bf16[128,1024]{1,0:T(8,128)(2,1)S(1)}, bf16[128,1024]{1,0:T(8,128)(2,1)S(1)}, u32[]{:S(2)}, u32[]{:S(2)}) collective-permute-start(bf16[128,1024]{1,0:T(8,128)(2,1)S(1)} %get-tuple-element.33), channel_id=1, source_target_pairs={{0,2},{1,3},{2,4},{3,5},{4,6},{5,7},{6,0},{7,1},{8,10},{9,11},{10,... | collective-permute-start | bytes 786440 | tf_op jit(solution)/shard_map/ppermute | solution.py:465
  19.2 7.5 %collective-permute-start.2 = (bf16[128,1024]{1,0:T(8,128)(2,1)S(1)}, bf16[128,1024]{1,0:T(8,128)(2,1)S(1)}, u32[]{:S(2)}, u32[]{:S(2)}) collective-permute-start(bf16[128,1024]{1,0:T(8,128)(2,1)S(1)} %get-tuple-element.35), channel_id=1, source_target_pairs={{0,6},{1,7},{2,0},{3,1},{4,2},{5,3},{6,4},{7,5},{8,14},{9,15},{10,... | collective-permute-start | bytes 786440 | tf_op jit(solution)/shard_map/ppermute | solution.py:465
  20.9 7.8 %collective-permute-start.7 = (bf16[64,2048]{1,0:T(8,128)(2,1)S(1)}, bf16[64,2048]{1,0:T(8,128)(2,1)S(1)}, u32[]{:S(2)}, u32[]{:S(2)}) collective-permute-start(bf16[64,2048]{1,0:T(8,128)(2,1)S(1)} %get-tuple-element.40), channel_id=1, source_target_pairs={{0,16},{8,24},{16,32},{24,40},{32,48},{40,56},{48,0},{56,8},{64,80... | collective-permute-start | bytes 786440 | tf_op jit(solution)/shard_map/ppermute | solution.py:469
  22.6 6.4 %collective-permute-start.8 = (bf16[64,2048]{1,0:T(8,128)(2,1)S(1)}, bf16[64,2048]{1,0:T(8,128)(2,1)S(1)}, u32[]{:S(2)}, u32[]{:S(2)}) collective-permute-start(bf16[64,2048]{1,0:T(8,128)(2,1)S(1)} %get-tuple-element.41), channel_id=1, source_target_pairs={{0,48},{8,56},{16,0},{24,8},{32,16},{40,24},{48,32},{56,40},{64,11... | collective-permute-start | bytes 786440 | tf_op jit(solution)/shard_map/ppermute | solution.py:469
  24.2 7.9 %collective-permute-start.5 = (bf16[4,128,256]{2,1,0:T(8,128)(2,1)S(1)}, bf16[4,128,256]{2,1,0:T(8,128)(2,1)S(1)}, u32[]{:S(2)}, u32[]{:S(2)}) collective-permute-start(bf16[4,128,256]{2,1,0:T(8,128)(2,1)S(1)} %own_keys.1.own_ref.after_ref), channel_id=1, source_target_pairs={{0,1},{1,0},{2,3},{3,2},{4,5},{5,4},{6,7},{7,6},{8,9},{9,8},{10,11... | collective-permute-start | bytes 786440 | tf_op jit(solution)/shard_map/ppermute | solution.py:461
  26.7 10.3 %collective-permute-start.9 = (bf16[128,2048]{1,0:T(8,128)(2,1)S(1)}, bf16[128,2048]{1,0:T(8,128)(2,1)S(1)}, u32[]{:S(2)}, u32[]{:S(2)}) collective-permute-start(bf16[128,2048]{1,0:T(8,128)(2,1)S(1)} %later.1.refs_0_), channel_id=1, source_target_pairs={{0,8},{8,0},{16,24},{24,16},{32,40},{40,32},{48,56},{56,48},{64,72... | collective-permute-start | bytes 1572872 | tf_op jit(solution)/shard_map/ppermute | solution.py:461
  29.0 8.1 %collective-permute-start.10 = (bf16[128,2048]{1,0:T(8,128)(2,1)S(1)}, bf16[128,2048]{1,0:T(8,128)(2,1)S(1)}, u32[]{:S(2)}, u32[]{:S(2)}) collective-permute-start(bf16[128,2048]{1,0:T(8,128)(2,1)S(1)} %stack.21.refs_1_), channel_id=1, source_target_pairs={{0,8},{8,0},{16,24},{24,16},{32,40},{40,32},{48,56},{56,48},{64,72... | collective-permute-start | bytes 1572872 | tf_op jit(solution)/shard_map/ppermute | solution.py:461
  32.1 4.9 %copy-start = (bf16[512,2048]{1,0:T(8,128)(2,1)S(1)}, bf16[512,2048]{1,0:T(8,128)(2,1)}, u32[]{:S(2)}) copy-start(bf16[512,2048]{1,0:T(8,128)(2,1)} %mine_ref.5) | copy-start | bytes 6291460
  37.0 15.0 %copy-start.2 = (s32[128,8]{0,1:T(8,128)S(1)}, s32[128,8]{0,1:T(8,128)}, u32[]{:S(2)}) copy-start(s32[128,8]{0,1:T(8,128)} %param.17) | copy-start | bytes 12292
  37.0 15.0 %copy-start.3 = (f32[128,8]{0,1:T(8,128)S(1)}, f32[128,8]{0,1:T(8,128)}, u32[]{:S(2)}) copy-start(f32[128,8]{0,1:T(8,128)} %param.18) | copy-start | bytes 12292
  37.0 16.5 %copy-start.1 = (bf16[128,2048]{1,0:T(8,128)(2,1)S(1)}, bf16[128,2048]{1,0:T(8,128)(2,1)}, u32[]{:S(2)}) copy-start(bf16[128,2048]{1,0:T(8,128)(2,1)} %refs_4_.1) | copy-start | bytes 1572868
  38.3 8.7 %collective-permute-start.11 = (bf16[128,1024]{1,0:T(8,128)(2,1)S(1)}, bf16[128,1024]{1,0:T(8,128)(2,1)S(1)}, u32[]{:S(2)}, u32[]{:S(2)}) collective-permute-start(bf16[128,1024]{1,0:T(8,128)(2,1)S(1)} %get-tuple-element.43), channel_id=1, source_target_pairs={{0,2},{1,3},{2,4},{3,5},{4,6},{5,7},{6,0},{7,1},{8,10},{9,11},{10,... | collective-permute-start | bytes 786440 | tf_op jit(solution)/shard_map/ppermute | solution.py:465
  39.9 17.7 %copy-start.9 = (f32[2048]{0:T(1024)S(1)}, f32[2048]{0:T(1024)}, u32[]{:S(2)}) copy-start(f32[2048]{0:T(1024)} %param.16) | copy-start | bytes 24580
  39.9 8.7 %collective-permute-start.12 = (bf16[128,1024]{1,0:T(8,128)(2,1)S(1)}, bf16[128,1024]{1,0:T(8,128)(2,1)S(1)}, u32[]{:S(2)}, u32[]{:S(2)}) collective-permute-start(bf16[128,1024]{1,0:T(8,128)(2,1)S(1)} %get-tuple-element.45), channel_id=1, source_target_pairs={{0,6},{1,7},{2,0},{3,1},{4,2},{5,3},{6,4},{7,5},{8,14},{9,15},{10,... | collective-permute-start | bytes 786440 | tf_op jit(solution)/shard_map/ppermute | solution.py:465
  43.4 11.4 %collective-permute-start.14 = (bf16[128,1024]{1,0:T(8,128)(2,1)S(1)}, bf16[128,1024]{1,0:T(8,128)(2,1)S(1)}, u32[]{:S(2)}, u32[]{:S(2)}) collective-permute-start(bf16[128,1024]{1,0:T(8,128)(2,1)S(1)} %get-tuple-element.47), channel_id=1, source_target_pairs={{0,2},{1,3},{2,4},{3,5},{4,6},{5,7},{6,0},{7,1},{8,10},{9,11},{10,... | collective-permute-start | bytes 786440 | tf_op jit(solution)/shard_map/ppermute | solution.py:465
  43.7 11.0 %collective-permute-start.15 = (bf16[128,1024]{1,0:T(8,128)(2,1)S(1)}, bf16[128,1024]{1,0:T(8,128)(2,1)S(1)}, u32[]{:S(2)}, u32[]{:S(2)}) collective-permute-start(bf16[128,1024]{1,0:T(8,128)(2,1)S(1)} %get-tuple-element.48), channel_id=1, source_target_pairs={{0,6},{1,7},{2,0},{3,1},{4,2},{5,3},{6,4},{7,5},{8,14},{9,15},{10,... | collective-permute-start | bytes 786440 | tf_op jit(solution)/shard_map/ppermute | solution.py:465
  48.7 8.6 %collective-permute-start.13 = (bf16[128,1024]{1,0:T(8,128)(2,1)S(1)}, bf16[128,1024]{1,0:T(8,128)(2,1)S(1)}, u32[]{:S(2)}, u32[]{:S(2)}) collective-permute-start(bf16[128,1024]{1,0:T(8,128)(2,1)S(1)} %get-tuple-element.46), channel_id=1, source_target_pairs={{0,2},{1,3},{2,4},{3,5},{4,6},{5,7},{6,0},{7,1},{8,10},{9,11},{10,... | collective-permute-start | bytes 786440 | tf_op jit(solution)/shard_map/ppermute | solution.py:465
  51.1 6.4 %collective-permute-start.16 = (bf16[128,1024]{1,0:T(8,128)(2,1)S(1)}, bf16[128,1024]{1,0:T(8,128)(2,1)S(1)}, u32[]{:S(2)}, u32[]{:S(2)}) collective-permute-start(bf16[128,1024]{1,0:T(8,128)(2,1)S(1)} %get-tuple-element.49), channel_id=1, source_target_pairs={{0,6},{1,7},{2,0},{3,1},{4,2},{5,3},{6,4},{7,5},{8,14},{9,15},{10,... | collective-permute-start | bytes 786440 | tf_op jit(solution)/shard_map/ppermute | solution.py:465
  59.6 81.5 %copy-start.4 = (bf16[1,2048,768]{2,1,0:T(8,128)(2,1)S(1)}, bf16[1,2048,768]{2,1,0:T(8,128)(2,1)}, u32[]{:S(2)}) copy-start(bf16[1,2048,768]{2,1,0:T(8,128)(2,1)} %gate_ref.1) | copy-start | bytes 9437188
  59.6 81.5 %copy-start.5 = (bf16[1,2048,768]{2,1,0:T(8,128)(2,1)S(1)}, bf16[1,2048,768]{2,1,0:T(8,128)(2,1)}, u32[]{:S(2)}) copy-start(bf16[1,2048,768]{2,1,0:T(8,128)(2,1)} %up_ref.1) | copy-start | bytes 9437188
  59.6 81.5 %copy-start.6 = (bf16[1,768,2048]{2,1,0:T(8,128)(2,1)S(1)}, bf16[1,768,2048]{2,1,0:T(8,128)(2,1)}, u32[]{:S(2)}) copy-start(bf16[1,768,2048]{2,1,0:T(8,128)(2,1)} %down_ref.1) | copy-start | bytes 9437188
  59.7 81.5 %copy-start.10 = (f32[8,128]{1,0:T(8,128)S(1)}, f32[8,128]{1,0:T(8,128)}, u32[]{:S(2)}) copy-start(f32[8,128]{1,0:T(8,128)} %get-tuple-element.56.stat_ref) | copy-start | bytes 12292
  157.5 82.4 %copy-start.7 = (bf16[256,1024]{1,0:T(8,128)(2,1)S(1)}, bf16[256,1024]{1,0:T(8,128)(2,1)}, u32[]{:S(2)}) copy-start(bf16[256,1024]{1,0:T(8,128)(2,1)} %get-tuple-element.54.mix2_ref) | copy-start | bytes 1572868
  157.6 82.4 %copy-start.8 = (bf16[128,1024]{1,0:T(8,128)(2,1)S(1)}, bf16[128,1024]{1,0:T(8,128)(2,1)}, u32[]{:S(2)}) copy-start(bf16[128,1024]{1,0:T(8,128)(2,1)} %get-tuple-element.53.mix1_ref) | copy-start | bytes 786436
